TPU v7x, 32 devices: a whole 2x2x4 slice. The times are simulated.
32 devices in a mesh: dp: 2 (over core), ctx: 8 (over z, y), fsdp: 2 (over x).
Axes of the slice: x: 2, y: 2, z: 4, core: 2. Of those that a mesh axis runs over, the one named last changes fastest.
Arguments:
- tokens: bfloat16 [4, 1024, 1152], P(('dp', 'fsdp'), 'ctx'), may hold values from -6 to 6
- cotangent: bfloat16 [4, 1024, 1152], P(('dp', 'fsdp'), 'ctx'), may hold values from -6 to 6
- segments: int32 [4, 1024], P(('dp', 'fsdp')), may hold values from 0 to 15, never falling along the last dimension, each value on 1 to 640 neighbouring positions
- qkv_weight: float32 [1536, 1152], P(('ctx', 'fsdp')), may hold values from -0.1875 to 0.1875
- out_weight: float32 [1024, 1152], P(('ctx', 'fsdp')), may hold values from -0.1875 to 0.1875
- gate_up_weight: float32 [13824, 1152], P(('ctx', 'fsdp')), may hold values from -0.1875 to 0.1875
- down_weight: float32 [6912, 1152], P(('ctx', 'fsdp')), may hold values from -0.078125 to 0.078125
- gains: float32 [5120], P(('ctx', 'fsdp')), may hold values from -0.15 to 0.15
- qkv_first: float32 [1536, 1152], P(('ctx', 'fsdp')), may hold values from -90 to 90
- out_first: float32 [1024, 1152], P(('ctx', 'fsdp')), may hold values from -90 to 90
- gate_up_first: float32 [13824, 1152], P(('ctx', 'fsdp')), may hold values from -90 to 90
- down_first: float32 [6912, 1152], P(('ctx', 'fsdp')), may hold values from -90 to 90
- gains_first: float32 [5120], P(('ctx', 'fsdp')), may hold values from -90 to 90
- qkv_second: float32 [1536, 1152], P(('ctx', 'fsdp')), may hold values from 300 to 3000
- out_second: float32 [1024, 1152], P(('ctx', 'fsdp')), may hold values from 300 to 3000
- gate_up_second: float32 [13824, 1152], P(('ctx', 'fsdp')), may hold values from 300 to 3000
- down_second: float32 [6912, 1152], P(('ctx', 'fsdp')), may hold values from 300 to 3000
- gains_second: float32 [5120], P(('ctx', 'fsdp')), may hold values from 300 to 3000
Outputs:
- output: bfloat16 [4, 1024, 1152], P(('dp', 'fsdp'), 'ctx')
- input_grad: float32 [4, 1024, 1152], P(('dp', 'fsdp'), 'ctx')
- qkv_grad: float32 [1536, 1152], P(('ctx', 'fsdp'))
- out_grad: float32 [1024, 1152], P(('ctx', 'fsdp'))
- gate_up_grad: float32 [13824, 1152], P(('ctx', 'fsdp'))
- down_grad: float32 [6912, 1152], P(('ctx', 'fsdp'))
- gains_grad: float32 [5120], P(('ctx', 'fsdp'))
- qkv_new: float32 [1536, 1152], P(('ctx', 'fsdp'))
- out_new: float32 [1024, 1152], P(('ctx', 'fsdp'))
- gate_up_new: float32 [13824, 1152], P(('ctx', 'fsdp'))
- down_new: float32 [6912, 1152], P(('ctx', 'fsdp'))
- gains_new: float32 [5120], P(('ctx', 'fsdp'))
- qkv_first_new: float32 [1536, 1152], P(('ctx', 'fsdp'))
- out_first_new: float32 [1024, 1152], P(('ctx', 'fsdp'))
- gate_up_first_new: float32 [13824, 1152], P(('ctx', 'fsdp'))
- down_first_new: float32 [6912, 1152], P(('ctx', 'fsdp'))
- gains_first_new: float32 [5120], P(('ctx', 'fsdp'))
- qkv_second_new: float32 [1536, 1152], P(('ctx', 'fsdp'))
- out_second_new: float32 [1024, 1152], P(('ctx', 'fsdp'))
- gate_up_second_new: float32 [13824, 1152], P(('ctx', 'fsdp'))
- down_second_new: float32 [6912, 1152], P(('ctx', 'fsdp'))
- gains_second_new: float32 [5120], P(('ctx', 'fsdp'))
Inputs may be any that keep to these rules, and one draw needn't show every extreme that they name: `segments`: in each sequence the segment numbers never fall, every number appears, each document has 1 to 640 tokens, and one has exactly 640.
All inputs are finite; a program needn't handle non-finite values.
Results may differ from a plain program's by a relative error of at most 0.018.
Values may be sent and summed in bfloat16 or wider, within the bound.
A program may use at most 320 MiB of HBM per device.

v0:
```python
import jax
import jax.numpy as jnp
from jax import lax
from jax.sharding import PartitionSpec as P

H = 4
HD = 256
STEP = 5


def normalize(value, gain):
    scale = lax.rsqrt(jnp.mean(value * value, axis=-1, keepdims=True) + 1e-06)
    return value * scale * (1.0 + gain)


def rotate(value, angles):
    half = value.shape[-1] // 2
    first = value[..., :half]
    second = value[..., half:]
    cosine = jnp.cos(angles)
    sine = jnp.sin(angles)
    return jnp.concatenate(
        [first * cosine - second * sine, second * cosine + first * sine], axis=-1
    )


def rope_angles(segments):
    count = segments.shape[0]
    index = jnp.arange(count, dtype=jnp.int32)
    change = jnp.concatenate([jnp.ones((1,), dtype=jnp.bool_), segments[1:] != segments[:-1]])
    starts = lax.cummax(jnp.where(change, index, 0), axis=0)
    offset = (index - starts).astype(jnp.float32)
    inverse = jnp.exp(-jnp.log(1000000.0) * (2.0 * jnp.arange(HD // 2, dtype=jnp.float32)) / HD)
    return offset[:, None] * inverse[None, :]


def contract_last(left, right):
    return lax.dot_general(
        left, right, (((1,), (1,)), ((), ())), preferred_element_type=jnp.float32
    )


def contract_first(left, right):
    return lax.dot_general(
        left, right, (((0,), (0,)), ((), ())), preferred_element_type=jnp.float32
    )


def activate(gate_up):
    half = gate_up.shape[-1] // 2
    return jax.nn.gelu(gate_up[:, :half], approximate=True) * gate_up[:, half:]


def adamw(weight, grad, first, second):
    first_new = 0.9 * first + 0.1 * grad
    second_new = 0.95 * second + 0.05 * grad * grad
    first_hat = first_new / (1.0 - 0.9**STEP)
    second_hat = second_new / (1.0 - 0.95**STEP)
    weight_new = weight - 0.03 * (first_hat / (jnp.sqrt(second_hat) + 1e-08) + 0.1 * weight)
    return (weight_new, first_new, second_new)


def body(
    tokens,
    cotangent,
    segments,
    qkv_weight,
    out_weight,
    gate_up_weight,
    down_weight,
    gains,
    qkv_first,
    out_first,
    gate_up_first,
    down_first,
    gains_first,
    qkv_second,
    out_second,
    gate_up_second,
    down_second,
    gains_second,
):
    rows = tokens.shape[1]
    width = tokens.shape[2]
    length = segments.shape[1]
    query_width = H * HD
    scale = HD ** (-0.5)
    reach = lax.axis_size("ctx") // 2 + 1
    front = reach * rows
    window = front + rows
    qkv_full, out_full, gains_full = (
        lax.all_gather(qkv_weight.astype(jnp.bfloat16), ("ctx", "fsdp"), axis=0, tiled=True),
        lax.all_gather(out_weight.astype(jnp.bfloat16), ("ctx", "fsdp"), axis=0, tiled=True),
        lax.all_gather(gains.astype(jnp.bfloat16), ("ctx", "fsdp"), axis=0, tiled=True),
    )
    gain_all = gains_full.astype(jnp.float32)
    gain_input = gain_all[:width]
    gain_attend = gain_all[width : 2 * width]
    gain_pre = gain_all[2 * width : 3 * width]
    gain_post = gain_all[3 * width : 4 * width]
    gain_query = gain_all[4 * width : 4 * width + HD]
    gain_key = gain_all[4 * width + HD :]
    first_row = lax.axis_index("ctx") * rows
    sequence_ids = segments[0]
    angles = lax.dynamic_slice_in_dim(rope_angles(sequence_ids), first_row, rows, 0)
    query_ids = lax.dynamic_slice_in_dim(sequence_ids, first_row, rows, 0)
    query_pos = first_row + jnp.arange(rows, dtype=jnp.int32)
    window_pos = first_row - front + jnp.arange(window, dtype=jnp.int32)
    padded_ids = jnp.concatenate([jnp.full((front,), -1, dtype=jnp.int32), sequence_ids])
    window_ids = lax.dynamic_slice_in_dim(padded_ids, first_row, window, 0)
    allowed = (window_pos[None, :] <= query_pos[:, None]) & (
        window_ids[None, :] == query_ids[:, None]
    )
    allowed = allowed[:, None, :]
    x_rows = tokens[0].astype(jnp.float32)
    normed, input_back = jax.vjp(normalize, x_rows, gain_input)
    normed_low = normed.astype(jnp.bfloat16)
    projected = contract_last(normed_low, qkv_full)
    proj_query = projected[:, :query_width].reshape(rows, H, HD)
    proj_key = projected[:, query_width : query_width + HD]
    proj_value = projected[:, query_width + HD :]

    def query_key(part_query, part_key, query_gain, key_gain):
        return (
            rotate(normalize(part_query, query_gain), angles[:, None, :]),
            rotate(normalize(part_key, key_gain), angles),
        )

    (rotated_query, rotated_key), rotate_back = jax.vjp(
        query_key, proj_query, proj_key, gain_query, gain_key
    )
    query = rotated_query.astype(jnp.bfloat16)
    key_low = rotated_key.astype(jnp.bfloat16)
    value_low = proj_value.astype(jnp.bfloat16)
    keys_all, values_all = (
        lax.all_gather(key_low, "ctx", axis=0, tiled=True),
        lax.all_gather(value_low, "ctx", axis=0, tiled=True),
    )
    blank = jnp.zeros((front, HD), jnp.bfloat16)
    keys = lax.dynamic_slice_in_dim(jnp.concatenate([blank, keys_all]), first_row, window, 0)
    values = lax.dynamic_slice_in_dim(jnp.concatenate([blank, values_all]), first_row, window, 0)
    scores = jnp.einsum("thd,ld->thl", query, keys, preferred_element_type=jnp.float32) * scale
    masked = jnp.where(allowed, scores, -1e30)
    largest = jnp.max(masked, axis=-1, keepdims=True)
    log_total = largest + jnp.log(jnp.sum(jnp.exp(masked - largest), axis=-1, keepdims=True))
    probs_low = jnp.exp(masked - log_total).astype(jnp.bfloat16)
    attended = jnp.einsum("thl,ld->thd", probs_low, values, preferred_element_type=jnp.float32)
    attended = attended.reshape(rows, query_width).astype(jnp.bfloat16)
    branch = jnp.dot(attended, out_full, preferred_element_type=jnp.float32)
    branch_normed, attend_back = jax.vjp(normalize, branch, gain_attend)
    hidden = x_rows + branch_normed
    gate_up_full, down_full = (
        lax.all_gather(gate_up_weight.astype(jnp.bfloat16), ("ctx", "fsdp"), axis=0, tiled=True),
        lax.all_gather(down_weight.astype(jnp.bfloat16), ("ctx", "fsdp"), axis=0, tiled=True),
    )
    hidden_normed, pre_back = jax.vjp(normalize, hidden, gain_pre)
    hidden_low = hidden_normed.astype(jnp.bfloat16)
    gate_up = contract_last(hidden_low, gate_up_full)
    mixed, mix_back = jax.vjp(activate, gate_up)
    mixed_low = mixed.astype(jnp.bfloat16)
    down = jnp.dot(mixed_low, down_full, preferred_element_type=jnp.float32)
    down_normed, post_back = jax.vjp(normalize, down, gain_post)
    output = (hidden + down_normed).astype(jnp.bfloat16)
    gate_up_back, down_back = (
        lax.all_gather(gate_up_weight.astype(jnp.bfloat16), ("ctx", "fsdp"), axis=0, tiled=True),
        lax.all_gather(down_weight.astype(jnp.bfloat16), ("ctx", "fsdp"), axis=0, tiled=True),
    )
    grad_rows = cotangent[0].astype(jnp.float32)
    grad_down, grad_gain_post = post_back(grad_rows)
    grad_down_low = grad_down.astype(jnp.bfloat16)
    down_grad = contract_first(mixed_low, grad_down_low)
    grad_mixed = contract_last(grad_down_low, down_back)
    (grad_gate_up,) = mix_back(grad_mixed)
    grad_gate_up_low = grad_gate_up.astype(jnp.bfloat16)
    gate_up_grad = contract_first(grad_gate_up_low, hidden_low)
    grad_hidden_low = jnp.dot(grad_gate_up_low, gate_up_back, preferred_element_type=jnp.float32)
    grad_from_pre, grad_gain_pre = pre_back(grad_hidden_low)
    grad_hidden = grad_rows + grad_from_pre
    gate_up_part, down_part = (
        lax.psum_scatter(gate_up_grad, ("ctx", "fsdp"), scatter_dimension=0, tiled=True),
        lax.psum_scatter(down_grad, ("ctx", "fsdp"), scatter_dimension=0, tiled=True),
    )
    qkv_back, out_back = (
        lax.all_gather(qkv_weight.astype(jnp.bfloat16), ("ctx", "fsdp"), axis=0, tiled=True),
        lax.all_gather(out_weight.astype(jnp.bfloat16), ("ctx", "fsdp"), axis=0, tiled=True),
    )
    grad_branch, grad_gain_attend = attend_back(grad_hidden)
    grad_branch_low = grad_branch.astype(jnp.bfloat16)
    out_grad = contract_first(attended, grad_branch_low)
    grad_attended = (
        contract_last(grad_branch_low, out_back).astype(jnp.bfloat16).reshape(rows, H, HD)
    )
    scores_again = (
        jnp.einsum("thd,ld->thl", query, keys, preferred_element_type=jnp.float32) * scale
    )
    probs = jnp.exp(jnp.where(allowed, scores_again, -1e30) - log_total)
    grad_probs = jnp.einsum(
        "thd,ld->thl", grad_attended, values, preferred_element_type=jnp.float32
    )
    row_term = jnp.sum(probs * grad_probs, axis=-1, keepdims=True)
    grad_scores = (probs * (grad_probs - row_term)).astype(jnp.bfloat16)
    grad_query = (
        jnp.einsum("thl,ld->thd", grad_scores, keys, preferred_element_type=jnp.float32) * scale
    )
    grad_keys = (
        jnp.einsum("thl,thd->ld", grad_scores, query, preferred_element_type=jnp.float32) * scale
    )
    grad_values = jnp.einsum(
        "thl,thd->ld", probs.astype(jnp.bfloat16), grad_attended, preferred_element_type=jnp.float32
    )
    empty = jnp.zeros((front + length, HD), jnp.float32)
    keys_spread = lax.dynamic_update_slice_in_dim(empty, grad_keys, first_row, 0)[front:]
    values_spread = lax.dynamic_update_slice_in_dim(empty, grad_values, first_row, 0)[front:]
    grad_key, grad_value = (
        lax.psum_scatter(keys_spread, "ctx", scatter_dimension=0, tiled=True),
        lax.psum_scatter(values_spread, "ctx", scatter_dimension=0, tiled=True),
    )
    grad_proj_query, grad_proj_key, grad_gain_query, grad_gain_key = rotate_back(
        (grad_query, grad_key)
    )
    grad_projected = jnp.concatenate(
        [grad_proj_query.reshape(rows, query_width), grad_proj_key, grad_value], axis=1
    ).astype(jnp.bfloat16)
    qkv_grad = contract_first(grad_projected, normed_low)
    grad_normed = jnp.dot(grad_projected, qkv_back, preferred_element_type=jnp.float32)
    grad_from_input, grad_gain_input = input_back(grad_normed)
    input_grad = grad_hidden + grad_from_input
    gains_grad = jnp.concatenate(
        [
            grad_gain_input,
            grad_gain_attend,
            grad_gain_pre,
            grad_gain_post,
            grad_gain_query,
            grad_gain_key,
        ]
    )
    qkv_part, out_part, gains_part = (
        lax.psum_scatter(qkv_grad, ("ctx", "fsdp"), scatter_dimension=0, tiled=True),
        lax.psum_scatter(out_grad, ("ctx", "fsdp"), scatter_dimension=0, tiled=True),
        lax.psum_scatter(gains_grad, ("ctx", "fsdp"), scatter_dimension=0, tiled=True),
    )
    qkv_total, out_total, gate_up_total, down_total, gains_total = (
        lax.psum(qkv_part.astype(jnp.bfloat16), "dp").astype(jnp.float32),
        lax.psum(out_part.astype(jnp.bfloat16), "dp").astype(jnp.float32),
        lax.psum(gate_up_part.astype(jnp.bfloat16), "dp").astype(jnp.float32),
        lax.psum(down_part.astype(jnp.bfloat16), "dp").astype(jnp.float32),
        lax.psum(gains_part.astype(jnp.bfloat16), "dp").astype(jnp.float32),
    )
    qkv_new, qkv_first_new, qkv_second_new = adamw(qkv_weight, qkv_total, qkv_first, qkv_second)
    out_new, out_first_new, out_second_new = adamw(out_weight, out_total, out_first, out_second)
    gate_up_new, gate_up_first_new, gate_up_second_new = adamw(
        gate_up_weight, gate_up_total, gate_up_first, gate_up_second
    )
    down_new, down_first_new, down_second_new = adamw(
        down_weight, down_total, down_first, down_second
    )
    gains_new, gains_first_new, gains_second_new = adamw(
        gains, gains_total, gains_first, gains_second
    )
    return (
        output[None],
        input_grad[None],
        qkv_total,
        out_total,
        gate_up_total,
        down_total,
        gains_total,
        qkv_new,
        out_new,
        gate_up_new,
        down_new,
        gains_new,
        qkv_first_new,
        out_first_new,
        gate_up_first_new,
        down_first_new,
        gains_first_new,
        qkv_second_new,
        out_second_new,
        gate_up_second_new,
        down_second_new,
        gains_second_new,
    )


def solution(mesh):
    in_specs = (
        P(("dp", "fsdp"), "ctx", None),
        P(("dp", "fsdp"), "ctx", None),
        P(("dp", "fsdp"), None),
        P(("ctx", "fsdp"), None),
        P(("ctx", "fsdp"), None),
        P(("ctx", "fsdp"), None),
        P(("ctx", "fsdp"), None),
        P(("ctx", "fsdp")),
        P(("ctx", "fsdp"), None),
        P(("ctx", "fsdp"), None),
        P(("ctx", "fsdp"), None),
        P(("ctx", "fsdp"), None),
        P(("ctx", "fsdp")),
        P(("ctx", "fsdp"), None),
        P(("ctx", "fsdp"), None),
        P(("ctx", "fsdp"), None),
        P(("ctx", "fsdp"), None),
        P(("ctx", "fsdp")),
    )
    out_specs = (
        P(("dp", "fsdp"), "ctx", None),
        P(("dp", "fsdp"), "ctx", None),
        P(("ctx", "fsdp"), None),
        P(("ctx", "fsdp"), None),
        P(("ctx", "fsdp"), None),
        P(("ctx", "fsdp"), None),
        P(("ctx", "fsdp")),
        P(("ctx", "fsdp"), None),
        P(("ctx", "fsdp"), None),
        P(("ctx", "fsdp"), None),
        P(("ctx", "fsdp"), None),
        P(("ctx", "fsdp")),
        P(("ctx", "fsdp"), None),
        P(("ctx", "fsdp"), None),
        P(("ctx", "fsdp"), None),
        P(("ctx", "fsdp"), None),
        P(("ctx", "fsdp")),
        P(("ctx", "fsdp"), None),
        P(("ctx", "fsdp"), None),
        P(("ctx", "fsdp"), None),
        P(("ctx", "fsdp"), None),
        P(("ctx", "fsdp")),
    )
    return jax.shard_map(body, mesh=mesh, in_specs=in_specs, out_specs=out_specs, check_vma=False)
```

profile of v0, /device:TPU:0, one launch (start us, length us, event | category | flops | bytes accessed | tf_op | source)
XLA Modules:
  0.0 2683.5 jit_solution(189627027710603914)
XLA Ops:
  10.8 3.7 convert_element_type.124
  17.3 79.4 %all-reduce.9 = bf16[5120]{0:T(1024)(128)(2,1)S(1)} all-reduce(bf16[5120]{0:T(1024)(128)(2,1)S(1)} %dynamic-update-slice), channel_id=1, replica_groups=mesh['dp'=2,'ctx'=8,'fsdp'=2] {'ctx','fsdp'}, use_global_device_ids=true, to_apply=%add.9 | all-reduce | flops 5120 | bytes 20480
  98.7 3.3 fusion.60
  103.2 32.1 %all_gather.27 = bf16[1024,256]{1,0:T(8,128)(2,1)S(1)} all-gather(bf16[128,256]{1,0:T(8,128)(2,1)S(1)} %pad_maximum_fusion.6), channel_id=1, replica_groups=mesh['dp'=2,'ctx'=8,'fsdp'=2] {'ctx'}, dimensions={0}, use_global_device_ids=true | all-gather | bytes 589824 | tf_op jit(solution)/shard_map/all_gather | solution.py:136
  137.8 32.1 %all_gather.28 = bf16[1024,256]{1,0:T(8,128)(2,1)S(1)} all-gather(bf16[128,256]{1,0:T(8,128)(2,1)S(1)} %slice.142), channel_id=1, replica_groups=mesh['dp'=2,'ctx'=8,'fsdp'=2] {'ctx'}, dimensions={0}, use_global_device_ids=true | all-gather | bytes 589824 | tf_op jit(solution)/shard_map/all_gather | solution.py:137
  170.8 2.3 multiply_reduce_fusion.7
  173.5 318.4 %all-gather.9.cloned.1.call-done = bf16[13824,1152]{1,0:T(8,128)(2,1)} async-done(((bf16[864,1152]{1,0:T(8,128)(2,1)}), bf16[13824,1152]{1,0:T(8,128)(2,1)}) %all-gather.9.cloned.1.call-update) | async-done | bytes 31850512 | tf_op jit(solution)/shard_map/all_gather | solution.py:153
  491.8 18.5 fusion.91
  510.3 4.3 multiply_convert_fusion
  514.6 162.3 %all-gather.11.cloned.1.call-done = bf16[6912,1152]{1,0:T(8,128)(2,1)} async-done(((bf16[432,1152]{1,0:T(8,128)(2,1)}), bf16[6912,1152]{1,0:T(8,128)(2,1)}) %all-gather.11.cloned.1.call-update) | async-done | bytes 15925264 | tf_op jit(solution)/shard_map/all_gather | solution.py:154
  676.9 8.1 multiply_reduce_fusion.5
  686.9 12.4 fusion.11
  699.3 18.4 multiply_reduce_fusion.1
  717.7 2.7 multiply_reduce_fusion.2
  729.3 2.9 fusion.99
  735.7 51.1 %reduce-scatter.9.cloned.1.call-done = f32[128,256]{1,0:T(8,128)} async-done(((f32[1024,256]{1,0:T(8,128)}), f32[128,256]{1,0:T(8,128)}) %reduce-scatter.9.cloned.1.call-update) | async-done | bytes 131088 | tf_op jit(solution)/shard_map/reduce_scatter | solution.py:216
  787.9 65.7 %reduce-scatter.7.cloned.1.call-done = f32[128,256]{1,0:T(8,128)} async-done(((f32[1024,256]{1,0:T(8,128)}), f32[128,256]{1,0:T(8,128)}) %reduce-scatter.7.cloned.1.call-update) | async-done | bytes 131088 | tf_op jit(solution)/shard_map/reduce_scatter | solution.py:215
  858.3 4.0 fusion.48
  863.3 13.0 fusion.100
  877.3 26.9 %fusion.29 = f32[13824,1152]{1,0:T(8,128)} fusion(f32[128,6912]{1,0:T(8,128)} %get-tuple-element.62, f32[128,6912]{1,0:T(8,128)} %get-tuple-element.61, f32[128,1152]{1,0:T(8,128)S(1)} %copy-done.2, f32[1152]{0:T(1024)S(1)} %get-tuple-element.74, f32[128]{0:T(128)S(1)} %fusion.79), kind=kOutput, calls=%fused_computation.81 | convolution fusion | flops 4080844800 | bytes 71373824 | tf_op jit(solution)/shard_map/dot_general | solution.py:44
  904.3 91.2 %reduce-scatter.13.cloned.1.call-done = f32[64,1152]{1,0:T(8,128)} async-done(((f32[1024,1152]{1,0:T(8,128)}), f32[64,1152]{1,0:T(8,128)}) %reduce-scatter.13.cloned.1.call-update) | async-done | bytes 294928 | tf_op jit(solution)/shard_map/reduce_scatter | solution.py:240
  997.1 155.0 %reduce-scatter.11.cloned.1.call-done = f32[96,1152]{1,0:T(8,128)} async-done(((f32[1536,1152]{1,0:T(8,128)}), f32[96,1152]{1,0:T(8,128)}) %reduce-scatter.11.cloned.1.call-update) | async-done | bytes 442384 | tf_op jit(solution)/shard_map/reduce_scatter | solution.py:239
  1153.9 483.4 %reduce-scatter.17.cloned.1.call-done = f32[432,1152]{1,0:T(8,128)} async-done(((f32[6912,1152]{1,0:T(8,128)}), f32[432,1152]{1,0:T(8,128)}) %reduce-scatter.17.cloned.1.call-update) | async-done | bytes 1990672 | tf_op jit(solution)/shard_map/reduce_scatter | solution.py:181
  1637.2 2.6 convert_element_type.141
  1639.8 920.2 %reduce-scatter.15.cloned.1.call-done = f32[864,1152]{1,0:T(8,128)} async-done(((f32[13824,1152]{1,0:T(8,128)}), f32[864,1152]{1,0:T(8,128)}) %reduce-scatter.15.cloned.1.call-update) | async-done | bytes 3981328 | tf_op jit(solution)/shard_map/reduce_scatter | solution.py:180
  2560.0 3.6 convert_element_type.139
  2564.4 3.2 fusion.18
  2575.5 75.5 %all-reduce.10 = bf16[5120]{0:T(1024)(128)(2,1)S(1)} all-reduce(f32[5120]{0:T(1024)} %constant_dynamic-update-slice_fusion), channel_id=8, replica_groups=mesh['dp'=2,'ctx'=8,'fsdp'=2] {'ctx','fsdp'}, use_global_device_ids=true, to_apply=%region_33.34.clone | all-reduce | flops 5120 | bytes 30720
  2651.1 2.4 psum.39
  2657.8 2.8 multiply_subtract_fusion.2
  2662.6 10.2 multiply_subtract_fusion
  2672.9 3.6 multiply_subtract_fusion.1
  (232 shorter events, 51.5 us)
Async XLA Ops:
  7.2 91.5 %all-gather.5.cloned.1.call-start = ((), (), s32[]{:S(2)}) async-start(), calls=%async_computation.6 | async-start | bytes 3760128 | tf_op jit(solution)/shard_map/all_gather | solution.py:92
  9.0 161.8 %all-gather.7.cloned.1.call-start = ((), (), s32[]{:S(2)}) async-start(), calls=%async_computation.7 | async-start | bytes 2506752 | tf_op jit(solution)/shard_map/all_gather | solution.py:93
  10.7 481.1 %all-gather.9.cloned.1.call-start = ((), (), s32[]{:S(2)}) async-start(), calls=%async_computation.8 | async-start | bytes 33841152 | tf_op jit(solution)/shard_map/all_gather | solution.py:153
  14.5 82.2 %copy-start.40 = (s32[1,1024]{1,0:T(1,128)S(1)}, s32[1,1024]{1,0:T(1,128)}, u32[]{:S(2)}) copy-start(s32[1,1024]{1,0:T(1,128)} %param.20) | copy-start | bytes 12292
  14.5 83.1 %copy-start.7 = (bf16[1,128,1152]{2,1,0:T(8,128)(2,1)S(1)}, bf16[1,128,1152]{2,1,0:T(8,128)(2,1)}, u32[]{:S(2)}) copy-start(bf16[1,128,1152]{2,1,0:T(8,128)(2,1)} %param.18) | copy-start | bytes 884740
  14.5 662.4 %all-gather.11.cloned.1.call-start = ((), (), s32[]{:S(2)}) async-start(), calls=%async_computation.9 | async-start | bytes 16920576 | tf_op jit(solution)/shard_map/all_gather | solution.py:154
  15.7 771.2 %reduce-scatter.9.cloned.1.call-start = ((), (), s32[]{:S(2)}) async-start(), calls=%async_computation.11 | async-start | bytes 1179648 | tf_op jit(solution)/shard_map/reduce_scatter | solution.py:216
  97.9 37.5 %copy-start.46 = (f32[256]{0:T(256)}, f32[256]{0:T(256)S(1)}, u32[]{:S(2)}) copy-start(f32[256]{0:T(256)S(1)} %get-tuple-element.77) | copy-start | bytes 3076
  101.9 35.4 %copy-start.15 = (f32[128,1536]{1,0:T(8,128)}, f32[128,1536]{1,0:T(8,128)S(1)}, u32[]{:S(2)}) copy-start(f32[128,1536]{1,0:T(8,128)S(1)} %fusion.60) | copy-start | bytes 2359300
  102.0 35.3 %copy-start.5 = (f32[128,1024]{1,0:T(8,128)}, f32[128,1024]{1,0:T(8,128)S(1)}, u32[]{:S(2)}) copy-start(f32[128,1024]{1,0:T(8,128)S(1)} %slice.89) | copy-start | bytes 1572868
  102.7 34.6 %copy-start.58 = (f32[128]{0:T(128)}, f32[128]{0:T(128)S(1)}, u32[]{:S(2)}) copy-start(f32[128]{0:T(128)S(1)} %multiply_reduce_fusion.12) | copy-start | bytes 1540
  102.7 32.8 %copy-start.51 = (f32[128]{0:T(128)}, f32[128]{0:T(128)S(1)}, u32[]{:S(2)}) copy-start(f32[128]{0:T(128)S(1)} %fusion.77) | copy-start | bytes 1540
  170.8 321.1 %copy-start.22 = (bf16[128,4,256]{0,2,1:T(8,128)(2,1)}, bf16[128,4,256]{0,2,1:T(8,128)(2,1)S(1)}, u32[]{:S(2)}) copy-start(bf16[128,4,256]{0,2,1:T(8,128)(2,1)S(1)} %copy.88) | copy-start | bytes 786436
  173.2 318.7 %copy-start.10 = (f32[128,1152]{1,0:T(8,128)}, f32[128,1152]{1,0:T(8,128)S(1)}, u32[]{:S(2)}) copy-start(f32[128,1152]{1,0:T(8,128)S(1)} %get-tuple-element.86) | copy-start | bytes 1769476
  173.5 318.4 %copy-start = (f32[128,1152]{1,0:T(8,128)}, f32[128,1152]{1,0:T(8,128)S(1)}, u32[]{:S(2)}) copy-start(f32[128,1152]{1,0:T(8,128)S(1)} %get-tuple-element.60) | copy-start | bytes 1769476
  686.8 12.4 copy-start.29
  725.2 128.4 %reduce-scatter.7.cloned.1.call-start = ((), (), s32[]{:S(2)}) async-start(), calls=%async_computation.10 | async-start | bytes 1179648 | tf_op jit(solution)/shard_map/reduce_scatter | solution.py:215
  729.2 266.3 %reduce-scatter.13.cloned.1.call-start = ((), (), s32[]{:S(2)}) async-start(), calls=%async_computation.13 | async-start | bytes 5013504 | tf_op jit(solution)/shard_map/reduce_scatter | solution.py:240
  732.2 122.7 %copy-start.45 = (f32[256]{0:T(256)S(1)}, f32[256]{0:T(256)}, u32[]{:S(2)}) copy-start(f32[256]{0:T(256)} %copy-done.44) | copy-start | bytes 3076
  732.2 126.1 %copy-start.8 = (bf16[1,128,1152]{2,1,0:T(8,128)(2,1)S(1)}, bf16[1,128,1152]{2,1,0:T(8,128)(2,1)}, u32[]{:S(2)}) copy-start(bf16[1,128,1152]{2,1,0:T(8,128)(2,1)} %param.18) | copy-start | bytes 884740
  732.2 126.1 %copy-start.50 = (f32[128]{0:T(128)S(1)}, f32[128]{0:T(128)}, u32[]{:S(2)}) copy-start(f32[128]{0:T(128)} %copy-done.49) | copy-start | bytes 1540
  732.2 419.9 %reduce-scatter.11.cloned.1.call-start = ((), (), s32[]{:S(2)}) async-start(), calls=%async_computation.12 | async-start | bytes 7520256 | tf_op jit(solution)/shard_map/reduce_scatter | solution.py:239
  735.7 126.6 %copy-start.24 = (bf16[128,4,256]{0,2,1:T(8,128)(2,1)}, bf16[128,4,256]{0,2,1:T(8,128)(2,1)S(1)}, u32[]{:S(2)}) copy-start(bf16[128,4,256]{0,2,1:T(8,128)(2,1)S(1)} %copy.92) | copy-start | bytes 786436
  787.9 74.4 %copy-start.32 = (bf16[128,256]{0,1:T(8,128)(2,1)}, bf16[128,256]{0,1:T(8,128)(2,1)S(1)}, u32[]{:S(2)}) copy-start(bf16[128,256]{0,1:T(8,128)(2,1)S(1)} %copy.97) | copy-start | bytes 196612
  862.4 774.8 %reduce-scatter.17.cloned.1.call-start = ((), (), s32[]{:S(2)}) async-start(), calls=%async_computation.15 | async-start | bytes 33841152 | tf_op jit(solution)/shard_map/reduce_scatter | solution.py:181
  876.3 1683.7 %reduce-scatter.15.cloned.1.call-start = ((), (), s32[]{:S(2)}) async-start(), calls=%async_computation.14 | async-start | bytes 67682304 | tf_op jit(solution)/shard_map/reduce_scatter | solution.py:180
  904.2 1753.6 %all-reduce.14.cloned.1.call-start = ((), (), s32[]{:S(2)}) async-start(), calls=%async_computation.16 | async-start | bytes 6709248 | tf_op jit(solution)/shard_map/psum | solution.py:244
  1639.8 924.5 %copy-start.4 = (bf16[1536,1152]{1,0:T(8,128)(2,1)S(1)}, bf16[1536,1152]{1,0:T(8,128)(2,1)}, u32[]{:S(2)}) copy-start(bf16[1536,1152]{1,0:T(8,128)(2,1)} %all-gather.5.cloned.1.call-done) | copy-start | bytes 10616836
  2567.6 93.0 %copy-start.28 = (f32[64,1152]{1,0:T(8,128)S(1)}, f32[64,1152]{1,0:T(8,128)}, u32[]{:S(2)}) copy-start(f32[64,1152]{1,0:T(8,128)} %param.22) | copy-start | bytes 884740
  2567.6 93.0 %copy-start.34 = (f32[64,1152]{1,0:T(8,128)S(1)}, f32[64,1152]{1,0:T(8,128)}, u32[]{:S(2)}) copy-start(f32[64,1152]{1,0:T(8,128)} %param.27) | copy-start | bytes 884740
  2567.6 93.0 %copy-start.35 = (f32[64,1152]{1,0:T(8,128)S(1)}, f32[64,1152]{1,0:T(8,128)}, u32[]{:S(2)}) copy-start(f32[64,1152]{1,0:T(8,128)} %param.32) | copy-start | bytes 884740
  2662.6 10.3 copy-start.27
  (38 other events, 154.8 us)
Sparse Core Ops, SparseCore 0:
  11.4 74.5 all-gather.4
  89.4 64.2 all-gather.6
  157.1 334.7 all-gather.8
  495.1 181.7 all-gather.10
  725.3 61.4 reduce-scatter.8
  791.1 62.5 reduce-scatter.6
  858.8 136.6 reduce-scatter.12
  1001.7 150.4 reduce-scatter.10
  1159.2 477.9 reduce-scatter.16
  1644.1 915.8 reduce-scatter.14
  2564.3 23.4 all-reduce.13
where the time goes:
time: 2690 us; the launch traced here: 2680 us
  waiting for transfers between devices  2250 us (84%)
  blocking collectives  222 us (8%)
  matrix products  120 us (4%)
  other arithmetic  60.8 us (2%)
    reduce_scatter x1, waiting for transfers between devices, body(): lax.psum_scatter(gate_up_grad, ('ctx', 'fsdp'), scatter_dimension=0, tile...  920 us
    reduce_scatter x1, waiting for transfers between devices, body(): lax.psum_scatter(down_grad, ('ctx', 'fsdp'), scatter_dimension=0, tiled=T...  483 us
    all_gather x1, waiting for transfers between devices, body(): lax.all_gather(gate_up_weight.astype(jnp.bfloat16), ('ctx', 'fsdp'), axis...  318 us
    all_gather x1, waiting for transfers between devices, body(): lax.all_gather(down_weight.astype(jnp.bfloat16), ('ctx', 'fsdp'), axis=0,...  162 us
    reduce_scatter x1, waiting for transfers between devices, body(): lax.psum_scatter(qkv_grad, ('ctx', 'fsdp'), scatter_dimension=0, tiled=True)  155 us
    unnamed x2, blocking collectives  155 us
    reduce_scatter x1, waiting for transfers between devices, body(): lax.psum_scatter(out_grad, ('ctx', 'fsdp'), scatter_dimension=0, tiled=True)  91.2 us
    reduce_scatter x1, waiting for transfers between devices, body(): lax.psum_scatter(keys_spread, 'ctx', scatter_dimension=0, tiled=True)  65.7 us
  transfers between devices with their start and end apart: 11, of which 8 were waited for; matrix products, arithmetic and copies ran while one was open for 5% of the time, Pallas kernels for 0%

commit v1 on v0

--- a/solution.py
+++ b/solution.py
@@ -1,7 +1,17 @@
+import functools
+
 import jax
 import jax.numpy as jnp
 from jax import lax
+from jax.experimental import pallas as pl
+from jax.experimental.pallas import tpu as pltpu
 from jax.sharding import PartitionSpec as P
+
+MESH = pl.DeviceIdType.MESH
+ANY = pl.BlockSpec(memory_space=pl.ANY)
+VMEM = pl.BlockSpec(memory_space=pltpu.VMEM)
+BF = jnp.bfloat16
+F32 = jnp.float32
 
 H = 4
 HD = 256
@@ -24,12 +34,10 @@
     )
 
 
-def rope_angles(segments):
-    count = segments.shape[0]
-    index = jnp.arange(count, dtype=jnp.int32)
-    change = jnp.concatenate([jnp.ones((1,), dtype=jnp.bool_), segments[1:] != segments[:-1]])
-    starts = lax.cummax(jnp.where(change, index, 0), axis=0)
-    offset = (index - starts).astype(jnp.float32)
+def rope_angles(segments, first, rows):
+    own = lax.dynamic_slice_in_dim(segments, first, rows, 0)
+    starts = jnp.sum((segments[None, :] < own[:, None]).astype(jnp.int32), axis=1)
+    offset = (first + jnp.arange(rows, dtype=jnp.int32) - starts).astype(jnp.float32)
     inverse = jnp.exp(-jnp.log(1000000.0) * (2.0 * jnp.arange(HD // 2, dtype=jnp.float32)) / HD)
     return offset[:, None] * inverse[None, :]
 
@@ -60,7 +68,7 @@
     return (weight_new, first_new, second_new)
 
 
-def body(
+def gather_weights_body(
     tokens,
     cotangent,
     segments,
@@ -102,7 +110,7 @@
     gain_key = gain_all[4 * width + HD :]
     first_row = lax.axis_index("ctx") * rows
     sequence_ids = segments[0]
-    angles = lax.dynamic_slice_in_dim(rope_angles(sequence_ids), first_row, rows, 0)
+    angles = rope_angles(sequence_ids, first_row, rows)
     query_ids = lax.dynamic_slice_in_dim(sequence_ids, first_row, rows, 0)
     query_pos = first_row + jnp.arange(rows, dtype=jnp.int32)
     window_pos = first_row - front + jnp.arange(window, dtype=jnp.int32)
@@ -284,6 +292,986 @@
     )
 
 
+def place():
+    return lax.axis_index("dp"), lax.axis_index("ctx"), lax.axis_index("fsdp")
+
+
+def greet(devices, extra=0):
+    barrier = pltpu.get_barrier_semaphore()
+    for device in devices:
+        pl.semaphore_signal(barrier, inc=1, device_id=device, device_id_type=MESH)
+    pl.semaphore_wait(barrier, len(devices))
+
+
+def remote(source, target, send, recv, device):
+    return pltpu.make_async_remote_copy(
+        src_ref=source,
+        dst_ref=target,
+        send_sem=send,
+        recv_sem=recv,
+        device_id=device,
+        device_id_type=MESH,
+    )
+
+
+def layers_of(z, y, count, dp, x):
+    return [(dp, lax.rem(z + step, count) * 2 + y, x) for step in range(1, count)]
+
+
+def gather_kernel(wq, wo, gn, wgu, wd, qkv, out, gain, gu, dn, send, recv, local, send_f, recv_f):
+    dp, ctx, x = place()
+    layers = qkv.shape[0]
+    z, y = ctx // 2, ctx % 2
+    cube = ctx // 4
+    sibling = (1 - dp, ctx, x)
+    y2, x2 = jnp.where(dp == 0, 1 - y, y), jnp.where(dp == 0, x, 1 - x)
+    y3, x3 = jnp.where(dp == 0, y, 1 - y), jnp.where(dp == 0, 1 - x, x)
+    second = (dp, z * 2 + y2, x2)
+    third = (dp, z * 2 + y3, x3)
+    others = layers_of(z, y, layers, dp, x)
+    down_to = (x, ctx // 2 + 4 * dp, ctx % 2)
+    group = (ctx % 4) * 2 + x
+    down_from = (cube, group, dp)
+    stays = (dp == x) & (ctx == down_to[1]) & (x == ctx % 2)
+    barrier = pltpu.get_barrier_semaphore()
+    for device in others + [second, third, sibling]:
+        pl.semaphore_signal(barrier, inc=1, device_id=device, device_id_type=MESH)
+
+    @pl.when(jnp.logical_not(stays))
+    def _():
+        for device in (down_to, down_from):
+            pl.semaphore_signal(barrier, inc=1, device_id=device, device_id_type=MESH)
+
+    pl.semaphore_wait(barrier, jnp.where(stays, layers + 2, layers + 4))
+
+    triples = ((wq, qkv), (gn, gain), (wo, out))
+    started = []
+
+    def start(copy):
+        copy.start()
+        started.append(copy)
+        return copy
+
+    own, first = [], []
+    for t, (part, full) in enumerate(triples):
+        copy = pltpu.make_async_copy(part.at[dp], full.at[z, y, x, dp], local.at[t])
+        copy.start()
+        own.append(copy)
+        first.append(
+            [
+                start(remote(part.at[dp], full.at[z, y, x, dp], send.at[t, i], recv.at[t, i], device))
+                for i, device in enumerate(others)
+            ]
+        )
+    gu_own = pltpu.make_async_copy(wgu, gu.at[cube], local.at[3])
+    gu_own.start()
+    gu_cross = start(
+        remote(wgu.at[dp], gu.at[cube, dp], send_f.at[0], recv_f.at[0], (dp, (ctx + 4) % 8, x))
+    )
+    down_local = pltpu.make_async_copy(wd, dn.at[x], recv_f.at[1])
+    down_move = remote(wd, dn.at[x], send_f.at[1], recv_f.at[1], down_to)
+
+    @pl.when(stays)
+    def _():
+        down_local.start()
+
+    @pl.when(jnp.logical_not(stays))
+    def _():
+        down_move.start()
+
+    line, third_own, sib = [], [], []
+    for t, (_, full) in enumerate(triples):
+        own[t].wait()
+        for copy in first[t]:
+            copy.wait_recv()
+        mine = full.at[:, y, x, dp]
+        line.append(start(remote(mine, mine, send.at[t, 3], recv.at[t, 3], second)))
+        third_own.append(start(remote(mine, mine, send.at[t, 4], recv.at[t, 4], third)))
+        sib.append(start(remote(mine, mine, send.at[t, 5], recv.at[t, 5], sibling)))
+    third_line = []
+    for t, (_, full) in enumerate(triples):
+        line[t].wait_recv()
+        seconds = full.at[:, y2, x2, dp]
+        third_line.append(start(remote(seconds, seconds, send.at[t, 6], recv.at[t, 6], third)))
+        sib.append(start(remote(seconds, seconds, send.at[t, 7], recv.at[t, 7], sibling)))
+    for t, (_, full) in enumerate(triples):
+        third_own[t].wait_recv()
+        thirds = full.at[:, y3, x3, dp]
+        sib.append(start(remote(thirds, thirds, send.at[t, 8], recv.at[t, 8], sibling)))
+        third_line[t].wait_recv()
+        far = full.at[:, 1 - y, 1 - x, dp]
+        sib.append(start(remote(far, far, send.at[t, 9], recv.at[t, 9], sibling)))
+    gu_cross.wait_recv()
+    crossed = gu.at[1 - cube, dp]
+    sib.append(start(remote(crossed, crossed, send_f.at[2], recv_f.at[2], sibling)))
+    down_local.wait()
+    landed = dn.at[dp]
+    sib.append(start(remote(landed, landed, send_f.at[3], recv_f.at[3], sibling)))
+    for copy in sib:
+        copy.wait_recv()
+    gu_own.wait()
+    for copy in started:
+        copy.wait_send()
+
+    @pl.when(jnp.logical_not(stays))
+    def _():
+        down_move.wait_send()
+
+
+def gather_weights(wq, wo, gn, wgu, wd, layers):
+    lead = (layers, 2, 2)
+
+    def full(part):
+        return jax.ShapeDtypeStruct(lead + part.shape, part.dtype)
+
+    return pl.pallas_call(
+        gather_kernel,
+        out_shape=(
+            full(wq),
+            full(wo),
+            full(gn),
+            jax.ShapeDtypeStruct((2,) + wgu.shape, BF),
+            jax.ShapeDtypeStruct((2,) + wd.shape, BF),
+        ),
+        in_specs=[ANY] * 5,
+        out_specs=(ANY,) * 5,
+        scratch_shapes=[
+            pltpu.SemaphoreType.DMA((3, 10)),
+            pltpu.SemaphoreType.DMA((3, 10)),
+            pltpu.SemaphoreType.DMA((4,)),
+            pltpu.SemaphoreType.DMA((4,)),
+            pltpu.SemaphoreType.DMA((4,)),
+        ],
+        compiler_params=pltpu.CompilerParams(collective_id=0, has_side_effects=True),
+    )(wq, wo, gn, wgu, wd)
+
+
+def keys_kernel(part, full, send, recv, local):
+    dp, ctx, x = place()
+    layers = full.shape[0]
+    z, y = ctx // 2, ctx % 2
+    others = layers_of(z, y, layers, dp, x)
+    beside = (dp, z * 2 + 1 - y, x)
+    greet(others + [beside])
+    own = pltpu.make_async_copy(part, full.at[z, y], local.at[0])
+    own.start()
+    copies = [
+        remote(part, full.at[z, y], send.at[i], recv.at[i], device)
+        for i, device in enumerate(others)
+    ]
+    for copy in copies:
+        copy.start()
+    own.wait()
+    for copy in copies:
+        copy.wait_recv()
+    line = remote(full.at[:, y], full.at[:, y], send.at[3], recv.at[3], beside)
+    line.start()
+    line.wait()
+    for copy in copies:
+        copy.wait_send()
+
+
+def gather_keys(part, layers):
+    return pl.pallas_call(
+        keys_kernel,
+        out_shape=jax.ShapeDtypeStruct((layers, 2) + part.shape, part.dtype),
+        in_specs=[VMEM],
+        out_specs=VMEM,
+        scratch_shapes=[
+            pltpu.SemaphoreType.DMA((4,)),
+            pltpu.SemaphoreType.DMA((4,)),
+            pltpu.SemaphoreType.DMA((1,)),
+        ],
+        compiler_params=pltpu.CompilerParams(collective_id=1, has_side_effects=True),
+    )(part)
+
+
+def scatter_keys_kernel(part, total, beside_in, sums, layer_in, send, recv):
+    dp, ctx, x = place()
+    layers = part.shape[0]
+    z, y = ctx // 2, ctx % 2
+    others = layers_of(z, y, layers, dp, x)
+    beside = (dp, z * 2 + 1 - y, x)
+    greet(others + [beside])
+    line = remote(part.at[:, 1 - y], beside_in, send.at[3], recv.at[3], beside)
+    line.start()
+    line.wait_recv()
+    for i in range(layers):
+        sums[i] = (part[i, y].astype(F32) + beside_in[i].astype(F32)).astype(BF)
+    copies = [
+        remote(sums.at[lax.rem(z + i + 1, layers)], layer_in.at[i], send.at[i], recv.at[i], device)
+        for i, device in enumerate(others)
+    ]
+    for copy in copies:
+        copy.start()
+    for copy in copies:
+        copy.wait_recv()
+    total[...] = sums[z].astype(F32)
+    for i in range(layers - 1):
+        total[...] += layer_in[i].astype(F32)
+    line.wait_send()
+    for copy in copies:
+        copy.wait_send()
+
+
+def scatter_keys(part):
+    layers, _, rows, width = part.shape
+    return pl.pallas_call(
+        scatter_keys_kernel,
+        out_shape=jax.ShapeDtypeStruct((rows, width), F32),
+        in_specs=[VMEM],
+        out_specs=VMEM,
+        scratch_shapes=[
+            pltpu.VMEM((layers, rows, width), BF),
+            pltpu.VMEM((layers, rows, width), BF),
+            pltpu.VMEM((layers - 1, rows, width), BF),
+            pltpu.SemaphoreType.DMA((4,)),
+            pltpu.SemaphoreType.DMA((4,)),
+        ],
+        compiler_params=pltpu.CompilerParams(collective_id=2, has_side_effects=True),
+    )(part)
+
+
+def cube_parts(rows):
+    third = -(-rows // 48) * 16
+    return ((0, third), (third, third), (2 * third, rows - 2 * third))
+
+
+class Cube:
+    def __init__(self, rows, gather_send, gather_recv, scatter_send, scatter_recv):
+        dp, ctx, x = place()
+        self.me = (ctx % 4) * 2 + x
+        self.masks = (1, 2, 4)
+        self.peers = (
+            (dp, ctx, 1 - x),
+            (dp, ctx + 1 - 2 * (ctx % 2), x),
+            (dp, ctx + 2 - 4 * (ctx // 2 % 2), x),
+        )
+        self.parts = cube_parts(rows)
+        self.sems = (gather_send, gather_recv, scatter_send, scatter_recv)
+
+    def block(self, mask):
+        me, result = self.me, 0
+        for bit in (1, 2, 4):
+            own = me // bit % 2
+            result = result + bit * (1 - own if mask & bit else own)
+        return result
+
+    def gather(self, buf):
+        send, recv = self.sems[:2]
+
+        def copy(p, index, mask, dim):
+            start, size = self.parts[p]
+            ref = buf.at[self.block(mask), pl.ds(start, size)]
+            return remote(ref, ref, send.at[p, index], recv.at[p, index], self.peers[dim])
+
+        orders = [(p, (p + 1) % 3, (p + 2) % 3) for p in range(3)]
+        sent = {}
+
+        def go(p, index, mask, dim):
+            sent[p, index] = copy(p, index, mask, dim)
+            sent[p, index].start()
+
+        for p, (a, b, c) in enumerate(orders):
+            go(p, 0, 0, a)
+        for p, (a, b, c) in enumerate(orders):
+            go(p, 1, 0, b)
+        for p, (a, b, c) in enumerate(orders):
+            go(p, 3, 0, c)
+        for p, (a, b, c) in enumerate(orders):
+            sent[p, 0].wait_recv()
+            go(p, 2, self.masks[a], b)
+            go(p, 4, self.masks[a], c)
+        for p, (a, b, c) in enumerate(orders):
+            sent[p, 1].wait_recv()
+            go(p, 5, self.masks[b], c)
+            sent[p, 2].wait_recv()
+            go(p, 6, self.masks[a] | self.masks[b], c)
+        for index in (3, 4, 5, 6):
+            for p in range(3):
+                sent[p, index].wait_recv()
+        for item in sent.values():
+            item.wait_send()
+
+    def scatter(self, buf, one, two, three, beside=None):
+        send, recv = self.sems[2:]
+        orders = [(p, (p + 1) % 3, (p + 2) % 3) for p in range(3)]
+        sent = {}
+
+        def go(p, index, mask, slot, dim):
+            start, size = self.parts[p]
+            rows = pl.ds(start, size)
+            sent[p, index] = remote(
+                buf.at[self.block(mask), rows],
+                slot.at[rows],
+                send.at[p, index],
+                recv.at[p, index],
+                self.peers[dim],
+            )
+            sent[p, index].start()
+
+        def add(p, mask, slot):
+            start, size = self.parts[p]
+            rows = pl.ds(start, size)
+            j = self.block(mask)
+            buf[j, rows] = (buf[j, rows].astype(F32) + slot[rows].astype(F32)).astype(BF)
+
+        for index in range(4):
+            for p, (a, b, c) in enumerate(orders):
+                ma, mb, mc = (self.masks[d] for d in (a, b, c))
+                mask = (mb, mb | ma, ma, 0)[index]
+                go(p, index, mc | mask, one.at[index], c)
+        if beside is not None:
+            beside()
+        for index in range(2):
+            for p, (a, b, c) in enumerate(orders):
+                ma, mb = self.masks[a], self.masks[b]
+                mask = (ma, 0)[index]
+                sent[p, 1 - index].wait_recv()
+                add(p, mb | mask, one.at[1 - index])
+                go(p, 4 + index, mb | mask, two.at[index], b)
+        for p, (a, b, c) in enumerate(orders):
+            ma = self.masks[a]
+            sent[p, 2].wait_recv()
+            add(p, ma, one.at[2])
+            sent[p, 4].wait_recv()
+            add(p, ma, two.at[0])
+            go(p, 6, ma, three, a)
+        for p in range(3):
+            sent[p, 3].wait_recv()
+            add(p, 0, one.at[3])
+            sent[p, 5].wait_recv()
+            add(p, 0, two.at[1])
+            sent[p, 6].wait_recv()
+        for item in sent.values():
+            item.wait_send()
+
+
+def norm_scale(value):
+    return lax.rsqrt(jnp.mean(value * value, axis=-1, keepdims=True) + 1e-06)
+
+
+def norm_back(value, scale, gained):
+    inner = jnp.mean(gained * value, axis=-1, keepdims=True)
+    return scale * gained - value * (scale * scale * scale * inner)
+
+
+ROOT = 0.7978845608028654
+
+
+def gelu_parts(v):
+    t = jnp.tanh(ROOT * (v + 0.044715 * (v * v * v)))
+    value = 0.5 * v * (1.0 + t)
+    slope = 0.5 * (1.0 + t) + 0.5 * v * (1.0 - t * t) * (ROOT * (1.0 + 0.134145 * (v * v)))
+    return value, slope
+
+
+def feed_kernel(
+    hidden,
+    cot,
+    gains,
+    gu_in,
+    dn_in,
+    output,
+    grad_hidden,
+    grad_gains,
+    gu_grad,
+    dn_grad,
+    wg,
+    wu,
+    wd,
+    acts,
+    downs,
+    gate,
+    up,
+    mixed,
+    sums,
+    one,
+    two,
+    three,
+    gsend,
+    grecv,
+    ssend,
+    srecv,
+    local,
+):
+    rows, width = hidden.shape
+    units = gu_in.shape[1] * gu_in.shape[2]
+    half = gu_in.shape[2]
+    wide = wg.shape[0]
+    cube = Cube(rows, gsend, grecv, ssend, srecv)
+    loads = []
+    for i, (source, target) in enumerate(
+        ((gu_in.at[0], wg), (gu_in.at[1], wu), (dn_in, wd))
+    ):
+        for h in range(2):
+            loads.append(
+                pltpu.make_async_copy(
+                    source.at[h], target.at[pl.ds(h * half, half)], local.at[i, h]
+                )
+            )
+            loads[-1].start()
+    for target in (wg, wu, wd):
+        target[units:, :] = jnp.zeros((wide - units, width), BF)
+    greet(cube.peers)
+    me = cube.me
+    value = hidden[...]
+    pre_scale = norm_scale(value)
+    pre_gain = 1.0 + gains[0:1, :]
+    acts[me] = (value * pre_scale * pre_gain).astype(BF)
+    cube.gather(acts)
+    for load in loads:
+        load.wait()
+
+    def forward(j, carry):
+        a = acts[j]
+        g = contract_last(a, wg[...])
+        u = contract_last(a, wu[...])
+        gate[j] = g
+        up[j] = u
+        m = (gelu_parts(g)[0] * u).astype(BF)
+        mixed[j] = m
+        sums[j] = jnp.dot(m, wd[...], preferred_element_type=F32).astype(BF)
+        return carry
+
+    lax.fori_loop(0, 8, forward, 0)
+    cube.scatter(sums, one, two, three)
+    down = sums[me].astype(F32) + three[...].astype(F32)
+    scale = norm_scale(down)
+    post_gain = 1.0 + gains[1:2, :]
+    normal = down * scale
+    output[...] = (value + normal * post_gain).astype(BF)
+    dy = cot[...].astype(F32)
+    grad_gains[1:2, :] = jnp.sum(dy * normal, axis=0, keepdims=True)
+    downs[me] = norm_back(down, scale, dy * post_gain).astype(BF)
+    cube.gather(downs)
+
+    def backward(j, carry):
+        d = contract_last(downs[j], wd[...])
+        value, slope = gelu_parts(gate[j])
+        dg = (d * up[j] * slope).astype(BF)
+        du = (d * value).astype(BF)
+        gate[j] = dg.astype(F32)
+        up[j] = du.astype(F32)
+        sums[j] = (
+            jnp.dot(dg, wg[...], preferred_element_type=F32)
+            + jnp.dot(du, wu[...], preferred_element_type=F32)
+        ).astype(BF)
+        return carry
+
+    lax.fori_loop(0, 8, backward, 0)
+
+    def weights():
+        tokens = 8 * rows
+        acts_all = acts[...].reshape(tokens, width)
+        downs_all = downs[...].reshape(tokens, width)
+        for lo in range(0, wide, 128):
+            hi = min(lo + 128, units)
+            cut = slice(lo, lo + 128)
+            kept = hi - lo
+            dg = gate[:, :, cut].reshape(tokens, 128).astype(BF)
+            du = up[:, :, cut].reshape(tokens, 128).astype(BF)
+            mx = mixed[:, :, cut].reshape(tokens, 128)
+            gu_grad[0, lo:hi, :] = contract_first(dg, acts_all)[:kept].astype(BF)
+            gu_grad[1, lo:hi, :] = contract_first(du, acts_all)[:kept].astype(BF)
+            dn_grad[lo:hi, :] = contract_first(mx, downs_all)[:kept].astype(BF)
+
+    cube.scatter(sums, one, two, three, weights)
+    total = sums[me].astype(F32) + three[...].astype(F32)
+    grad_gains[0:1, :] = jnp.sum(total * (value * pre_scale), axis=0, keepdims=True)
+    grad_hidden[...] = dy + norm_back(value, pre_scale, total * pre_gain)
+
+
+def feed_forward(hidden, cot, gains, gu, dn):
+    rows, width = hidden.shape
+    units = gu.shape[1] * gu.shape[2]
+    wide = -(-units // 128) * 128
+    return pl.pallas_call(
+        feed_kernel,
+        out_shape=(
+            jax.ShapeDtypeStruct((rows, width), BF),
+            jax.ShapeDtypeStruct((rows, width), F32),
+            jax.ShapeDtypeStruct((2, width), F32),
+            jax.ShapeDtypeStruct((2, units, width), BF),
+            jax.ShapeDtypeStruct((units, width), BF),
+        ),
+        in_specs=[VMEM, VMEM, VMEM, ANY, ANY],
+        out_specs=(VMEM,) * 5,
+        scratch_shapes=[
+            pltpu.VMEM((wide, width), BF),
+            pltpu.VMEM((wide, width), BF),
+            pltpu.VMEM((wide, width), BF),
+            pltpu.VMEM((8, rows, width), BF),
+            pltpu.VMEM((8, rows, width), BF),
+            pltpu.VMEM((8, rows, wide), F32),
+            pltpu.VMEM((8, rows, wide), F32),
+            pltpu.VMEM((8, rows, wide), BF),
+            pltpu.VMEM((8, rows, width), BF),
+            pltpu.VMEM((4, rows, width), BF),
+            pltpu.VMEM((2, rows, width), BF),
+            pltpu.VMEM((rows, width), BF),
+            pltpu.SemaphoreType.DMA((3, 7)),
+            pltpu.SemaphoreType.DMA((3, 7)),
+            pltpu.SemaphoreType.DMA((3, 7)),
+            pltpu.SemaphoreType.DMA((3, 7)),
+            pltpu.SemaphoreType.DMA((3, 2)),
+        ],
+        compiler_params=pltpu.CompilerParams(
+            collective_id=3, has_side_effects=True, vmem_limit_bytes=60 * 2**20
+        ),
+    )(hidden, cot, gains, gu, dn)
+
+
+def reduce_kernel(
+    pq,
+    po,
+    pg,
+    pgu,
+    pd,
+    rq,
+    ro,
+    rg,
+    rgu,
+    rd,
+    q_in,
+    q_sum,
+    o_in,
+    o_sum,
+    q_one,
+    o_one,
+    q_two,
+    o_two,
+    q_far,
+    o_far,
+    g_in,
+    g_sum,
+    gu_in,
+    gu_far,
+    d_in,
+    d_far,
+    send,
+    recv,
+    send_f,
+    recv_f,
+    local,
+):
+    dp, ctx, x = place()
+    layers = pq.shape[0]
+    z, y = ctx // 2, ctx % 2
+    cube = ctx // 4
+    sibling = (1 - dp, ctx, x)
+    y2, x2 = jnp.where(dp == 0, 1 - y, y), jnp.where(dp == 0, x, 1 - x)
+    y3, x3 = jnp.where(dp == 0, y, 1 - y), jnp.where(dp == 0, 1 - x, x)
+    mine2, mine3 = jnp.where(dp == 0, y, x), jnp.where(dp == 0, x, y)
+    second = (dp, z * 2 + y2, x2)
+    third = (dp, z * 2 + y3, x3)
+    others = layers_of(z, y, layers, dp, x)
+    group = (ctx % 4) * 2 + x
+    down_to = (cube, group, dp)
+    down_from = (x, ctx // 2 + 4 * dp, ctx % 2)
+    stays = (dp == cube) & (ctx == group) & (x == dp)
+    barrier = pltpu.get_barrier_semaphore()
+    for device in others + [second, third, sibling]:
+        pl.semaphore_signal(barrier, inc=1, device_id=device, device_id_type=MESH)
+
+    @pl.when(jnp.logical_not(stays))
+    def _():
+        for device in (down_to, down_from):
+            pl.semaphore_signal(barrier, inc=1, device_id=device, device_id_type=MESH)
+
+    pl.semaphore_wait(barrier, jnp.where(stays, layers + 2, layers + 4))
+
+    started = []
+
+    def start(copy):
+        copy.start()
+        started.append(copy)
+        return copy
+
+    gu_swap = start(remote(pgu.at[:, 1 - dp], gu_in, send_f.at[0], recv_f.at[0], sibling))
+    d_swap = start(remote(pd.at[1 - dp], d_in, send_f.at[1], recv_f.at[1], sibling))
+    swaps = [
+        start(remote(pq.at[:, :, :, 1 - dp], q_in, send.at[0, 0], recv.at[0, 0], sibling)),
+        start(remote(po.at[:, :, :, 1 - dp], o_in, send.at[1, 0], recv.at[1, 0], sibling)),
+    ]
+    gains0 = start(remote(pg, g_in.at[0], send_f.at[2], recv_f.at[2], sibling))
+    gu_swap.wait_recv()
+    for q in range(2):
+        gu_in[q] = (gu_in[q].astype(F32) + pgu[q, dp].astype(F32)).astype(BF)
+    gu_cross = start(
+        remote(
+            gu_in.at[1 - cube], gu_far, send_f.at[3], recv_f.at[3], (dp, (ctx + 4) % 8, x)
+        )
+    )
+    d_swap.wait_recv()
+    d_in[...] = (d_in[...].astype(F32) + pd[dp].astype(F32)).astype(BF)
+    d_local = pltpu.make_async_copy(d_in, d_far.at[cube], recv_f.at[4])
+    d_move = remote(d_in, d_far.at[cube], send_f.at[4], recv_f.at[4], down_to)
+
+    @pl.when(stays)
+    def _():
+        d_local.start()
+
+    @pl.when(jnp.logical_not(stays))
+    def _():
+        d_move.start()
+
+    gains0.wait_recv()
+    g_sum[0] = pg[...] + g_in[0]
+    gains1 = start(remote(g_sum.at[0], g_in.at[1], send_f.at[5], recv_f.at[5], (dp, ctx, 1 - x)))
+    sets = (
+        (pq, q_in, q_sum, q_one, q_two, q_far, rq),
+        (po, o_in, o_sum, o_one, o_two, o_far, ro),
+    )
+    ones = []
+    for t, (part, came, total, _, _, _, _) in enumerate(sets):
+        swaps[t].wait_recv()
+        for i in range(layers):
+            for a in range(2):
+                for b in range(2):
+                    yy, xx = jnp.where(dp == 0, a, b), jnp.where(dp == 0, b, a)
+                    total[a, b, i] = (
+                        part[i, yy, xx, dp].astype(F32) + came[i, yy, xx].astype(F32)
+                    ).astype(BF)
+        ones.append(
+            start(
+                remote(
+                    total.at[:, 1 - mine3], sets[t][3], send.at[t, 1], recv.at[t, 1], third
+                )
+            )
+        )
+    gains1.wait_recv()
+    g_sum[1] = g_sum[0] + g_in[1]
+    gains2 = start(
+        remote(g_sum.at[1], g_in.at[2], send_f.at[6], recv_f.at[6], (dp, z * 2 + 1 - y, x))
+    )
+    twos = []
+    for t, (_, _, total, first, second_in, _, _) in enumerate(sets):
+        ones[t].wait_recv()
+        for i in range(layers):
+            for a in range(2):
+                total[a, mine3, i] = (
+                    total[a, mine3, i].astype(F32) + first[a, i].astype(F32)
+                ).astype(BF)
+        twos.append(
+            start(
+                remote(
+                    total.at[1 - mine2, mine3],
+                    second_in,
+                    send.at[t, 2],
+                    recv.at[t, 2],
+                    second,
+                )
+            )
+        )
+    gains2.wait_recv()
+    g_sum[2] = g_sum[1] + g_in[2]
+    gains3 = [
+        start(remote(g_sum.at[2], g_in.at[3 + z], send_f.at[8 + i], recv_f.at[8 + i], device))
+        for i, device in enumerate(others)
+    ]
+    own_gains = pltpu.make_async_copy(g_sum.at[2], g_in.at[3 + z], local.at[0])
+    own_gains.start()
+    fars = []
+    for t, (_, _, total, _, second_in, far, _) in enumerate(sets):
+        twos[t].wait_recv()
+        for i in range(layers):
+            total[mine2, mine3, i] = (
+                total[mine2, mine3, i].astype(F32) + second_in[i].astype(F32)
+            ).astype(BF)
+        fars.append(
+            [
+                start(
+                    remote(
+                        total.at[mine2, mine3, lax.rem(z + i + 1, layers)],
+                        far.at[i],
+                        send.at[t, 3 + i],
+                        recv.at[t, 3 + i],
+                        device,
+                    )
+                )
+                for i, device in enumerate(others)
+            ]
+        )
+    last = []
+    for t, (_, _, total, _, _, far, result) in enumerate(sets):
+        value = total[mine2, mine3, z].astype(F32)
+        for i in range(layers - 1):
+            fars[t][i].wait_recv()
+            value = value + far[i].astype(F32)
+        result[dp] = value.astype(BF)
+        last.append(start(remote(result.at[dp], result.at[dp], send.at[t, 6], recv.at[t, 6], sibling)))
+    own_gains.wait()
+    for copy in gains3:
+        copy.wait_recv()
+    value = g_in[3]
+    for i in range(1, layers):
+        value = value + g_in[3 + i]
+    rg[...] = value
+    gu_cross.wait_recv()
+    rgu[dp] = (gu_in[cube].astype(F32) + gu_far[...].astype(F32)).astype(BF)
+    last.append(start(remote(rgu.at[dp], rgu.at[dp], send_f.at[11], recv_f.at[11], sibling)))
+    d_local.wait()
+    landed = d_far.at[dp]
+    d_last = start(remote(landed, landed, send_f.at[12], recv_f.at[12], sibling))
+    d_last.wait_recv()
+    rd[...] = (d_far[0].astype(F32) + d_far[1].astype(F32)).astype(BF)
+    for copy in last:
+        copy.wait_recv()
+    for copy in started:
+        copy.wait_send()
+
+    @pl.when(jnp.logical_not(stays))
+    def _():
+        d_move.wait_send()
+
+
+def reduce_grads(pq, po, pg, pgu, pd):
+    layers = pq.shape[0]
+    hq, width = pq.shape[-2:]
+    ho = po.shape[-2]
+    hgu = pgu.shape[-2]
+    down_rows = pd.shape[-2]
+    return pl.pallas_call(
+        reduce_kernel,
+        out_shape=(
+            jax.ShapeDtypeStruct((2, hq, width), BF),
+            jax.ShapeDtypeStruct((2, ho, width), BF),
+            jax.ShapeDtypeStruct(pg.shape, F32),
+            jax.ShapeDtypeStruct((2, hgu, width), BF),
+            jax.ShapeDtypeStruct((down_rows, width), BF),
+        ),
+        in_specs=[VMEM] * 5,
+        out_specs=(VMEM,) * 5,
+        scratch_shapes=[
+            pltpu.VMEM((layers, 2, 2, hq, width), BF),
+            pltpu.VMEM((2, 2, layers, hq, width), BF),
+            pltpu.VMEM((layers, 2, 2, ho, width), BF),
+            pltpu.VMEM((2, 2, layers, ho, width), BF),
+            pltpu.VMEM((2, layers, hq, width), BF),
+            pltpu.VMEM((2, layers, ho, width), BF),
+            pltpu.VMEM((layers, hq, width), BF),
+            pltpu.VMEM((layers, ho, width), BF),
+            pltpu.VMEM((layers - 1, hq, width), BF),
+            pltpu.VMEM((layers - 1, ho, width), BF),
+            pltpu.VMEM((3 + layers,) + pg.shape, F32),
+            pltpu.VMEM((3,) + pg.shape, F32),
+            pltpu.VMEM((2, hgu, width), BF),
+            pltpu.VMEM((hgu, width), BF),
+            pltpu.VMEM((down_rows, width), BF),
+            pltpu.VMEM((2, down_rows, width), BF),
+            pltpu.SemaphoreType.DMA((2, 7)),
+            pltpu.SemaphoreType.DMA((2, 7)),
+            pltpu.SemaphoreType.DMA((13,)),
+            pltpu.SemaphoreType.DMA((13,)),
+            pltpu.SemaphoreType.DMA((1,)),
+        ],
+        compiler_params=pltpu.CompilerParams(
+            collective_id=4, has_side_effects=True, vmem_limit_bytes=60 * 2**20
+        ),
+    )(pq, po, pg, pgu, pd)
+
+
+def moves_tokens(mesh):
+    return mesh.shape["ctx"] == 8 and mesh.shape["fsdp"] == 2 and mesh.shape["dp"] == 2
+
+
+def move_tokens_body(
+    tokens,
+    cotangent,
+    segments,
+    qkv_weight,
+    out_weight,
+    gate_up_weight,
+    down_weight,
+    gains,
+    qkv_first,
+    out_first,
+    gate_up_first,
+    down_first,
+    gains_first,
+    qkv_second,
+    out_second,
+    gate_up_second,
+    down_second,
+    gains_second,
+):
+    rows = tokens.shape[1]
+    width = tokens.shape[2]
+    length = segments.shape[1]
+    query_width = H * HD
+    scale = HD ** (-0.5)
+    layers = lax.axis_size("ctx") // 2
+    reach = lax.axis_size("ctx") // 2 + 1
+    front = reach * rows
+    window = front + rows
+    ctx = lax.axis_index("ctx")
+    chip = ctx * 2 + lax.axis_index("fsdp")
+    own_gains = gains.shape[0]
+    gain_rows = -(-own_gains * 4 * layers // 1024) * 8 + 8
+
+    def halves(weight):
+        return weight.astype(BF).reshape(2, weight.shape[0] // 2, width)
+
+    gain_part = lax.dynamic_update_slice_in_dim(
+        jnp.zeros((gain_rows * 128,), F32),
+        gains.astype(BF).astype(F32),
+        chip * own_gains,
+        0,
+    )
+    qkv_parts, out_parts, gain_parts, gu, dn = gather_weights(
+        halves(qkv_weight),
+        halves(out_weight),
+        gain_part.reshape(2, gain_rows // 2, 128),
+        halves(gate_up_weight),
+        down_weight.astype(BF),
+        layers,
+    )
+    qkv_full = qkv_parts.reshape(-1, width)
+    out_full = out_parts.reshape(-1, width)
+    gain_all = jnp.sum(gain_parts, axis=(0, 1, 2)).reshape(-1)
+    gain_input = gain_all[:width]
+    gain_attend = gain_all[width : 2 * width]
+    gain_pre = gain_all[2 * width : 3 * width]
+    gain_post = gain_all[3 * width : 4 * width]
+    gain_query = gain_all[4 * width : 4 * width + HD]
+    gain_key = gain_all[4 * width + HD : 4 * width + 2 * HD]
+    first_row = ctx * rows
+    sequence_ids = segments[0]
+    query_ids = lax.dynamic_slice_in_dim(sequence_ids, first_row, rows, 0)
+    query_pos = first_row + jnp.arange(rows, dtype=jnp.int32)
+    angles = rope_angles(sequence_ids, first_row, rows)
+    window_pos = first_row - front + jnp.arange(window, dtype=jnp.int32)
+    padded_ids = jnp.concatenate([jnp.full((front,), -1, dtype=jnp.int32), sequence_ids])
+    window_ids = lax.dynamic_slice_in_dim(padded_ids, first_row, window, 0)
+    allowed = (window_pos[None, :] <= query_pos[:, None]) & (
+        window_ids[None, :] == query_ids[:, None]
+    )
+    allowed = allowed[:, None, :]
+    x_rows = tokens[0].astype(F32)
+    normed, input_back = jax.vjp(normalize, x_rows, gain_input)
+    normed_low = normed.astype(BF)
+    projected = contract_last(normed_low, qkv_full)
+    proj_query = projected[:, :query_width].reshape(rows, H, HD)
+    proj_key = projected[:, query_width : query_width + HD]
+    proj_value = projected[:, query_width + HD :]
+
+    def query_key(part_query, part_key, query_gain, key_gain):
+        return (
+            rotate(normalize(part_query, query_gain), angles[:, None, :]),
+            rotate(normalize(part_key, key_gain), angles),
+        )
+
+    (rotated_query, rotated_key), rotate_back = jax.vjp(
+        query_key, proj_query, proj_key, gain_query, gain_key
+    )
+    query = rotated_query.astype(BF)
+    pairs = jnp.concatenate([rotated_key.astype(BF), proj_value.astype(BF)], axis=1)
+    pairs_all = gather_keys(pairs, layers).reshape(length, 2 * HD)
+    blank = jnp.zeros((front, 2 * HD), BF)
+    pairs_near = lax.dynamic_slice_in_dim(
+        jnp.concatenate([blank, pairs_all]), first_row, window, 0
+    )
+    keys, values = pairs_near[:, :HD], pairs_near[:, HD:]
+    scores = jnp.einsum("thd,ld->thl", query, keys, preferred_element_type=F32) * scale
+    masked = jnp.where(allowed, scores, -1e30)
+    largest = jnp.max(masked, axis=-1, keepdims=True)
+    log_total = largest + jnp.log(jnp.sum(jnp.exp(masked - largest), axis=-1, keepdims=True))
+    probs = jnp.exp(masked - log_total)
+    probs_low = probs.astype(BF)
+    attended = jnp.einsum("thl,ld->thd", probs_low, values, preferred_element_type=F32)
+    attended = attended.reshape(rows, query_width).astype(BF)
+    branch = jnp.dot(attended, out_full, preferred_element_type=F32)
+    branch_normed, attend_back = jax.vjp(normalize, branch, gain_attend)
+    hidden = x_rows + branch_normed
+    output, grad_hidden, grad_gain_feed, gate_up_grad, down_grad = feed_forward(
+        hidden, cotangent[0], jnp.stack([gain_pre, gain_post]), gu, dn
+    )
+    grad_branch, grad_gain_attend = attend_back(grad_hidden)
+    grad_branch_low = grad_branch.astype(BF)
+    out_grad = contract_first(attended, grad_branch_low)
+    grad_attended = contract_last(grad_branch_low, out_full).astype(BF).reshape(rows, H, HD)
+    grad_probs = jnp.einsum("thd,ld->thl", grad_attended, values, preferred_element_type=F32)
+    row_term = jnp.sum(probs * grad_probs, axis=-1, keepdims=True)
+    grad_scores = (probs * (grad_probs - row_term)).astype(BF)
+    grad_query = jnp.einsum("thl,ld->thd", grad_scores, keys, preferred_element_type=F32) * scale
+    grad_keys = jnp.einsum("thl,thd->ld", grad_scores, query, preferred_element_type=F32) * scale
+    grad_values = jnp.einsum("thl,thd->ld", probs_low, grad_attended, preferred_element_type=F32)
+    grad_pairs = jnp.concatenate([grad_keys, grad_values], axis=1)
+    spread = lax.dynamic_update_slice_in_dim(
+        jnp.zeros((front + length, 2 * HD), F32), grad_pairs, first_row, 0
+    )[front:]
+    grad_pair = scatter_keys(spread.astype(BF).reshape(layers, 2, rows, 2 * HD))
+    grad_key, grad_value = grad_pair[:, :HD], grad_pair[:, HD:]
+    grad_proj_query, grad_proj_key, grad_gain_query, grad_gain_key = rotate_back(
+        (grad_query, grad_key)
+    )
+    grad_projected = jnp.concatenate(
+        [grad_proj_query.reshape(rows, query_width), grad_proj_key, grad_value], axis=1
+    ).astype(BF)
+    qkv_grad = contract_first(grad_projected, normed_low)
+    grad_normed = jnp.dot(grad_projected, qkv_full, preferred_element_type=F32)
+    grad_from_input, grad_gain_input = input_back(grad_normed)
+    input_grad = grad_hidden + grad_from_input
+    gains_grad = jnp.concatenate(
+        [
+            grad_gain_input,
+            grad_gain_attend,
+            grad_gain_feed.reshape(-1),
+            grad_gain_query,
+            grad_gain_key,
+        ]
+    )
+    gains_grad = jnp.pad(gains_grad, (0, gain_rows * 128 - gains_grad.shape[0]))
+    qkv_low, out_low, gains_sum, gate_up_low, down_low = reduce_grads(
+        qkv_grad.astype(BF).reshape(layers, 2, 2, 2, -1, width),
+        out_grad.astype(BF).reshape(layers, 2, 2, 2, -1, width),
+        gains_grad.reshape(gain_rows, 128),
+        gate_up_grad.reshape(2, 2, -1, width),
+        down_grad.reshape(2, -1, width),
+    )
+    qkv_total = qkv_low.reshape(-1, width).astype(F32)
+    out_total = out_low.reshape(-1, width).astype(F32)
+    gate_up_total = gate_up_low.reshape(-1, width).astype(F32)
+    down_total = down_low.astype(F32)
+    gains_total = lax.dynamic_slice_in_dim(gains_sum.reshape(-1), chip * own_gains, own_gains, 0)
+    qkv_new, qkv_first_new, qkv_second_new = adamw(qkv_weight, qkv_total, qkv_first, qkv_second)
+    out_new, out_first_new, out_second_new = adamw(out_weight, out_total, out_first, out_second)
+    gate_up_new, gate_up_first_new, gate_up_second_new = adamw(
+        gate_up_weight, gate_up_total, gate_up_first, gate_up_second
+    )
+    down_new, down_first_new, down_second_new = adamw(
+        down_weight, down_total, down_first, down_second
+    )
+    gains_new, gains_first_new, gains_second_new = adamw(
+        gains, gains_total, gains_first, gains_second
+    )
+    return (
+        output[None],
+        input_grad[None],
+        qkv_total,
+        out_total,
+        gate_up_total,
+        down_total,
+        gains_total,
+        qkv_new,
+        out_new,
+        gate_up_new,
+        down_new,
+        gains_new,
+        qkv_first_new,
+        out_first_new,
+        gate_up_first_new,
+        down_first_new,
+        gains_first_new,
+        qkv_second_new,
+        out_second_new,
+        gate_up_second_new,
+        down_second_new,
+        gains_second_new,
+    )
+
+
 def solution(mesh):
     in_specs = (
         P(("dp", "fsdp"), "ctx", None),
@@ -329,4 +1317,5 @@
         P(("ctx", "fsdp"), None),
         P(("ctx", "fsdp")),
     )
+    body = move_tokens_body if moves_tokens(mesh) else gather_weights_body
     return jax.shard_map(body, mesh=mesh, in_specs=in_specs, out_specs=out_specs, check_vma=False)

time: 2690 us -> 430 us (0.16)
  waiting for transfers between devices: 2250 us -> 0 us
  Pallas kernels: 0 us -> 355 us
  blocking collectives: 222 us -> 0 us
  matrix products: 120 us -> 17.6 us
    reduce_scatter x6 -> x0, waiting for transfers between devices: 1770 us -> none  [the longest x1 920 us: body(): lax.psum_scatter(gate_up_grad, ('ctx', 'fsdp'), scatter_dimension=0, tile...]
    all_gather x4 -> x0, waiting for transfers between devices: 481 us -> none  [the longest x1 318 us: body(): lax.all_gather(gate_up_weight.astype(jnp.bfloat16), ('ctx', 'fsdp'), axis...]
    pallas_call x0 -> x5, Pallas kernels: none -> 355 us  [the longest x1 106 us: gather_weights(): pl.pallas_call(gather_kernel, out_shape=(full(wq), full(wo), full(gn), ja...]
    unnamed x2 -> x0, blocking collectives: 155 us -> none
    all_gather x2 -> x0, blocking collectives: 64.2 us -> none  [the longest x1 32.1 us: body(): lax.all_gather(value_low, 'ctx', axis=0, tiled=True)]
    dot_general x4 -> x2, matrix products: 46.8 us -> 5.11 us  [contract_first(): lax.dot_general(left, right, (((0,), (0,)), ((), ())), preferred_element_...]
    dot_general x4 -> x2, matrix products: 35 us -> 4.17 us  [contract_last(): lax.dot_general(left, right, (((1,), (1,)), ((), ())), preferred_element_...]
    dot_general x10 -> x8, matrix products: 38.2 us -> 8.36 us  [the longest x1 2.38 us: move_tokens_body(): branch = jnp.dot(attended, out_full, preferred_element_type=F32)]
  transfers between devices with their start and end apart: 11 -> 0, of which waited for: 8 -> 0; matrix products, arithmetic and copies ran while one was open for 5% -> 0% of each run, Pallas kernels for 0% -> 0%
where the time goes in v1:
time: 430 us; the launch traced here: 429 us
  Pallas kernels  355 us (83%)
  other arithmetic  44.5 us (10%)
  matrix products  17.6 us (4%)
  local copies, waits for them, and re-layouts  10.9 us (3%)
    pallas_call x1, Pallas kernels, gather_weights(): pl.pallas_call(gather_kernel, out_shape=(full(wq), full(wo), full(gn), ja...  106 us
    pallas_call x1, Pallas kernels, feed_forward(): pl.pallas_call(feed_kernel, out_shape=(jax.ShapeDtypeStruct((rows, width)...  103 us
    pallas_call x1, Pallas kernels, reduce_grads(): pl.pallas_call(reduce_kernel, out_shape=(jax.ShapeDtypeStruct((2, hq, wid...  101 us
    pallas_call x1, Pallas kernels, gather_keys(): pl.pallas_call(keys_kernel, out_shape=jax.ShapeDtypeStruct((layers, 2) +...  25.8 us
    pallas_call x1, Pallas kernels, scatter_keys(): pl.pallas_call(scatter_keys_kernel, out_shape=jax.ShapeDtypeStruct((rows,...  19.3 us
    sub x5, other arithmetic, adamw(): weight - 0.03 * (first_hat / (jnp.sqrt(second_hat) + 1e-08) + 0.1 * weight)  17.9 us

profile of v1, /device:TPU:0, one launch (start us, length us, event | category | flops | bytes accessed | tf_op | source)
XLA Modules:
  0.0 429.4 jit_solution(10837905045986243822)
XLA Ops:
  0.7 1.7 convert_element_type.101
  2.4 1.6 convert_element_type.102
  4.8 3.8 convert_element_type.105
  8.6 1.1 convert_element_type.106.wd
  9.6 105.8 %shard_map.345 = (bf16[4,2,2,2,48,1152]{5,4,3,2,1,0:T(8,128)(2,1)}, bf16[4,2,2,2,32,1152]{5,4,3,2,1,0:T(8,128)(2,1)}, f32[4,2,2,2,24,128]{5,4,3,2,1,0:T(8,128)},...) custom-call(bf16[2,48,1152]{2,1,0:T(8,128)(2,1)} %bitcast.138, bf16[2,32,1152]{2,1,0:T(8,128)(2,1)} %bitcast.139, ...), custom_call_target="tpu_custom_call" | custom-call | tf_op jit(solution)/shard_map/pallas_call | solution.py:427
  115.4 1.0 reduce_sum.141
  117.1 3.3 fusion.33
  122.5 25.8 %shard_map.346 = bf16[4,2,128,512]{3,2,1,0:T(8,128)(2,1)} custom-call(bf16[128,512]{1,0:T(8,128)(2,1)} %pad_maximum_fusion.7.part), custom_call_target="tpu_custom_call" | custom-call | tf_op jit(solution)/shard_map/pallas_call | solution.py:475
  152.5 2.4 multiply_reduce_fusion.3
  154.9 1.0 fusion.7.hidden
  156.5 103.4 %shard_map.347 = (bf16[128,1152]{1,0:T(8,128)(2,1)}, f32[128,1152]{1,0:T(8,128)}, f32[2,1152]{1,0:T(2,128)}, bf16[2,864,1152]{2,1,0:T(8,128)(2,1)}, bf16[864,1152]{1,0:T(8,128)(2,1)}) custom-call(f32[128,1152]{1,0:T(8,128)} %fusion.7.hidden, bf16[128,1152]{1,0:T(8,128)(2,1)} %bitcast.140, f32[2,1152]{1,0:T(2,128)} %pad_maximum_fusion.8.gains, ...), custom_call_target="tpu_custom_call" | custom-call | tf_op jit(solution)/shard_map/pallas_call | solution.py:789
  259.9 2.0 multiply_reduce_fusion.1
  261.8 1.2 fusion.17
  268.0 1.0 slice.109
  269.0 19.3 %shard_map.348 = f32[128,512]{1,0:T(8,128)} custom-call(bf16[4,2,128,512]{3,2,1,0:T(8,128)(2,1)} %bitcast.129), custom_call_target="tpu_custom_call" | custom-call | tf_op jit(solution)/shard_map/pallas_call | solution.py:519
  288.3 0.9 slice.110
  290.0 1.2 fusion.56
  291.2 1.6 multiply_reduce_fusion.6
  292.8 1.0 fusion.43
  295.2 1.1 multiply_add_fusion.5
  296.3 1.9 multiply_reduce_fusion.4
  299.1 1.8 copy.107
  301.0 2.0 fusion.12
  303.1 1.0 fusion.19
  304.1 2.9 convolution_convert_fusion
  307.1 2.2 convolution_convert_fusion.1
  310.0 100.6 %shard_map.349 = (bf16[2,48,1152]{2,1,0:T(8,128)(2,1)}, bf16[2,32,1152]{2,1,0:T(8,128)(2,1)}, f32[48,128]{1,0:T(8,128)}, bf16[2,432,1152]{2,1,0:T(8,128)(2,1)}, bf16[432,1152]{1,0:T(8,128)(2,1)}) custom-call(bf16[4,2,2,2,48,1152]{5,4,3,2,1,0:T(8,128)(2,1)} %bitcast.119, bf16[4,2,2,2,32,1152]{5,4,3,2,1,0:T(8,128)(2,1)} %bitcast.127, ...), custom_call_target="tpu_custom_call" | custom-call | tf_op jit(solution)/shard_map/pallas_call | solution.py:1035
  410.6 2.8 multiply_subtract_fusion.2
  413.4 1.1 multiply_subtract_fusion.3
  414.6 9.0 %multiply_subtract_fusion = (f32[864,1152]{1,0:T(8,128)}, f32[864,1152]{1,0:T(8,128)}, f32[864,1152]{1,0:T(8,128)}, f32[864,1152]{1,0:T(8,128)}) fusion(f32[864,1152]{1,0:T(8,128)S(1)} %copy-done.1, f32[864,1152]{1,0:T(8,128)S(1)} %copy-done.12, f32[864,1152]{1,0:T(8,128)} %param.33, bf16[2,432,1152]{2,1,0:T(8,128)(2,1)} %get-tuple-element.49), kind=kLoop, calls=%fused_computation.3 | loop fusion | flops 15925248 | bytes 29859840 | tf_op jit(solution)/shard_map/sub | solution.py:67
  423.7 3.6 multiply_subtract_fusion.1
  427.3 1.4 multiply_subtract_fusion.4
  (181 shorter events, 17.4 us)
Async XLA Ops:
  4.8 3.8 copy-start.35
  4.8 3.8 copy-start.8
  9.6 106.8 %copy-start.5 = (bf16[1,128,1152]{2,1,0:T(8,128)(2,1)S(1)}, bf16[1,128,1152]{2,1,0:T(8,128)(2,1)}, u32[]{:S(2)}) copy-start(bf16[1,128,1152]{2,1,0:T(8,128)(2,1)} %param.18) | copy-start | bytes 884740
  117.1 3.3 copy-start.44
  117.1 3.4 copy-start.39
  120.4 27.9 %copy-start.11 = (f32[128,1536]{1,0:T(8,128)}, f32[128,1536]{1,0:T(8,128)S(1)}, u32[]{:S(2)}) copy-start(f32[128,1536]{1,0:T(8,128)S(1)} %fusion.33) | copy-start | bytes 2359300
  120.4 27.9 %copy-start.52 = (f32[128]{0:T(128)}, f32[128]{0:T(128)S(1)}, u32[]{:S(2)}) copy-start(f32[128]{0:T(128)S(1)} %multiply_exponential_fusion) | copy-start | bytes 1540
  120.7 27.7 %copy-start.48 = (f32[128]{0:T(128)}, f32[128]{0:T(128)S(1)}, u32[]{:S(2)}) copy-start(f32[128]{0:T(128)S(1)} %get-tuple-element.105) | copy-start | bytes 1540
  120.7 27.9 %copy-start.37 = (f32[256]{0:T(256)}, f32[256]{0:T(256)S(1)}, u32[]{:S(2)}) copy-start(f32[256]{0:T(256)S(1)} %get-tuple-element.93) | copy-start | bytes 3076
  120.7 28.2 %copy-start.40 = (f32[256]{0:T(256)}, f32[256]{0:T(256)S(1)}, u32[]{:S(2)}) copy-start(f32[256]{0:T(256)S(1)} %get-tuple-element.92) | copy-start | bytes 3076
  120.9 27.5 %copy-start.58 = (f32[128]{0:T(128)}, f32[128]{0:T(128)S(1)}, u32[]{:S(2)}) copy-start(f32[128]{0:T(128)S(1)} %multiply_reduce_fusion.8) | copy-start | bytes 1540
  121.8 27.3 %copy-start.25 = (f32[128,128]{1,0:T(8,128)}, f32[128,128]{1,0:T(8,128)S(1)}, u32[]{:S(2)}) copy-start(f32[128,128]{1,0:T(8,128)S(1)} %get-tuple-element.94) | copy-start | bytes 196612
  121.8 27.3 %copy-start.26 = (f32[128,128]{1,0:T(8,128)}, f32[128,128]{1,0:T(8,128)S(1)}, u32[]{:S(2)}) copy-start(f32[128,128]{1,0:T(8,128)S(1)} %get-tuple-element.95) | copy-start | bytes 196612
  267.9 22.1 %copy-start.49 = (f32[128]{0:T(128)S(1)}, f32[128]{0:T(128)}, u32[]{:S(2)}) copy-start(f32[128]{0:T(128)} %copy-done.48) | copy-start | bytes 1540
  267.9 22.1 %copy-start.53 = (f32[128]{0:T(128)S(1)}, f32[128]{0:T(128)}, u32[]{:S(2)}) copy-start(f32[128]{0:T(128)} %copy-done.52) | copy-start | bytes 1540
  267.9 23.3 %copy-start.38 = (f32[256]{0:T(256)S(1)}, f32[256]{0:T(256)}, u32[]{:S(2)}) copy-start(f32[256]{0:T(256)} %copy-done.37) | copy-start | bytes 3076
  267.9 23.3 %copy-start.47 = (f32[128]{0:T(128)S(1)}, f32[128]{0:T(128)}, u32[]{:S(2)}) copy-start(f32[128]{0:T(128)} %copy-done.46) | copy-start | bytes 1540
  267.9 24.9 %copy-start.59 = (f32[128]{0:T(128)S(1)}, f32[128]{0:T(128)}, u32[]{:S(2)}) copy-start(f32[128]{0:T(128)} %copy-done.58) | copy-start | bytes 1540
  268.0 26.6 %copy-start.14 = (bf16[128,4,768]{2,0,1:T(8,128)(2,1)S(1)}, bf16[128,4,768]{2,0,1:T(8,128)(2,1)}, u32[]{:S(2)}) copy-start(bf16[128,4,768]{2,0,1:T(8,128)(2,1)} %copy-done.13) | copy-start | bytes 2359300
  294.6 3.6 copy-start.4
  294.6 3.6 copy-start.41
  295.2 5.7 %copy-start.2 = (bf16[4,2,2,2,48,1152]{5,4,3,2,1,0:T(8,128)(2,1)S(1)}, bf16[4,2,2,2,48,1152]{5,4,3,2,1,0:T(8,128)(2,1)}, u32[]{:S(2)}) copy-start(bf16[4,2,2,2,48,1152]{5,4,3,2,1,0:T(8,128)(2,1)} %get-tuple-element.38) | copy-start | bytes 10616836
  310.0 104.5 %copy-start.12 = (f32[864,1152]{1,0:T(8,128)S(1)}, f32[864,1152]{1,0:T(8,128)}, u32[]{:S(2)}) copy-start(f32[864,1152]{1,0:T(8,128)} %param.28) | copy-start | bytes 11943940
  410.6 3.9 copy-start.1
  414.5 9.1 %copy-start.9 = (f32[432,1152]{1,0:T(8,128)S(1)}, f32[432,1152]{1,0:T(8,128)}, u32[]{:S(2)}) copy-start(f32[432,1152]{1,0:T(8,128)} %param.24) | copy-start | bytes 5971972
  414.5 9.1 %copy-start.19 = (f32[432,1152]{1,0:T(8,128)S(1)}, f32[432,1152]{1,0:T(8,128)}, u32[]{:S(2)}) copy-start(f32[432,1152]{1,0:T(8,128)} %param.29) | copy-start | bytes 5971972
  414.5 9.1 %copy-start.20 = (f32[432,1152]{1,0:T(8,128)S(1)}, f32[432,1152]{1,0:T(8,128)}, u32[]{:S(2)}) copy-start(f32[432,1152]{1,0:T(8,128)} %param.34) | copy-start | bytes 5971972
  414.6 9.1 %copy-start.22 = (bf16[432,1152]{1,0:T(8,128)(2,1)S(1)}, bf16[432,1152]{1,0:T(8,128)(2,1)}, u32[]{:S(2)}) copy-start(bf16[432,1152]{1,0:T(8,128)(2,1)} %get-tuple-element.50) | copy-start | bytes 2985988
  423.6 3.7 copy-start.43
  423.6 3.7 copy-start.54
  423.7 3.7 copy-start.55
  423.7 5.0 %copy-start.33 = (bf16[128,1152]{1,0:T(8,128)(2,1)S(1)}, bf16[128,1152]{1,0:T(8,128)(2,1)}, u32[]{:S(2)}) copy-start(bf16[128,1152]{1,0:T(8,128)(2,1)} %get-tuple-element.42) | copy-start | bytes 884740
  (28 other events, 53.2 us)

commit v2 on v0

--- a/solution.py
+++ b/solution.py
@@ -1,7 +1,17 @@
+import functools
+
 import jax
 import jax.numpy as jnp
 from jax import lax
+from jax.experimental import pallas as pl
+from jax.experimental.pallas import tpu as pltpu
 from jax.sharding import PartitionSpec as P
+
+MESH = pl.DeviceIdType.MESH
+ANY = pl.BlockSpec(memory_space=pl.ANY)
+VMEM = pl.BlockSpec(memory_space=pltpu.VMEM)
+BF = jnp.bfloat16
+F32 = jnp.float32
 
 H = 4
 HD = 256
@@ -24,12 +34,10 @@
     )
 
 
-def rope_angles(segments):
-    count = segments.shape[0]
-    index = jnp.arange(count, dtype=jnp.int32)
-    change = jnp.concatenate([jnp.ones((1,), dtype=jnp.bool_), segments[1:] != segments[:-1]])
-    starts = lax.cummax(jnp.where(change, index, 0), axis=0)
-    offset = (index - starts).astype(jnp.float32)
+def rope_angles(segments, first, rows):
+    own = lax.dynamic_slice_in_dim(segments, first, rows, 0)
+    starts = jnp.sum((segments[None, :] < own[:, None]).astype(jnp.int32), axis=1)
+    offset = (first + jnp.arange(rows, dtype=jnp.int32) - starts).astype(jnp.float32)
     inverse = jnp.exp(-jnp.log(1000000.0) * (2.0 * jnp.arange(HD // 2, dtype=jnp.float32)) / HD)
     return offset[:, None] * inverse[None, :]
 
@@ -60,7 +68,7 @@
     return (weight_new, first_new, second_new)
 
 
-def body(
+def gather_weights_body(
     tokens,
     cotangent,
     segments,
@@ -102,7 +110,7 @@
     gain_key = gain_all[4 * width + HD :]
     first_row = lax.axis_index("ctx") * rows
     sequence_ids = segments[0]
-    angles = lax.dynamic_slice_in_dim(rope_angles(sequence_ids), first_row, rows, 0)
+    angles = rope_angles(sequence_ids, first_row, rows)
     query_ids = lax.dynamic_slice_in_dim(sequence_ids, first_row, rows, 0)
     query_pos = first_row + jnp.arange(rows, dtype=jnp.int32)
     window_pos = first_row - front + jnp.arange(window, dtype=jnp.int32)
@@ -284,6 +292,971 @@
     )
 
 
+def place():
+    return lax.axis_index("dp"), lax.axis_index("ctx"), lax.axis_index("fsdp")
+
+
+class Links:
+    def __init__(self, send, recv):
+        self.send, self.recv, self.used, self.sent, self.some = send, recv, 0, [], []
+
+    def slot(self):
+        self.used += 1
+        return self.send.at[self.used - 1], self.recv.at[self.used - 1]
+
+    def make(self, source, target, device):
+        send, recv = self.slot()
+        return pltpu.make_async_remote_copy(
+            src_ref=source,
+            dst_ref=target,
+            send_sem=send,
+            recv_sem=recv,
+            device_id=device,
+            device_id_type=MESH,
+        )
+
+    def go(self, source, target, device):
+        copy = self.make(source, target, device)
+        copy.start()
+        self.sent.append(copy)
+        return copy
+
+    def go_if(self, condition, source, target, device):
+        copy = self.make(source, target, device)
+        pl.when(condition)(copy.start)
+        self.some.append((condition, copy))
+        return copy
+
+    def drain(self):
+        for copy in self.sent:
+            copy.wait_send()
+        for condition, copy in self.some:
+            pl.when(condition)(copy.wait_send)
+        self.sent, self.some = [], []
+
+
+TILE = 16
+AXES = (1, 2, 4)
+ORDERS = ((0, 1, 2), (1, 2, 0), (2, 0, 1))
+
+
+class Cube:
+    def __init__(self, links, tiles):
+        dp, ctx, x = place()
+        self.links, self.tiles = links, tiles
+        self.me = (ctx % 4) * 2 + x
+        self.peers = (
+            (dp, ctx, 1 - x),
+            (dp, ctx + 1 - 2 * (ctx % 2), x),
+            (dp, ctx + 2 - 4 * (ctx // 2 % 2), x),
+        )
+        third = -(-tiles // 3)
+        self.parts = ((0, third), (third, third), (2 * third, tiles - 2 * third))
+
+    def block(self, mask):
+        result = 0
+        for bit in AXES:
+            own = self.me // bit % 2
+            result = result + bit * (1 - own if mask & bit else own)
+        return result
+
+    def cut(self, buf, p, mask):
+        start, size = self.parts[p]
+        return buf.at[pl.ds(self.block(mask) * self.tiles + start, size)]
+
+    def gather(self, buf):
+        sent = {}
+
+        def go(p, index, mask, dim):
+            ref = self.cut(buf, p, mask)
+            sent[p, index] = self.links.go(ref, ref, self.peers[dim])
+
+        for index, where in ((0, 0), (1, 1), (3, 2)):
+            for p, order in enumerate(ORDERS):
+                go(p, index, 0, order[where])
+        for p, (a, b, c) in enumerate(ORDERS):
+            sent[p, 0].wait_recv()
+            go(p, 2, AXES[a], b)
+            go(p, 4, AXES[a], c)
+        for p, (a, b, c) in enumerate(ORDERS):
+            sent[p, 1].wait_recv()
+            go(p, 5, AXES[b], c)
+            sent[p, 2].wait_recv()
+            go(p, 6, AXES[a] | AXES[b], c)
+        for index in (3, 4, 5, 6):
+            for p in range(3):
+                sent[p, index].wait_recv()
+
+    def scatter(self, buf, one, two, three, beside=None):
+        sent = {}
+
+        def go(p, index, mask, slot, dim):
+            start, size = self.parts[p]
+            target = slot.at[pl.ds(start, size)]
+            sent[p, index] = self.links.go(self.cut(buf, p, mask), target, self.peers[dim])
+
+        def add(p, mask, slot):
+            start, size = self.parts[p]
+            mine = self.cut(buf, p, mask)
+            mine[...] = (mine[...].astype(F32) + slot[pl.ds(start, size)].astype(F32)).astype(BF)
+
+        for index in range(4):
+            for p, (a, b, c) in enumerate(ORDERS):
+                mask = (AXES[b], AXES[b] | AXES[a], AXES[a], 0)[index]
+                go(p, index, AXES[c] | mask, one.at[index], c)
+        if beside is not None:
+            beside()
+        for index in range(2):
+            for p, (a, b, c) in enumerate(ORDERS):
+                mask = AXES[b] | (AXES[a], 0)[index]
+                sent[p, 1 - index].wait_recv()
+                add(p, mask, one.at[1 - index])
+                go(p, 4 + index, mask, two.at[index], b)
+        for p, (a, b, c) in enumerate(ORDERS):
+            sent[p, 2].wait_recv()
+            add(p, AXES[a], one.at[2])
+            sent[p, 4].wait_recv()
+            add(p, AXES[a], two.at[0])
+            go(p, 6, AXES[a], three, a)
+        for p in range(3):
+            sent[p, 3].wait_recv()
+            add(p, 0, one.at[3])
+            sent[p, 5].wait_recv()
+            add(p, 0, two.at[1])
+            sent[p, 6].wait_recv()
+
+
+def flat(value):
+    return value.reshape(-1, value.shape[-1])
+
+
+def tiled(value):
+    return value.reshape(-1, TILE, value.shape[-1])
+
+
+def norm_scale(value):
+    return lax.rsqrt(jnp.mean(value * value, axis=-1, keepdims=True) + 1e-06)
+
+
+def norm_back(value, scale, gained):
+    inner = jnp.mean(gained * value, axis=-1, keepdims=True)
+    return scale * gained - value * (scale * scale * scale * inner)
+
+
+ROOT = 0.7978845608028654
+
+
+def gelu_parts(v):
+    t = jnp.tanh(ROOT * (v + 0.044715 * (v * v * v)))
+    value = 0.5 * v * (1.0 + t)
+    slope = 0.5 * (1.0 + t) + 0.5 * v * (1.0 - t * t) * (ROOT * (1.0 + 0.134145 * (v * v)))
+    return value, slope
+
+
+def add_low(left, right):
+    return (left.astype(F32) + right.astype(F32)).astype(BF)
+
+
+def layer_kernel(
+    tok,
+    cot,
+    seg,
+    gpad,
+    wq,
+    wo,
+    wgu_in,
+    wd_in,
+    output,
+    input_grad,
+    rq,
+    ro,
+    rg,
+    rgu,
+    rd,
+    qkv_w,
+    out_w,
+    gains,
+    wgu,
+    wd,
+    stage,
+    acts,
+    downs,
+    gate,
+    up,
+    mixed,
+    sums,
+    one,
+    two,
+    three,
+    pairs,
+    query,
+    proj,
+    probs,
+    attended,
+    xn,
+    turn,
+    dscores,
+    dpairs,
+    kv_in,
+    kv_sum,
+    kv_far,
+    pool,
+    q_two,
+    o_two,
+    q_far,
+    o_far,
+    g_in,
+    g_sum,
+    gu_in,
+    gu_far,
+    d_in,
+    d_far,
+    send,
+    recv,
+    local,
+):
+    dp, ctx, x = place()
+    rows, width = tok.shape
+    layers = pairs.shape[0]
+    length = seg.shape[0] * seg.shape[1]
+    tiles = rows // TILE
+    hq, ho = qkv_w.shape[4], out_w.shape[4]
+    tq, to = hq // TILE, ho // TILE
+    half = wd_in.shape[0]
+    units = 2 * half
+    thalf = half // TILE
+    wide = wd.shape[0] * TILE
+    query_width = H * HD
+    scale = HD ** (-0.5)
+    z, y = ctx // 2, ctx % 2
+    cube_of = ctx // 4
+    links = Links(send, recv)
+    cube = Cube(links, tiles)
+    sibling = (1 - dp, ctx, x)
+    beside = (dp, z * 2 + 1 - y, x)
+    across = (dp, lax.rem(ctx + 4, 8), x)
+    others = [(dp, lax.rem(z + step, layers) * 2 + y, x) for step in range(1, layers)]
+    y2, x2 = jnp.where(dp == 0, 1 - y, y), jnp.where(dp == 0, x, 1 - x)
+    y3, x3 = jnp.where(dp == 0, y, 1 - y), jnp.where(dp == 0, 1 - x, x)
+    mine2, mine3 = jnp.where(dp == 0, y, x), jnp.where(dp == 0, x, y)
+    second = (dp, z * 2 + y2, x2)
+    third = (dp, z * 2 + y3, x3)
+    group = (ctx % 4) * 2 + x
+    user = (x, ctx // 2 + 4 * dp, ctx % 2)
+    owner = (cube_of, group, dp)
+    stays_in = (dp == x) & (ctx == ctx // 2 + 4 * dp) & (x == ctx % 2)
+    stays_back = (dp == cube_of) & (ctx == group)  & (x == dp)
+
+    def bring(source, first, index):
+        copy = pltpu.make_async_copy(
+            source, stage.at[pl.ds(first, source.shape[0])], local.at[index]
+        )
+        copy.start()
+        return copy
+
+    bring_q = bring(wq, 0, 0)
+    bring_o = bring(wo, 2 * hq, 1)
+    bring_gu = bring(wgu_in.at[pl.ds(dp * half, half)], 2 * hq + 2 * ho, 2)
+
+    pairs[...] = jnp.zeros(pairs.shape, BF)
+    barrier = pltpu.get_barrier_semaphore()
+    for device in others + [second, third, sibling, cube.peers[2]]:
+        pl.semaphore_signal(barrier, inc=1, device_id=device, device_id_type=MESH)
+
+    @pl.when(jnp.logical_not(stays_in))
+    def _():
+        for device in (user, owner):
+            pl.semaphore_signal(barrier, inc=1, device_id=device, device_id_type=MESH)
+
+    gains[z, y, x, dp] = gpad[dp]
+    bring_q.wait()
+    qkv_w[z, y, x, dp] = stage[pl.ds(dp * hq, hq), :].astype(BF)
+    pl.semaphore_wait(barrier, jnp.where(stays_in, layers + 3, layers + 5))
+    fulls = (gains, qkv_w, out_w)
+
+    def first_steps(full):
+        part = full.at[z, y, x, dp]
+        return [links.go(part, part, device) for device in others]
+
+    def pass_on(zz, yy, xx, *devices):
+        part = qkv_w.at[zz, yy, xx, dp]
+        return [links.go(part, part, device) for device in devices]
+
+    firsts = [first_steps(gains), first_steps(qkv_w)]
+    passed = [pass_on(z, y, x, second, third, sibling)]
+    bring_o.wait()
+    out_w[z, y, x, dp] = stage[pl.ds(2 * hq + dp * ho, ho), :].astype(BF)
+    bring_gu.wait()
+    low = 2 * hq + 2 * ho
+    wgu[cube_of, pl.ds(dp * half, half), :] = stage[low : low + half, :].astype(BF)
+    bring_d = bring(wd_in, 0, 3)
+
+    row_id = lax.broadcasted_iota(jnp.int32, (rows, rows), 0)
+    lane_id = lax.broadcasted_iota(jnp.int32, (rows, rows), 1)
+    own_ids = seg[pl.ds(ctx, 1), :]
+    ids = jnp.sum(jnp.where(row_id == lane_id, own_ids, 0), axis=1, keepdims=True)
+    start = jnp.zeros((rows, 1), jnp.int32)
+    for b in range(length // rows):
+        start = start + jnp.sum((seg[b : b + 1, :] < ids).astype(jnp.int32), axis=1, keepdims=True)
+    position = ctx * rows + lax.broadcasted_iota(jnp.int32, (rows, 1), 0)
+    offset = (position - start).astype(F32)
+    lane = lax.broadcasted_iota(jnp.int32, (1, HD // 2), 1).astype(F32)
+    angle = offset * jnp.exp(lane * (-2.0 * 13.815510557964274 / HD))
+    turn[0] = jnp.cos(angle)
+    turn[1] = jnp.sin(angle)
+
+    bring_d.wait()
+    d_in[...] = tiled(stage[0:half, :].astype(BF))
+    bring_rest = bring(wgu_in.at[pl.ds((1 - dp) * half, half)], 0, 4)
+    bring_rest.wait()
+    wgu[cube_of, pl.ds((1 - dp) * half, half), :] = stage[0:half, :].astype(BF)
+    wgu[:, units:, :] = jnp.zeros((2, wide - units, width), BF)
+    wd[2 * thalf :] = jnp.zeros((wide // TILE - 2 * thalf, TILE, width), BF)
+
+    sib, seconds, thirds = {0: [], 2: []}, {}, {}
+
+    def second_steps(t):
+        for copy in firsts[t]:
+            copy.wait_recv()
+        line = fulls[t].at[:, y, x, dp]
+        seconds[t] = links.go(line, line, second)
+        thirds[t] = [links.go(line, line, third)]
+        sib[t].append(links.go(line, line, sibling))
+
+    def third_steps(t):
+        seconds[t].wait_recv()
+        line = fulls[t].at[:, y2, x2, dp]
+        thirds[t].append(links.go(line, line, third))
+        sib[t].append(links.go(line, line, sibling))
+
+    def last_steps(t):
+        for copy, (yy, xx) in zip(thirds[t], ((y3, x3), (1 - y, 1 - x))):
+            copy.wait_recv()
+            line = fulls[t].at[:, yy, xx, dp]
+            sib[t].append(links.go(line, line, sibling))
+
+    second_steps(0)
+    behind = [lax.rem(z + layers - 1 - i, layers) for i in range(layers - 1)]
+    for i, copy in enumerate(firsts[1]):
+        copy.wait_recv()
+        passed.append(pass_on(behind[i], y, x, second, third, sibling))
+    half_rows = wgu.at[cube_of, pl.ds(dp * half, half)]
+    gu_cross = links.go(half_rows, half_rows, across)
+    firsts.append(first_steps(out_w))
+    third_steps(0)
+    line_order = [z] + behind
+    far = []
+    for i, zz in enumerate(line_order):
+        passed[i][0].wait_recv()
+        far.append(pass_on(zz, y2, x2, third, sibling))
+    last_steps(0)
+    ends_q = []
+    for i, zz in enumerate(line_order):
+        passed[i][1].wait_recv()
+        ends_q += pass_on(zz, y3, x3, sibling)
+        far[i][0].wait_recv()
+        ends_q += pass_on(zz, 1 - y, 1 - x, sibling)
+    second_steps(2)
+    ends_q += [copies[2] for copies in passed] + [copies[1] for copies in far]
+    for copy in ends_q + sib[0]:
+        copy.wait_recv()
+
+    total = jnp.zeros(gains.shape[-2:], F32)
+    for h in range(2):
+        part = jnp.zeros(gains.shape[-2:], F32)
+        for zz in range(layers):
+            for yy in range(2):
+                for xx in range(2):
+                    part = part + gains[zz, yy, xx, h]
+        g_in[0, h * part.shape[0] : (h + 1) * part.shape[0], :] = part
+
+    def gain_row(first, size):
+        lo = first // 128
+        return 1.0 + jnp.concatenate(
+            [g_in[0, lo + i : lo + i + 1, :] for i in range(size // 128)], axis=1
+        )
+
+    gain_in = gain_row(0, width)
+    gain_query = gain_row(4 * width, HD)
+    gain_key = gain_row(4 * width + HD, HD)
+
+    value = tok[...].astype(F32)
+    xn[...] = (value * norm_scale(value) * gain_in).astype(BF)
+    proj[...] = contract_last(xn[...], flat(qkv_w[...]))
+
+    def turned(part, gain):
+        part = part * norm_scale(part) * gain
+        first, last = part[:, : HD // 2], part[:, HD // 2 :]
+        cosine, sine = turn[0], turn[1]
+        return jnp.concatenate(
+            [first * cosine - last * sine, last * cosine + first * sine], axis=1
+        )
+
+    pairs[z, y, :, :HD] = turned(proj[:, query_width : query_width + HD], gain_key).astype(BF)
+    pairs[z, y, :, HD:] = proj[:, query_width + HD :].astype(BF)
+    own_pairs = pairs.at[z, y]
+    upper = (dp, lax.rem(z + 1, layers) * 2 + y, x)
+    rises = z < layers - 1
+    pair_up = [links.go_if(rises, own_pairs, own_pairs, upper)]
+    pair_side = [links.go(own_pairs, own_pairs, beside)]
+    for h in range(H):
+        query[h * rows : (h + 1) * rows, :] = turned(
+            proj[:, h * HD : (h + 1) * HD], gain_query
+        ).astype(BF)
+    third_steps(2)
+    for k in range(1, layers):
+        below = z >= k
+        part = pairs.at[lax.rem(z + layers - k, layers), y]
+        pl.when(below)(pair_up[k - 1].wait_recv)
+        if k < layers - 1:
+            pair_up.append(links.go_if(below & rises, part, part, upper))
+        pair_side.append(links.go_if(below, part, part, beside))
+    own_down = wd.at[pl.ds(x * thalf, thalf)]
+    down_local = pltpu.make_async_copy(d_in, own_down, local.at[5])
+    down_move = links.make(d_in, own_down, user)
+
+    @pl.when(stays_in)
+    def _():
+        down_local.start()
+
+    @pl.when(jnp.logical_not(stays_in))
+    def _():
+        down_move.start()
+
+    last_steps(2)
+    pair_side[0].wait_recv()
+    for k in range(1, layers):
+        pl.when(z >= k)(pair_side[k].wait_recv)
+
+    def allowed(b):
+        key_pos = b * rows + lax.broadcasted_iota(jnp.int32, (1, rows), 1)
+        return (key_pos <= position) & (seg[b : b + 1, :] == ids)
+
+    keep = jnp.concatenate([allowed(b) for b in range(length // rows)], axis=1)
+    keys = flat(pairs[:, :, :, :HD])
+    values = flat(pairs[:, :, :, HD:])
+    for h in range(H):
+        part = slice(h * rows, (h + 1) * rows)
+        scores = jnp.where(keep, contract_last(query[part, :], keys) * scale, -1e30)
+        largest = jnp.max(scores, axis=-1, keepdims=True)
+        raised = jnp.exp(scores - largest)
+        p = raised / jnp.sum(raised, axis=-1, keepdims=True)
+        probs[part, :] = p
+        attended[:, h * HD : (h + 1) * HD] = jnp.dot(
+            p.astype(BF), values, preferred_element_type=F32
+        ).astype(BF)
+    for copy in sib[2]:
+        copy.wait_recv()
+    branch = stage.at[0:rows]
+    hidden = stage.at[rows : 2 * rows]
+    grad_hidden = stage.at[2 * rows : 3 * rows]
+    branch[...] = jnp.dot(attended[...], flat(out_w[...]), preferred_element_type=F32)
+    gain_attend = gain_row(width, width)
+    value = branch[...]
+    hidden[...] = tok[...].astype(F32) + value * norm_scale(value) * gain_attend
+    value = hidden[...]
+    gain_pre = gain_row(2 * width, width)
+    gain_post = gain_row(3 * width, width)
+
+    def block_of(buf, j):
+        return flat(buf[pl.ds(j * tiles, tiles)])
+
+    def put_block(buf, j, block):
+        buf[pl.ds(j * tiles, tiles)] = tiled(block)
+
+    me = cube.me
+    put_block(acts, me, (value * norm_scale(value) * gain_pre).astype(BF))
+    cube.gather(acts)
+    gu_cross.wait_recv()
+    landed = wgu.at[1 - cube_of, pl.ds(dp * half, half)]
+    links.go(landed, landed, sibling).wait_recv()
+
+    def forward(j, carry):
+        a = block_of(acts, j)
+        g = contract_last(a, wgu[0])
+        u = contract_last(a, wgu[1])
+        gate[j] = g
+        up[j] = u
+        mixed[j] = (gelu_parts(g)[0] * u).astype(BF)
+        return carry
+
+    lax.fori_loop(0, 8, forward, 0)
+
+    @pl.when(stays_in)
+    def _():
+        down_local.wait()
+
+    @pl.when(jnp.logical_not(stays_in))
+    def _():
+        down_move.wait_send()
+
+    @pl.when(jnp.logical_not(stays_in))
+    def _():
+        down_move.wait_recv()
+
+    landed = wd.at[pl.ds(dp * thalf, thalf)]
+    links.go(landed, landed, sibling).wait_recv()
+
+    def project(j, carry):
+        put_block(sums, j, jnp.dot(mixed[j], flat(wd[...]), preferred_element_type=F32).astype(BF))
+        return carry
+
+    lax.fori_loop(0, 8, project, 0)
+    links.drain()
+    cube.scatter(sums, one, two, three)
+    links.drain()
+    down = block_of(sums, me).astype(F32) + flat(three[...]).astype(F32)
+    down_scale = norm_scale(down)
+    normal = down * down_scale
+    output[...] = (hidden[...] + normal * gain_post).astype(BF)
+    dy = cot[...].astype(F32)
+    put_block(downs, me, norm_back(down, down_scale, dy * gain_post).astype(BF))
+
+    def put_gain(first, row):
+        lo = first // 128
+        for i in range(row.shape[1] // 128):
+            g_sum[0, lo + i : lo + i + 1, :] = row[:, i * 128 : (i + 1) * 128]
+
+    g_sum[0] = jnp.zeros(g_sum.shape[1:], F32)
+    put_gain(3 * width, jnp.sum(dy * normal, axis=0, keepdims=True))
+    cube.gather(downs)
+
+    def put_rows(first, limit, block):
+        kept = min(block.shape[0], limit)
+        pool[first // TILE : (first + kept) // TILE] = tiled(block[:kept].astype(BF))
+
+    downs_all = flat(downs[...])
+    acts_all = flat(acts[...])
+    tokens = 8 * rows
+    for lo in range(0, wide, 128):
+        cut = slice(lo, lo + 128)
+        mx = mixed[:, :, cut].reshape(tokens, 128)
+        put_rows(2 * units + lo, units - lo, contract_first(mx, downs_all))
+
+    def slab(first, size):
+        return pool.at[pl.ds(first, size)]
+
+    d_swap = links.go(slab(4 * thalf + (1 - dp) * thalf, thalf), d_in, sibling)
+
+    def backward(j, carry):
+        d = contract_last(block_of(downs, j), flat(wd[...]))
+        value, slope = gelu_parts(gate[j])
+        dg = (d * up[j] * slope).astype(BF)
+        du = (d * value).astype(BF)
+        gate[j] = dg.astype(F32)
+        up[j] = du.astype(F32)
+        put_block(
+            sums,
+            j,
+            (
+                jnp.dot(dg, wgu[0], preferred_element_type=F32)
+                + jnp.dot(du, wgu[1], preferred_element_type=F32)
+            ).astype(BF),
+        )
+        return carry
+
+    links.drain()
+    lax.fori_loop(0, 8, backward, 0)
+    moved = {}
+
+    def weights():
+        d_swap.wait_recv()
+        d_in[...] = add_low(d_in[...], pool[pl.ds(4 * thalf + dp * thalf, thalf)])
+        moved["local"] = pltpu.make_async_copy(d_in, d_far.at[cube_of], local.at[6])
+        moved["down"] = links.make(d_in, d_far.at[cube_of], owner)
+
+        @pl.when(stays_back)
+        def _():
+            moved["local"].start()
+
+        @pl.when(jnp.logical_not(stays_back))
+        def _():
+            moved["down"].start()
+
+        for lo in range(0, wide, 128):
+            cut = slice(lo, lo + 128)
+            for i, buf in enumerate((gate, up)):
+                grad = buf[:, :, cut].reshape(tokens, 128).astype(BF)
+                put_rows(i * units + lo, units - lo, contract_first(grad, acts_all))
+        swap = [
+            links.go(slab(i * 2 * thalf + (1 - dp) * thalf, thalf), gu_in.at[i], sibling)
+            for i in range(2)
+        ]
+        for i in range(2):
+            swap[i].wait_recv()
+            gu_in[i] = add_low(gu_in[i], pool[pl.ds(i * 2 * thalf + dp * thalf, thalf)])
+        moved["gu"] = links.go(gu_in.at[1 - cube_of], gu_far, across)
+
+    cube.scatter(sums, one, two, three, weights)
+    value = hidden[...]
+    hidden_scale = norm_scale(value)
+    total = block_of(sums, me).astype(F32) + flat(three[...]).astype(F32)
+    put_gain(2 * width, jnp.sum(total * (value * hidden_scale), axis=0, keepdims=True))
+    grad = cot[...].astype(F32) + norm_back(value, hidden_scale, total * gain_pre)
+    grad_hidden[...] = grad
+    value = branch[...]
+    branch_scale = norm_scale(value)
+    put_gain(width, jnp.sum(grad * (value * branch_scale), axis=0, keepdims=True))
+    grad_branch = norm_back(value, branch_scale, grad * gain_attend).astype(BF)
+    links.drain()
+
+    def spot(h, zz, yy, xx):
+        a, b = (yy, xx) if h == 0 else (xx, yy)
+        return (b * 2 + a) * layers + zz
+
+    def put_parts(base, count, block):
+        for zz in range(layers):
+            for yy in range(2):
+                for xx in range(2):
+                    for h in range(2):
+                        first = (((zz * 2 + yy) * 2 + xx) * 2 + h) * count * TILE
+                        at = base + (h * 4 * layers + spot(h, zz, yy, xx)) * count
+                        pool[at : at + count] = tiled(
+                            block[first : first + count * TILE].astype(BF)
+                        )
+
+    base_out = 8 * layers * tq
+    q_in = downs.at[pl.ds(0, 4 * layers * tq)]
+    o_in = acts.at[pl.ds(0, 4 * layers * to)]
+    q_one = acts.at[pl.ds(4 * layers * to, 2 * layers * tq)]
+    o_one = downs.at[pl.ds(4 * layers * tq, 2 * layers * to)]
+    put_parts(base_out, to, contract_first(attended[...], grad_branch))
+    per_out = 4 * layers * to
+    per_qkv = 4 * layers * tq
+    o_swap = links.go(slab(base_out + (1 - dp) * per_out, per_out), o_in, sibling)
+    grad_att = contract_last(grad_branch, flat(out_w[...])).astype(BF)
+    for h in range(H):
+        part = slice(h * rows, (h + 1) * rows)
+        p = probs[part, :]
+        grad_p = contract_last(grad_att[:, h * HD : (h + 1) * HD], values)
+        row = jnp.sum(p * grad_p, axis=-1, keepdims=True)
+        dscores[part, :] = (p * (grad_p - row)).astype(BF)
+    grad_heads = jnp.concatenate([grad_att[:, h * HD : (h + 1) * HD] for h in range(H)], axis=0)
+    grad_keys = contract_first(dscores[...], query[...]) * scale
+    dpairs[:, :, :, :HD] = grad_keys.astype(BF).reshape(layers, 2, rows, HD)
+    grad_values = contract_first(probs[...].astype(BF), grad_heads)
+    dpairs[:, :, :, HD:] = grad_values.astype(BF).reshape(layers, 2, rows, HD)
+    kv_line = links.go(dpairs.at[:, 1 - y], kv_in, beside)
+
+    def turned_back(part, gain, grad):
+        cosine, sine = turn[0], turn[1]
+        first, last = grad[:, : HD // 2], grad[:, HD // 2 :]
+        grad = jnp.concatenate(
+            [first * cosine + last * sine, last * cosine - first * sine], axis=1
+        )
+        part_scale = norm_scale(part)
+        gain_term = jnp.sum(grad * (part * part_scale), axis=0, keepdims=True)
+        return norm_back(part, part_scale, grad * gain), gain_term
+
+    o_swap.wait_recv()
+    mine_out = pl.ds(base_out + dp * per_out, per_out)
+    pool[mine_out] = add_low(pool[mine_out], o_in[...])
+    o_third = links.go(
+        slab(base_out + dp * per_out + (1 - mine3) * per_out // 2, per_out // 2), o_one, third
+    )
+    query_term = jnp.zeros((1, HD), F32)
+    grads = []
+    for h in range(H):
+        part = slice(h * rows, (h + 1) * rows)
+        grad_query = jnp.dot(dscores[part, :], keys, preferred_element_type=F32) * scale
+        grad, term = turned_back(proj[:, h * HD : (h + 1) * HD], gain_query, grad_query)
+        grads.append(grad.astype(BF))
+        query_term = query_term + term
+    put_gain(4 * width, query_term)
+    kv_line.wait_recv()
+    for i in range(layers):
+        kv_sum[i] = add_low(kv_in[i], dpairs[i, y])
+    kv_copies = []
+    for i, device in enumerate(others):
+        to_layer = lax.rem(z + i + 1, layers)
+        kv_copies.append(
+            links.go_if(to_layer < z, kv_sum.at[to_layer], kv_far.at[i], device)
+        )
+    o_third.wait_recv()
+    quarter_out = per_out // 4
+    at_out = base_out + dp * per_out + mine3 * (per_out // 2)
+    near = pl.ds(at_out, per_out // 2)
+    pool[near] = add_low(pool[near], o_one[...])
+    o_second = links.go(slab(at_out + (1 - mine2) * quarter_out, quarter_out), o_two, second)
+    kv_total = stage.at[3 * rows : 4 * rows, 0 : 2 * HD]
+    kv_total[...] = kv_sum[z].astype(F32)
+    for i, copy in enumerate(kv_copies):
+
+        @pl.when(behind[i] > z)
+        def _():
+            copy.wait_recv()
+            kv_total[...] += kv_far[i].astype(F32)
+
+    grad_pair = kv_total[...]
+    grad, term = turned_back(
+        proj[:, query_width : query_width + HD], gain_key, grad_pair[:, :HD]
+    )
+    put_gain(4 * width + HD, term)
+    grads += [grad.astype(BF), grad_pair[:, HD:].astype(BF)]
+    grad_proj = jnp.concatenate(grads, axis=1)
+    put_parts(0, tq, contract_first(grad_proj, xn[...]))
+    q_swap = links.go(slab((1 - dp) * per_qkv, per_qkv), q_in, sibling)
+    grad_normed = jnp.dot(grad_proj, flat(qkv_w[...]), preferred_element_type=F32)
+    value = tok[...].astype(F32)
+    in_scale = norm_scale(value)
+    put_gain(0, jnp.sum(grad_normed * (value * in_scale), axis=0, keepdims=True))
+    g_swap = links.go(g_sum.at[0], g_in.at[1], sibling)
+    input_grad[...] = grad_hidden[...] + norm_back(value, in_scale, grad_normed * gain_in)
+    o_second.wait_recv()
+    at_out = at_out + mine2 * quarter_out
+    near = pl.ds(at_out, quarter_out)
+    pool[near] = add_low(pool[near], o_two[...])
+    o_fars = [
+        links.go(slab(at_out + lax.rem(z + i + 1, layers) * to, to), o_far.at[i], device)
+        for i, device in enumerate(others)
+    ]
+    g_swap.wait_recv()
+    g_sum[1] = g_sum[0] + g_in[1]
+    g_x = links.go(g_sum.at[1], g_in.at[2], cube.peers[0])
+    q_swap.wait_recv()
+    mine_qkv = pl.ds(dp * per_qkv, per_qkv)
+    pool[mine_qkv] = add_low(pool[mine_qkv], q_in[...])
+    q_third = links.go(slab(dp * per_qkv + (1 - mine3) * per_qkv // 2, per_qkv // 2), q_one, third)
+    g_x.wait_recv()
+    g_sum[2] = g_sum[1] + g_in[2]
+    g_y = links.go(g_sum.at[2], g_in.at[3], beside)
+    q_third.wait_recv()
+    quarter_qkv = per_qkv // 4
+    at_qkv = dp * per_qkv + mine3 * (per_qkv // 2)
+    near = pl.ds(at_qkv, per_qkv // 2)
+    pool[near] = add_low(pool[near], q_one[...])
+    q_second = links.go(slab(at_qkv + (1 - mine2) * quarter_qkv, quarter_qkv), q_two, second)
+    g_y.wait_recv()
+    g_sum[3] = g_sum[2] + g_in[3]
+    g_in[4 + z] = g_sum[3]
+    g_z = [links.go(g_sum.at[3], g_in.at[4 + z], device) for device in others]
+    q_second.wait_recv()
+    at_qkv = at_qkv + mine2 * quarter_qkv
+    near = pl.ds(at_qkv, quarter_qkv)
+    pool[near] = add_low(pool[near], q_two[...])
+    q_fars = [
+        links.go(slab(at_qkv + lax.rem(z + i + 1, layers) * tq, tq), q_far.at[i], device)
+        for i, device in enumerate(others)
+    ]
+    ends = []
+
+    def finish(fars, far, at, count, result):
+        value = pool[pl.ds(at + z * count, count)].astype(F32)
+        for i, copy in enumerate(fars):
+            copy.wait_recv()
+            value = value + far[i].astype(F32)
+        result[dp] = value.astype(BF)
+        ends.append(links.go(result.at[dp], result.at[dp], sibling))
+
+    finish(o_fars, o_far, at_out, to, ro)
+    for copy in g_z:
+        copy.wait_recv()
+    value = g_in[4]
+    for i in range(1, layers):
+        value = value + g_in[4 + i]
+    rg[...] = value
+
+    @pl.when(stays_back)
+    def _():
+        moved["local"].wait()
+
+    @pl.when(jnp.logical_not(stays_back))
+    def _():
+        moved["down"].wait_send()
+
+    @pl.when(jnp.logical_not(stays_back))
+    def _():
+        moved["down"].wait_recv()
+
+    landed = d_far.at[dp]
+    d_end = links.go(landed, landed, sibling)
+    finish(q_fars, q_far, at_qkv, tq, rq)
+    d_end.wait_recv()
+    d_in[...] = add_low(d_far[0], d_far[1])
+    keep_d = pltpu.make_async_copy(d_in, rd, local.at[7])
+    keep_d.start()
+    moved["gu"].wait_recv()
+    gu_far[...] = add_low(gu_in[cube_of], gu_far[...])
+    keep_gu = pltpu.make_async_copy(gu_far, rgu.at[dp], local.at[8])
+    keep_gu.start()
+    ends.append(links.go(gu_far, rgu.at[dp], sibling))
+    for copy in ends:
+        copy.wait_recv()
+    keep_d.wait()
+    keep_gu.wait()
+    links.drain()
+
+
+def whole_layer(tok, cot, seg, gpad, wq, wo, wgu, wd, layers):
+    rows, width = tok.shape
+    units = 2 * wd.shape[0]
+    wide = -(-units // 128) * 128
+    hq, ho, half = wq.shape[0] // 2, wo.shape[0] // 2, wd.shape[0]
+    tq, to, thalf, tiles = hq // TILE, ho // TILE, half // TILE, rows // TILE
+    gain_rows = gpad.shape[0] * gpad.shape[1]
+    length = seg.shape[0] * seg.shape[1]
+    pool = max(6 * thalf, 8 * layers * (tq + to))
+
+    def low(*shape):
+        return pltpu.VMEM(shape, BF)
+
+    def full(*shape):
+        return pltpu.VMEM(shape, F32)
+
+    def tile(*lead):
+        return pltpu.VMEM(lead + (TILE, width), BF)
+
+    return pl.pallas_call(
+        layer_kernel,
+        out_shape=(
+            jax.ShapeDtypeStruct((rows, width), BF),
+            jax.ShapeDtypeStruct((rows, width), F32),
+            jax.ShapeDtypeStruct((2, tq, TILE, width), BF),
+            jax.ShapeDtypeStruct((2, to, TILE, width), BF),
+            jax.ShapeDtypeStruct((gain_rows, 128), F32),
+            jax.ShapeDtypeStruct((2, thalf, TILE, width), BF),
+            jax.ShapeDtypeStruct((thalf, TILE, width), BF),
+        ),
+        in_specs=[VMEM] * 4 + [ANY] * 4,
+        out_specs=(VMEM,) * 5 + (ANY, ANY),
+        scratch_shapes=[
+            low(layers, 2, 2, 2, hq, width),
+            low(layers, 2, 2, 2, ho, width),
+            full(layers, 2, 2, 2, gain_rows // 2, 128),
+            low(2, wide, width),
+            tile(wide // TILE),
+            full(2 * hq + 2 * ho + half, width),
+            tile(8 * tiles),
+            tile(8 * tiles),
+            full(8, rows, wide),
+            full(8, rows, wide),
+            low(8, rows, wide),
+            tile(8 * tiles),
+            tile(4, tiles),
+            tile(2, tiles),
+            tile(tiles),
+            low(layers, 2, rows, 2 * HD),
+            low(H * rows, HD),
+            full(rows, (H + 2) * HD),
+            full(H * rows, length),
+            low(rows, H * HD),
+            low(rows, width),
+            full(2, rows, HD // 2),
+            low(H * rows, length),
+            low(layers, 2, rows, 2 * HD),
+            low(layers, rows, 2 * HD),
+            low(layers, rows, 2 * HD),
+            low(layers - 1, rows, 2 * HD),
+            tile(pool),
+            tile(layers * tq),
+            tile(layers * to),
+            tile(layers - 1, tq),
+            tile(layers - 1, to),
+            full(4 + layers, gain_rows, 128),
+            full(4, gain_rows, 128),
+            tile(2, thalf),
+            tile(thalf),
+            tile(thalf),
+            tile(2, thalf),
+            pltpu.SemaphoreType.DMA((220,)),
+            pltpu.SemaphoreType.DMA((220,)),
+            pltpu.SemaphoreType.DMA((9,)),
+        ],
+        compiler_params=pltpu.CompilerParams(
+            collective_id=0, has_side_effects=True, vmem_limit_bytes=62 * 2**20
+        ),
+    )(tok, cot, seg, gpad, wq, wo, wgu, wd)
+
+
+def moves_tokens(mesh):
+    return mesh.shape["ctx"] == 8 and mesh.shape["fsdp"] == 2 and mesh.shape["dp"] == 2
+
+
+def move_tokens_body(
+    tokens,
+    cotangent,
+    segments,
+    qkv_weight,
+    out_weight,
+    gate_up_weight,
+    down_weight,
+    gains,
+    qkv_first,
+    out_first,
+    gate_up_first,
+    down_first,
+    gains_first,
+    qkv_second,
+    out_second,
+    gate_up_second,
+    down_second,
+    gains_second,
+):
+    rows = tokens.shape[1]
+    width = tokens.shape[2]
+    layers = lax.axis_size("ctx") // 2
+    chip = lax.axis_index("ctx") * 2 + lax.axis_index("fsdp")
+    own_gains = gains.shape[0]
+    gain_rows = -(-own_gains * 4 * layers // 1024) * 8 + 8
+    gain_part = lax.dynamic_update_slice_in_dim(
+        jnp.zeros((gain_rows * 128,), F32),
+        gains.astype(BF).astype(F32),
+        chip * own_gains,
+        0,
+    )
+    output, input_grad, qkv_low, out_low, gains_sum, gate_up_low, down_low = whole_layer(
+        tokens[0],
+        cotangent[0],
+        segments.reshape(-1, rows),
+        gain_part.reshape(2, gain_rows // 2, 128),
+        qkv_weight,
+        out_weight,
+        gate_up_weight,
+        down_weight,
+        layers,
+    )
+    qkv_total = qkv_low.reshape(-1, width).astype(F32)
+    out_total = out_low.reshape(-1, width).astype(F32)
+    gate_up_total = gate_up_low.reshape(-1, width).astype(F32)
+    down_total = down_low.reshape(-1, width).astype(F32)
+    gains_total = lax.dynamic_slice_in_dim(gains_sum.reshape(-1), chip * own_gains, own_gains, 0)
+    qkv_new, qkv_first_new, qkv_second_new = adamw(qkv_weight, qkv_total, qkv_first, qkv_second)
+    out_new, out_first_new, out_second_new = adamw(out_weight, out_total, out_first, out_second)
+    gate_up_new, gate_up_first_new, gate_up_second_new = adamw(
+        gate_up_weight, gate_up_total, gate_up_first, gate_up_second
+    )
+    down_new, down_first_new, down_second_new = adamw(
+        down_weight, down_total, down_first, down_second
+    )
+    gains_new, gains_first_new, gains_second_new = adamw(
+        gains, gains_total, gains_first, gains_second
+    )
+    return (
+        output[None],
+        input_grad[None],
+        qkv_total,
+        out_total,
+        gate_up_total,
+        down_total,
+        gains_total,
+        qkv_new,
+        out_new,
+        gate_up_new,
+        down_new,
+        gains_new,
+        qkv_first_new,
+        out_first_new,
+        gate_up_first_new,
+        down_first_new,
+        gains_first_new,
+        qkv_second_new,
+        out_second_new,
+        gate_up_second_new,
+        down_second_new,
+        gains_second_new,
+    )
+
+
 def solution(mesh):
     in_specs = (
         P(("dp", "fsdp"), "ctx", None),
@@ -329,4 +1302,5 @@
         P(("ctx", "fsdp"), None),
         P(("ctx", "fsdp")),
     )
+    body = move_tokens_body if moves_tokens(mesh) else gather_weights_body
     return jax.shard_map(body, mesh=mesh, in_specs=in_specs, out_specs=out_specs, check_vma=False)

time: 2690 us -> 367 us (0.14)
  waiting for transfers between devices: 2250 us -> 0 us
  Pallas kernels: 0 us -> 343 us
  blocking collectives: 222 us -> 0 us
  matrix products: 120 us -> 0 us
  other arithmetic: 60.8 us -> 19.8 us
    reduce_scatter x6 -> x0, waiting for transfers between devices: 1770 us -> none  [the longest x1 920 us: body(): lax.psum_scatter(gate_up_grad, ('ctx', 'fsdp'), scatter_dimension=0, tile...]
    all_gather x4 -> x0, waiting for transfers between devices: 481 us -> none  [the longest x1 318 us: body(): lax.all_gather(gate_up_weight.astype(jnp.bfloat16), ('ctx', 'fsdp'), axis...]
    pallas_call x0 -> x1, Pallas kernels: none -> 343 us  [whole_layer(): pl.pallas_call(layer_kernel, out_shape=(jax.ShapeDtypeStruct((rows, width...]
    unnamed x2 -> x0, blocking collectives: 155 us -> none
    dot_general x18 -> x0, matrix products: 120 us -> none  [the longest x4 46.8 us: contract_first(): lax.dot_general(left, right, (((0,), (0,)), ((), ())), preferred_element_...]
    all_gather x2 -> x0, blocking collectives: 64.2 us -> none  [the longest x1 32.1 us: body(): lax.all_gather(value_low, 'ctx', axis=0, tiled=True)]
  transfers between devices with their start and end apart: 11 -> 0, of which waited for: 8 -> 0; matrix products, arithmetic and copies ran while one was open for 5% -> 0% of each run, Pallas kernels for 0% -> 0%
where the time goes in v2:
time: 367 us
  Pallas kernels  343 us (93%)
  other arithmetic  19.8 us (5%)
    pallas_call x1, Pallas kernels, whole_layer(): pl.pallas_call(layer_kernel, out_shape=(jax.ShapeDtypeStruct((rows, width...  343 us
    sub x5, other arithmetic, adamw(): weight - 0.03 * (first_hat / (jnp.sqrt(second_hat) + 1e-08) + 0.1 * weight)  19 us

profile of v2, /device:TPU:0, one launch (start us, length us, event | category | flops | bytes accessed | tf_op | source)
XLA Modules:
  0.0 366.7 jit_solution(12623406355694524961)
XLA Ops:
  0.7 0.8 convert_dynamic-update-slice_fusion
  1.5 0.0 copy-start.14
  1.5 0.6 copy-done.14
  2.1 0.0 copy-start.15
  2.1 0.0 copy-start.16
  2.1 0.0 copy-start.17
  2.1 342.9 %shard_map.345 = (bf16[128,1152]{1,0:T(8,128)(2,1)}, f32[128,1152]{1,0:T(8,128)}, bf16[2,3,16,1152]{3,2,1,0:T(8,128)(2,1)}, bf16[2,2,16,1152]{3,2,1,0:T(8,128)(2...) custom-call(bf16[128,1152]{1,0:T(8,128)(2,1)} %bitcast.24, ...), custom_call_target="tpu_custom_call" | custom-call | tf_op jit(solution)/shard_map/pallas_call | solution.py:1109
  345.0 0.0 copy-done.15
  345.0 0.0 copy-done.16
  345.0 0.0 copy-done.17
  345.0 1.4 multiply_subtract_fusion.4
  346.4 11.5 %multiply_subtract_fusion = (f32[864,1152]{1,0:T(8,128)}, f32[864,1152]{1,0:T(8,128)}, f32[864,1152]{1,0:T(8,128)}, f32[864,1152]{1,0:T(8,128)}) fusion(f32[864,1152]{1,0:T(8,128)} %wgu_in.1, f32[864,1152]{1,0:T(8,128)} %param.28, f32[864,1152]{1,0:T(8,128)} %param.33, bf16[2,27,16,1152]{3,2,1,0:T(8,128)(2,1)} %get-tuple-element.33), kind=kLoop, calls=%fused_computation.2 | loop fusion | flops 15925248 | bytes 29859840 | tf_op jit(solution)/shard_map/sub | solution.py:67
  357.9 0.0 copy-done
  357.9 0.0 copy-done.1
  357.9 0.1 copy-done.2
  358.0 0.8 copy-done.5
  358.9 3.7 %multiply_subtract_fusion.1 = (f32[432,1152]{1,0:T(8,128)}, f32[432,1152]{1,0:T(8,128)}, f32[432,1152]{1,0:T(8,128)}, f32[432,1152]{1,0:T(8,128)}) fusion(f32[432,1152]{1,0:T(8,128)S(1)} %copy-done, f32[432,1152]{1,0:T(8,128)S(1)} %copy-done.1, f32[432,1152]{1,0:T(8,128)S(1)} %copy-done.2, bf16[27,16,1152]{2,1,0:T(8,128)(2,1)S(1)} %copy-done.5), kind=kLoop, calls=%fused_computation.7 | loop fusion | flops 7962624 | bytes 14929920 | tf_op jit(solution)/shard_map/sub | solution.py:67
  362.6 0.0 copy-done.3
  362.6 0.0 copy-done.7
  362.6 0.0 copy-done.8
  362.6 0.0 copy-done.12
  362.6 0.0 copy-start.11
  362.6 1.3 multiply_subtract_fusion.2
  364.0 0.0 copy-done.4
  364.0 0.0 copy-done.9
  364.0 0.0 copy-done.10
  364.0 0.1 copy-done.13
  364.0 1.1 multiply_subtract_fusion.3
  365.1 0.0 copy-done.11
  365.1 0.7 copy.43
  365.9 0.0 copy-done.6
  365.9 0.8 copy.44
  (14 shorter events, 0.0 us)
Async XLA Ops:
  1.5 0.6 copy-start.14
  2.1 342.9 %copy-start.15 = (f32[320]{0:T(512)S(1)}, f32[320]{0:T(512)}, u32[]{:S(2)}) copy-start(f32[320]{0:T(512)} %param.25) | copy-start | bytes 3844
  2.1 342.9 %copy-start.16 = (f32[320]{0:T(512)S(1)}, f32[320]{0:T(512)}, u32[]{:S(2)}) copy-start(f32[320]{0:T(512)} %param.30) | copy-start | bytes 3844
  2.1 342.9 %copy-start.17 = (f32[320]{0:T(512)S(1)}, f32[320]{0:T(512)}, u32[]{:S(2)}) copy-start(f32[320]{0:T(512)} %param.35) | copy-start | bytes 3844
  346.4 11.5 %copy-start = (f32[432,1152]{1,0:T(8,128)S(1)}, f32[432,1152]{1,0:T(8,128)}, u32[]{:S(2)}) copy-start(f32[432,1152]{1,0:T(8,128)} %wd_in.1) | copy-start | bytes 5971972
  346.4 11.5 %copy-start.1 = (f32[432,1152]{1,0:T(8,128)S(1)}, f32[432,1152]{1,0:T(8,128)}, u32[]{:S(2)}) copy-start(f32[432,1152]{1,0:T(8,128)} %param.29) | copy-start | bytes 5971972
  346.4 11.7 %copy-start.2 = (f32[432,1152]{1,0:T(8,128)S(1)}, f32[432,1152]{1,0:T(8,128)}, u32[]{:S(2)}) copy-start(f32[432,1152]{1,0:T(8,128)} %param.34) | copy-start | bytes 5971972
  346.4 12.5 %copy-start.5 = (bf16[27,16,1152]{2,1,0:T(8,128)(2,1)S(1)}, bf16[27,16,1152]{2,1,0:T(8,128)(2,1)}, u32[]{:S(2)}) copy-start(bf16[27,16,1152]{2,1,0:T(8,128)(2,1)} %get-tuple-element.34) | copy-start | bytes 2985988
  358.9 3.7 %copy-start.3 = (f32[96,1152]{1,0:T(8,128)S(1)}, f32[96,1152]{1,0:T(8,128)}, u32[]{:S(2)}) copy-start(f32[96,1152]{1,0:T(8,128)} %wq.1) | copy-start | bytes 1327108
  358.9 3.7 %copy-start.7 = (f32[96,1152]{1,0:T(8,128)S(1)}, f32[96,1152]{1,0:T(8,128)}, u32[]{:S(2)}) copy-start(f32[96,1152]{1,0:T(8,128)} %param.26) | copy-start | bytes 1327108
  358.9 3.8 %copy-start.8 = (f32[96,1152]{1,0:T(8,128)S(1)}, f32[96,1152]{1,0:T(8,128)}, u32[]{:S(2)}) copy-start(f32[96,1152]{1,0:T(8,128)} %param.31) | copy-start | bytes 1327108
  358.9 3.8 %copy-start.12 = (bf16[2,3,16,1152]{3,2,1,0:T(8,128)(2,1)S(1)}, bf16[2,3,16,1152]{3,2,1,0:T(8,128)(2,1)}, u32[]{:S(2)}) copy-start(bf16[2,3,16,1152]{3,2,1,0:T(8,128)(2,1)} %get-tuple-element.31) | copy-start | bytes 663556
  362.6 1.4 copy-start.4
  362.6 1.4 copy-start.9
  362.6 1.4 copy-start.10
  362.6 1.5 copy-start.13
  362.6 2.5 copy-start.11
  364.0 1.9 copy-start.6

commit v3 on v2

--- a/solution.py
+++ b/solution.py
@@ -640,8 +640,18 @@
     for i, copy in enumerate(firsts[1]):
         copy.wait_recv()
         passed.append(pass_on(behind[i], y, x, second, third, sibling))
-    half_rows = wgu.at[cube_of, pl.ds(dp * half, half)]
-    gu_cross = links.go(half_rows, half_rows, across)
+    own_down = wd.at[pl.ds(x * thalf, thalf)]
+    down_local = pltpu.make_async_copy(d_in, own_down, local.at[5])
+    down_move = links.make(d_in, own_down, user)
+
+    @pl.when(stays_in)
+    def _():
+        down_local.start()
+
+    @pl.when(jnp.logical_not(stays_in))
+    def _():
+        down_move.start()
+
     firsts.append(first_steps(out_w))
     third_steps(0)
     line_order = [z] + behind
@@ -711,23 +721,13 @@
         if k < layers - 1:
             pair_up.append(links.go_if(below & rises, part, part, upper))
         pair_side.append(links.go_if(below, part, part, beside))
-    own_down = wd.at[pl.ds(x * thalf, thalf)]
-    down_local = pltpu.make_async_copy(d_in, own_down, local.at[5])
-    down_move = links.make(d_in, own_down, user)
-
-    @pl.when(stays_in)
-    def _():
-        down_local.start()
-
-    @pl.when(jnp.logical_not(stays_in))
-    def _():
-        down_move.start()
-
     last_steps(2)
     pair_side[0].wait_recv()
     for k in range(1, layers):
         pl.when(z >= k)(pair_side[k].wait_recv)
 
+    half_rows = wgu.at[cube_of, pl.ds(dp * half, half)]
+    gu_cross = links.go(half_rows, half_rows, across)
     def allowed(b):
         key_pos = b * rows + lax.broadcasted_iota(jnp.int32, (1, rows), 1)
         return (key_pos <= position) & (seg[b : b + 1, :] == ids)

time: 367 us -> 347 us (0.946)
  Pallas kernels: 343 us -> 322 us
    pallas_call x1, Pallas kernels: 343 us -> 322 us  [whole_layer(): pl.pallas_call(layer_kernel, out_shape=(jax.ShapeDtypeStruct((rows, width...]
where the time goes in v3:
time: 347 us; the launch traced here: 346 us
  Pallas kernels  322 us (93%)
  other arithmetic  19.8 us (6%)
    pallas_call x1, Pallas kernels, whole_layer(): pl.pallas_call(layer_kernel, out_shape=(jax.ShapeDtypeStruct((rows, width...  322 us
    sub x5, other arithmetic, adamw(): weight - 0.03 * (first_hat / (jnp.sqrt(second_hat) + 1e-08) + 0.1 * weight)  19 us

profile of v3, /device:TPU:0, one launch (start us, length us, event | category | flops | bytes accessed | tf_op | source)
XLA Modules:
  0.0 346.3 jit_solution(13882092378644397253)
XLA Ops:
  0.7 0.8 convert_dynamic-update-slice_fusion
  1.5 0.0 copy-start.14
  1.5 0.6 copy-done.14
  2.1 0.0 copy-start.15
  2.1 0.0 copy-start.16
  2.1 0.0 copy-start.17
  2.1 322.5 %shard_map.345 = (bf16[128,1152]{1,0:T(8,128)(2,1)}, f32[128,1152]{1,0:T(8,128)}, bf16[2,3,16,1152]{3,2,1,0:T(8,128)(2,1)}, bf16[2,2,16,1152]{3,2,1,0:T(8,128)(2...) custom-call(bf16[128,1152]{1,0:T(8,128)(2,1)} %bitcast.24, ...), custom_call_target="tpu_custom_call" | custom-call | tf_op jit(solution)/shard_map/pallas_call | solution.py:1109
  324.6 0.0 copy-done.15
  324.6 0.0 copy-done.16
  324.6 0.0 copy-done.17
  324.6 1.4 multiply_subtract_fusion.4
  326.0 11.5 %multiply_subtract_fusion = (f32[864,1152]{1,0:T(8,128)}, f32[864,1152]{1,0:T(8,128)}, f32[864,1152]{1,0:T(8,128)}, f32[864,1152]{1,0:T(8,128)}) fusion(f32[864,1152]{1,0:T(8,128)} %wgu_in.1, f32[864,1152]{1,0:T(8,128)} %param.28, f32[864,1152]{1,0:T(8,128)} %param.33, bf16[2,27,16,1152]{3,2,1,0:T(8,128)(2,1)} %get-tuple-element.33), kind=kLoop, calls=%fused_computation.2 | loop fusion | flops 15925248 | bytes 29859840 | tf_op jit(solution)/shard_map/sub | solution.py:67
  337.5 0.0 copy-done
  337.5 0.0 copy-done.1
  337.5 0.1 copy-done.2
  337.7 0.8 copy-done.5
  338.5 3.7 %multiply_subtract_fusion.1 = (f32[432,1152]{1,0:T(8,128)}, f32[432,1152]{1,0:T(8,128)}, f32[432,1152]{1,0:T(8,128)}, f32[432,1152]{1,0:T(8,128)}) fusion(f32[432,1152]{1,0:T(8,128)S(1)} %copy-done, f32[432,1152]{1,0:T(8,128)S(1)} %copy-done.1, f32[432,1152]{1,0:T(8,128)S(1)} %copy-done.2, bf16[27,16,1152]{2,1,0:T(8,128)(2,1)S(1)} %copy-done.5), kind=kLoop, calls=%fused_computation.7 | loop fusion | flops 7962624 | bytes 14929920 | tf_op jit(solution)/shard_map/sub | solution.py:67
  342.2 0.0 copy-done.3
  342.2 0.0 copy-done.7
  342.2 0.0 copy-done.8
  342.2 0.0 copy-done.12
  342.2 0.0 copy-start.11
  342.3 1.3 multiply_subtract_fusion.2
  343.6 0.0 copy-done.4
  343.6 0.0 copy-done.9
  343.6 0.0 copy-done.10
  343.6 0.1 copy-done.13
  343.7 1.1 multiply_subtract_fusion.3
  344.7 0.0 copy-done.11
  344.7 0.7 copy.43
  345.5 0.0 copy-done.6
  345.5 0.8 copy.44
  (14 shorter events, 0.0 us)
Async XLA Ops:
  1.5 0.6 copy-start.14
  2.1 322.5 %copy-start.15 = (f32[320]{0:T(512)S(1)}, f32[320]{0:T(512)}, u32[]{:S(2)}) copy-start(f32[320]{0:T(512)} %param.25) | copy-start | bytes 3844
  2.1 322.5 %copy-start.16 = (f32[320]{0:T(512)S(1)}, f32[320]{0:T(512)}, u32[]{:S(2)}) copy-start(f32[320]{0:T(512)} %param.30) | copy-start | bytes 3844
  2.1 322.5 %copy-start.17 = (f32[320]{0:T(512)S(1)}, f32[320]{0:T(512)}, u32[]{:S(2)}) copy-start(f32[320]{0:T(512)} %param.35) | copy-start | bytes 3844
  326.0 11.5 %copy-start = (f32[432,1152]{1,0:T(8,128)S(1)}, f32[432,1152]{1,0:T(8,128)}, u32[]{:S(2)}) copy-start(f32[432,1152]{1,0:T(8,128)} %wd_in.1) | copy-start | bytes 5971972
  326.0 11.5 %copy-start.1 = (f32[432,1152]{1,0:T(8,128)S(1)}, f32[432,1152]{1,0:T(8,128)}, u32[]{:S(2)}) copy-start(f32[432,1152]{1,0:T(8,128)} %param.29) | copy-start | bytes 5971972
  326.0 11.7 %copy-start.2 = (f32[432,1152]{1,0:T(8,128)S(1)}, f32[432,1152]{1,0:T(8,128)}, u32[]{:S(2)}) copy-start(f32[432,1152]{1,0:T(8,128)} %param.34) | copy-start | bytes 5971972
  326.0 12.5 %copy-start.5 = (bf16[27,16,1152]{2,1,0:T(8,128)(2,1)S(1)}, bf16[27,16,1152]{2,1,0:T(8,128)(2,1)}, u32[]{:S(2)}) copy-start(bf16[27,16,1152]{2,1,0:T(8,128)(2,1)} %get-tuple-element.34) | copy-start | bytes 2985988
  338.5 3.7 %copy-start.3 = (f32[96,1152]{1,0:T(8,128)S(1)}, f32[96,1152]{1,0:T(8,128)}, u32[]{:S(2)}) copy-start(f32[96,1152]{1,0:T(8,128)} %wq.1) | copy-start | bytes 1327108
  338.5 3.7 %copy-start.7 = (f32[96,1152]{1,0:T(8,128)S(1)}, f32[96,1152]{1,0:T(8,128)}, u32[]{:S(2)}) copy-start(f32[96,1152]{1,0:T(8,128)} %param.26) | copy-start | bytes 1327108
  338.5 3.8 %copy-start.8 = (f32[96,1152]{1,0:T(8,128)S(1)}, f32[96,1152]{1,0:T(8,128)}, u32[]{:S(2)}) copy-start(f32[96,1152]{1,0:T(8,128)} %param.31) | copy-start | bytes 1327108
  338.5 3.8 %copy-start.12 = (bf16[2,3,16,1152]{3,2,1,0:T(8,128)(2,1)S(1)}, bf16[2,3,16,1152]{3,2,1,0:T(8,128)(2,1)}, u32[]{:S(2)}) copy-start(bf16[2,3,16,1152]{3,2,1,0:T(8,128)(2,1)} %get-tuple-element.31) | copy-start | bytes 663556
  342.2 1.4 copy-start.4
  342.2 1.4 copy-start.9
  342.2 1.4 copy-start.10
  342.2 1.5 copy-start.13
  342.2 2.5 copy-start.11
  343.6 1.9 copy-start.6

commit v4 on v3

--- a/solution.py
+++ b/solution.py
@@ -481,8 +481,7 @@
     stage,
     acts,
     downs,
-    gate,
-    up,
+    ff,
     mixed,
     sums,
     one,
@@ -767,20 +766,35 @@
     me = cube.me
     put_block(acts, me, (value * norm_scale(value) * gain_pre).astype(BF))
     cube.gather(acts)
+    pair = 2
+
+    def pair_of(buf, j):
+        return flat(buf[pl.ds(j * pair * tiles, pair * tiles)])
+
+    def put_pair(buf, j, block):
+        buf[pl.ds(j * pair * tiles, pair * tiles)] = tiled(block)
+
+    def spread(block):
+        return block.reshape(pair, rows, block.shape[-1])
+
+    def near(j, carry):
+        ff[cube_of, pl.ds(j * pair, pair)] = spread(
+            contract_last(pair_of(acts, j), wgu[cube_of])
+        )
+        return carry
+
+    lax.fori_loop(0, 8 // pair, near, 0)
     gu_cross.wait_recv()
     landed = wgu.at[1 - cube_of, pl.ds(dp * half, half)]
     links.go(landed, landed, sibling).wait_recv()
 
     def forward(j, carry):
-        a = block_of(acts, j)
-        g = contract_last(a, wgu[0])
-        u = contract_last(a, wgu[1])
-        gate[j] = g
-        up[j] = u
-        mixed[j] = (gelu_parts(g)[0] * u).astype(BF)
+        here = pl.ds(j * pair, pair)
+        ff[1 - cube_of, here] = spread(contract_last(pair_of(acts, j), wgu[1 - cube_of]))
+        mixed[here] = (gelu_parts(ff[0, here])[0] * ff[1, here]).astype(BF)
         return carry
 
-    lax.fori_loop(0, 8, forward, 0)
+    lax.fori_loop(0, 8 // pair, forward, 0)
 
     @pl.when(stays_in)
     def _():
@@ -798,10 +812,11 @@
     links.go(landed, landed, sibling).wait_recv()
 
     def project(j, carry):
-        put_block(sums, j, jnp.dot(mixed[j], flat(wd[...]), preferred_element_type=F32).astype(BF))
+        m = flat(mixed[pl.ds(j * pair, pair)])
+        put_pair(sums, j, jnp.dot(m, flat(wd[...]), preferred_element_type=F32).astype(BF))
         return carry
 
-    lax.fori_loop(0, 8, project, 0)
+    lax.fori_loop(0, 8 // pair, project, 0)
     links.drain()
     cube.scatter(sums, one, two, three)
     links.drain()
@@ -839,24 +854,25 @@
     d_swap = links.go(slab(4 * thalf + (1 - dp) * thalf, thalf), d_in, sibling)
 
     def backward(j, carry):
-        d = contract_last(block_of(downs, j), flat(wd[...]))
-        value, slope = gelu_parts(gate[j])
-        dg = (d * up[j] * slope).astype(BF)
+        here = pl.ds(j * pair, pair)
+        d = spread(contract_last(pair_of(downs, j), flat(wd[...])))
+        value, slope = gelu_parts(ff[0, here])
+        dg = (d * ff[1, here] * slope).astype(BF)
         du = (d * value).astype(BF)
-        gate[j] = dg.astype(F32)
-        up[j] = du.astype(F32)
-        put_block(
+        ff[0, here] = dg.astype(F32)
+        ff[1, here] = du.astype(F32)
+        put_pair(
             sums,
             j,
             (
-                jnp.dot(dg, wgu[0], preferred_element_type=F32)
-                + jnp.dot(du, wgu[1], preferred_element_type=F32)
+                jnp.dot(flat(dg), wgu[0], preferred_element_type=F32)
+                + jnp.dot(flat(du), wgu[1], preferred_element_type=F32)
             ).astype(BF),
         )
         return carry
 
     links.drain()
-    lax.fori_loop(0, 8, backward, 0)
+    lax.fori_loop(0, 8 // pair, backward, 0)
     moved = {}
 
     def weights():
@@ -875,8 +891,8 @@
 
         for lo in range(0, wide, 128):
             cut = slice(lo, lo + 128)
-            for i, buf in enumerate((gate, up)):
-                grad = buf[:, :, cut].reshape(tokens, 128).astype(BF)
+            for i in range(2):
+                grad = ff[i, :, :, cut].reshape(tokens, 128).astype(BF)
                 put_rows(i * units + lo, units - lo, contract_first(grad, acts_all))
         swap = [
             links.go(slab(i * 2 * thalf + (1 - dp) * thalf, thalf), gu_in.at[i], sibling)
@@ -900,30 +916,105 @@
     grad_branch = norm_back(value, branch_scale, grad * gain_attend).astype(BF)
     links.drain()
 
-    def spot(h, zz, yy, xx):
-        a, b = (yy, xx) if h == 0 else (xx, yy)
-        return (b * 2 + a) * layers + zz
-
-    def put_parts(base, count, block):
-        for zz in range(layers):
-            for yy in range(2):
-                for xx in range(2):
-                    for h in range(2):
-                        first = (((zz * 2 + yy) * 2 + xx) * 2 + h) * count * TILE
-                        at = base + (h * 4 * layers + spot(h, zz, yy, xx)) * count
-                        pool[at : at + count] = tiled(
-                            block[first : first + count * TILE].astype(BF)
-                        )
-
-    base_out = 8 * layers * tq
-    q_in = downs.at[pl.ds(0, 4 * layers * tq)]
+    class Reduce:
+        def __init__(self, base, count, layers_in, came, one_in, two_in, far_in):
+            self.base, self.count, self.layers_in = base, count, layers_in
+            self.size = len(layers_in)
+            self.per = 4 * self.size * count
+            self.quarter = self.per // 4
+            self.came, self.one_in, self.two_in, self.far_in = came, one_in, two_in, far_in
+            self.whole = self.size == layers
+            self.takes = (z >= layers_in[0]) & (z <= layers_in[-1])
+
+        def put(self, block):
+            size = self.count * TILE
+            for zi in range(self.size):
+                for yy in range(2):
+                    for xx in range(2):
+                        for h in range(2):
+                            a, b = (yy, xx) if h == 0 else (xx, yy)
+                            first = (((zi * 2 + yy) * 2 + xx) * 2 + h) * size
+                            spot = (b * 2 + a) * self.size + zi
+                            at = self.base + h * self.per + spot * self.count
+                            pool[at : at + self.count] = tiled(
+                                block[first : first + size].astype(BF)
+                            )
+            self.swap = links.go(
+                slab(self.base + (1 - dp) * self.per, self.per), self.came, sibling
+            )
+
+        def on_chip(self):
+            self.swap.wait_recv()
+            mine = pl.ds(self.base + dp * self.per, self.per)
+            pool[mine] = add_low(pool[mine], self.came[...])
+            away = self.base + dp * self.per + (1 - mine3) * 2 * self.quarter
+            self.at = self.base + dp * self.per + mine3 * 2 * self.quarter
+            self.steps = []
+            for a in (1 - mine2, mine2):
+                cut = pl.ds(a * self.quarter, self.quarter)
+                part = slab(away + a * self.quarter, self.quarter)
+                self.steps.append((a, links.go(part, self.one_in.at[cut], third)))
+
+        def across_third(self):
+            for i, (a, copy) in enumerate(self.steps):
+                copy.wait_recv()
+                near = pl.ds(self.at + a * self.quarter, self.quarter)
+                cut = pl.ds(a * self.quarter, self.quarter)
+                pool[near] = add_low(pool[near], self.one_in[cut])
+                if i == 0:
+                    self.step = links.go(pool.at[near], self.two_in, second)
+            self.at = self.at + mine2 * self.quarter
+
+        def across_second(self):
+            self.step.wait_recv()
+            near = pl.ds(self.at, self.quarter)
+            pool[near] = add_low(pool[near], self.two_in[...])
+            self.fars = []
+            for i, device in enumerate(others):
+                to_layer = lax.rem(z + i + 1, layers)
+                if self.whole:
+                    part = slab(self.at + to_layer * self.count, self.count)
+                    self.fars.append(links.go(part, self.far_in.at[i], device))
+                    continue
+                inside = (to_layer >= self.layers_in[0]) & (to_layer <= self.layers_in[-1])
+                index = jnp.where(inside, to_layer - self.layers_in[0], 0)
+                part = slab(self.at + index * self.count, self.count)
+                self.fars.append(links.go_if(inside, part, self.far_in.at[i], device))
+
+        def along(self, result):
+            def add():
+                index = z if self.whole else z - self.layers_in[0]
+                value = pool[pl.ds(self.at + index * self.count, self.count)].astype(F32)
+                for i, copy in enumerate(self.fars):
+                    copy.wait_recv()
+                    value = value + self.far_in[i].astype(F32)
+                result[dp] = value.astype(BF)
+
+            if self.whole:
+                add()
+            else:
+                pl.when(self.takes)(add)
+
+    per_qkv = 2 * layers * tq
+    q_buf = downs.at[pl.ds(0, 2 * per_qkv)]
     o_in = acts.at[pl.ds(0, 4 * layers * to)]
-    q_one = acts.at[pl.ds(4 * layers * to, 2 * layers * tq)]
-    o_one = downs.at[pl.ds(4 * layers * tq, 2 * layers * to)]
-    put_parts(base_out, to, contract_first(attended[...], grad_branch))
-    per_out = 4 * layers * to
-    per_qkv = 4 * layers * tq
-    o_swap = links.go(slab(base_out + (1 - dp) * per_out, per_out), o_in, sibling)
+    q_one = acts.at[pl.ds(4 * layers * to, per_qkv)]
+    o_one = downs.at[pl.ds(2 * per_qkv, 2 * layers * to)]
+    few = layers // 2
+    sets = [
+        Reduce(
+            i * 2 * per_qkv,
+            tq,
+            tuple(range(i * few, (i + 1) * few)),
+            q_buf.at[pl.ds(i * per_qkv, per_qkv)],
+            q_one.at[pl.ds(i * per_qkv // 2, per_qkv // 2)],
+            q_two.at[pl.ds(i * per_qkv // 4, per_qkv // 4)],
+            q_far,
+        )
+        for i in range(2)
+    ]
+    outs = Reduce(4 * per_qkv, to, tuple(range(layers)), o_in, o_one, o_two, o_far)
+    outs.put(contract_first(attended[...], grad_branch))
     grad_att = contract_last(grad_branch, flat(out_w[...])).astype(BF)
     for h in range(H):
         part = slice(h * rows, (h + 1) * rows)
@@ -936,7 +1027,9 @@
     dpairs[:, :, :, :HD] = grad_keys.astype(BF).reshape(layers, 2, rows, HD)
     grad_values = contract_first(probs[...].astype(BF), grad_heads)
     dpairs[:, :, :, HD:] = grad_values.astype(BF).reshape(layers, 2, rows, HD)
-    kv_line = links.go(dpairs.at[:, 1 - y], kv_in, beside)
+    kv_lines = [
+        links.go_if(z >= zz, dpairs.at[zz, 1 - y], kv_in.at[zz], beside) for zz in range(layers)
+    ]
 
     def turned_back(part, gain, grad):
         cosine, sine = turn[0], turn[1]
@@ -948,12 +1041,7 @@
         gain_term = jnp.sum(grad * (part * part_scale), axis=0, keepdims=True)
         return norm_back(part, part_scale, grad * gain), gain_term
 
-    o_swap.wait_recv()
-    mine_out = pl.ds(base_out + dp * per_out, per_out)
-    pool[mine_out] = add_low(pool[mine_out], o_in[...])
-    o_third = links.go(
-        slab(base_out + dp * per_out + (1 - mine3) * per_out // 2, per_out // 2), o_one, third
-    )
+    outs.on_chip()
     query_term = jnp.zeros((1, HD), F32)
     grads = []
     for h in range(H):
@@ -963,24 +1051,30 @@
         grads.append(grad.astype(BF))
         query_term = query_term + term
     put_gain(4 * width, query_term)
-    kv_line.wait_recv()
-    for i in range(layers):
-        kv_sum[i] = add_low(kv_in[i], dpairs[i, y])
+    grad_queries = jnp.concatenate(grads, axis=1)
+    half_cols = (H + 2) * HD // 2
+
     kv_copies = []
     for i, device in enumerate(others):
         to_layer = lax.rem(z + i + 1, layers)
-        kv_copies.append(
-            links.go_if(to_layer < z, kv_sum.at[to_layer], kv_far.at[i], device)
-        )
-    o_third.wait_recv()
-    quarter_out = per_out // 4
-    at_out = base_out + dp * per_out + mine3 * (per_out // 2)
-    near = pl.ds(at_out, per_out // 2)
-    pool[near] = add_low(pool[near], o_one[...])
-    o_second = links.go(slab(at_out + (1 - mine2) * quarter_out, quarter_out), o_two, second)
+        copy = links.make(kv_sum.at[to_layer], kv_far.at[i], device)
+        links.some.append((to_layer < z, copy))
+        kv_copies.append((to_layer, copy))
+    for zz in range(layers):
+
+        @pl.when(z >= zz)
+        def _():
+            kv_lines[zz].wait_recv()
+            kv_sum[zz] = add_low(kv_in[zz], dpairs[zz, y])
+
+        for to_layer, copy in kv_copies:
+            pl.when((to_layer == zz) & (z > zz))(copy.start)
+    sets[0].put(contract_first(grad_queries[:, :half_cols], xn[...]))
+    outs.across_third()
+    sets[0].on_chip()
     kv_total = stage.at[3 * rows : 4 * rows, 0 : 2 * HD]
     kv_total[...] = kv_sum[z].astype(F32)
-    for i, copy in enumerate(kv_copies):
+    for i, (_, copy) in enumerate(kv_copies):
 
         @pl.when(behind[i] > z)
         def _():
@@ -992,63 +1086,38 @@
         proj[:, query_width : query_width + HD], gain_key, grad_pair[:, :HD]
     )
     put_gain(4 * width + HD, term)
-    grads += [grad.astype(BF), grad_pair[:, HD:].astype(BF)]
-    grad_proj = jnp.concatenate(grads, axis=1)
-    put_parts(0, tq, contract_first(grad_proj, xn[...]))
-    q_swap = links.go(slab((1 - dp) * per_qkv, per_qkv), q_in, sibling)
+    grad_proj = jnp.concatenate(
+        [grad_queries, grad.astype(BF), grad_pair[:, HD:].astype(BF)], axis=1
+    )
+    sets[1].put(contract_first(grad_proj[:, half_cols:], xn[...]))
+    sets[0].across_third()
+    sets[1].on_chip()
     grad_normed = jnp.dot(grad_proj, flat(qkv_w[...]), preferred_element_type=F32)
     value = tok[...].astype(F32)
     in_scale = norm_scale(value)
     put_gain(0, jnp.sum(grad_normed * (value * in_scale), axis=0, keepdims=True))
     g_swap = links.go(g_sum.at[0], g_in.at[1], sibling)
     input_grad[...] = grad_hidden[...] + norm_back(value, in_scale, grad_normed * gain_in)
-    o_second.wait_recv()
-    at_out = at_out + mine2 * quarter_out
-    near = pl.ds(at_out, quarter_out)
-    pool[near] = add_low(pool[near], o_two[...])
-    o_fars = [
-        links.go(slab(at_out + lax.rem(z + i + 1, layers) * to, to), o_far.at[i], device)
-        for i, device in enumerate(others)
-    ]
+    outs.across_second()
     g_swap.wait_recv()
     g_sum[1] = g_sum[0] + g_in[1]
     g_x = links.go(g_sum.at[1], g_in.at[2], cube.peers[0])
-    q_swap.wait_recv()
-    mine_qkv = pl.ds(dp * per_qkv, per_qkv)
-    pool[mine_qkv] = add_low(pool[mine_qkv], q_in[...])
-    q_third = links.go(slab(dp * per_qkv + (1 - mine3) * per_qkv // 2, per_qkv // 2), q_one, third)
+    sets[0].across_second()
+    sets[1].across_third()
     g_x.wait_recv()
     g_sum[2] = g_sum[1] + g_in[2]
     g_y = links.go(g_sum.at[2], g_in.at[3], beside)
-    q_third.wait_recv()
-    quarter_qkv = per_qkv // 4
-    at_qkv = dp * per_qkv + mine3 * (per_qkv // 2)
-    near = pl.ds(at_qkv, per_qkv // 2)
-    pool[near] = add_low(pool[near], q_one[...])
-    q_second = links.go(slab(at_qkv + (1 - mine2) * quarter_qkv, quarter_qkv), q_two, second)
+    sets[1].across_second()
     g_y.wait_recv()
     g_sum[3] = g_sum[2] + g_in[3]
     g_in[4 + z] = g_sum[3]
     g_z = [links.go(g_sum.at[3], g_in.at[4 + z], device) for device in others]
-    q_second.wait_recv()
-    at_qkv = at_qkv + mine2 * quarter_qkv
-    near = pl.ds(at_qkv, quarter_qkv)
-    pool[near] = add_low(pool[near], q_two[...])
-    q_fars = [
-        links.go(slab(at_qkv + lax.rem(z + i + 1, layers) * tq, tq), q_far.at[i], device)
-        for i, device in enumerate(others)
-    ]
     ends = []
-
-    def finish(fars, far, at, count, result):
-        value = pool[pl.ds(at + z * count, count)].astype(F32)
-        for i, copy in enumerate(fars):
-            copy.wait_recv()
-            value = value + far[i].astype(F32)
-        result[dp] = value.astype(BF)
-        ends.append(links.go(result.at[dp], result.at[dp], sibling))
-
-    finish(o_fars, o_far, at_out, to, ro)
+    outs.along(ro)
+    ends.append(links.go(ro.at[dp], ro.at[dp], sibling))
+    sets[0].along(rq)
+    sets[1].along(rq)
+    ends.append(links.go(rq.at[dp], rq.at[dp], sibling))
     for copy in g_z:
         copy.wait_recv()
     value = g_in[4]
@@ -1070,7 +1139,6 @@
 
     landed = d_far.at[dp]
     d_end = links.go(landed, landed, sibling)
-    finish(q_fars, q_far, at_qkv, tq, rq)
     d_end.wait_recv()
     d_in[...] = add_low(d_far[0], d_far[1])
     keep_d = pltpu.make_async_copy(d_in, rd, local.at[7])
@@ -1128,8 +1196,7 @@
             full(2 * hq + 2 * ho + half, width),
             tile(8 * tiles),
             tile(8 * tiles),
-            full(8, rows, wide),
-            full(8, rows, wide),
+            full(2, 8, rows, wide),
             low(8, rows, wide),
             tile(8 * tiles),
             tile(4, tiles),

time: 347 us -> 330 us (0.951)
  Pallas kernels: 322 us -> 304 us
    pallas_call x1, Pallas kernels: 322 us -> 304 us  [whole_layer(): pl.pallas_call(layer_kernel, out_shape=(jax.ShapeDtypeStruct((rows, width...]
where the time goes in v4:
time: 330 us; the launch traced here: 328 us
  Pallas kernels  304 us (92%)
  other arithmetic  19.8 us (6%)
    pallas_call x1, Pallas kernels, whole_layer(): pl.pallas_call(layer_kernel, out_shape=(jax.ShapeDtypeStruct((rows, width...  304 us
    sub x5, other arithmetic, adamw(): weight - 0.03 * (first_hat / (jnp.sqrt(second_hat) + 1e-08) + 0.1 * weight)  19 us

profile of v4, /device:TPU:0, one launch (start us, length us, event | category | flops | bytes accessed | tf_op | source)
XLA Modules:
  0.0 328.2 jit_solution(11094203059353142262)
XLA Ops:
  0.7 0.8 convert_dynamic-update-slice_fusion
  1.5 0.0 copy-start.14
  1.5 0.6 copy-done.14
  2.1 0.0 copy-start.15
  2.1 0.0 copy-start.16
  2.1 0.0 copy-start.17
  2.1 304.4 %shard_map.345 = (bf16[128,1152]{1,0:T(8,128)(2,1)}, f32[128,1152]{1,0:T(8,128)}, bf16[2,3,16,1152]{3,2,1,0:T(8,128)(2,1)}, bf16[2,2,16,1152]{3,2,1,0:T(8,128)(2...) custom-call(bf16[128,1152]{1,0:T(8,128)(2,1)} %bitcast.24, ...), custom_call_target="tpu_custom_call" | custom-call | tf_op jit(solution)/shard_map/pallas_call | solution.py:1177
  306.5 0.0 copy-done.15
  306.5 0.0 copy-done.16
  306.5 0.0 copy-done.17
  306.5 1.4 multiply_subtract_fusion.4
  307.9 11.5 %multiply_subtract_fusion = (f32[864,1152]{1,0:T(8,128)}, f32[864,1152]{1,0:T(8,128)}, f32[864,1152]{1,0:T(8,128)}, f32[864,1152]{1,0:T(8,128)}) fusion(f32[864,1152]{1,0:T(8,128)} %wgu_in.1, f32[864,1152]{1,0:T(8,128)} %param.28, f32[864,1152]{1,0:T(8,128)} %param.33, bf16[2,27,16,1152]{3,2,1,0:T(8,128)(2,1)} %get-tuple-element.33), kind=kLoop, calls=%fused_computation.2 | loop fusion | flops 15925248 | bytes 29859840 | tf_op jit(solution)/shard_map/sub | solution.py:67
  319.4 0.0 copy-done
  319.4 0.0 copy-done.1
  319.4 0.1 copy-done.2
  319.6 0.8 copy-done.5
  320.4 3.7 %multiply_subtract_fusion.1 = (f32[432,1152]{1,0:T(8,128)}, f32[432,1152]{1,0:T(8,128)}, f32[432,1152]{1,0:T(8,128)}, f32[432,1152]{1,0:T(8,128)}) fusion(f32[432,1152]{1,0:T(8,128)S(1)} %copy-done, f32[432,1152]{1,0:T(8,128)S(1)} %copy-done.1, f32[432,1152]{1,0:T(8,128)S(1)} %copy-done.2, bf16[27,16,1152]{2,1,0:T(8,128)(2,1)S(1)} %copy-done.5), kind=kLoop, calls=%fused_computation.7 | loop fusion | flops 7962624 | bytes 14929920 | tf_op jit(solution)/shard_map/sub | solution.py:67
  324.1 0.0 copy-done.3
  324.1 0.0 copy-done.7
  324.1 0.0 copy-done.8
  324.1 0.0 copy-done.12
  324.1 0.0 copy-start.11
  324.2 1.3 multiply_subtract_fusion.2
  325.5 0.0 copy-done.4
  325.5 0.0 copy-done.9
  325.5 0.0 copy-done.10
  325.5 0.1 copy-done.13
  325.6 1.1 multiply_subtract_fusion.3
  326.6 0.0 copy-done.11
  326.6 0.7 copy.43
  327.4 0.0 copy-done.6
  327.4 0.8 copy.44
  (14 shorter events, 0.0 us)
Async XLA Ops:
  1.5 0.6 copy-start.14
  2.1 304.4 %copy-start.15 = (f32[320]{0:T(512)S(1)}, f32[320]{0:T(512)}, u32[]{:S(2)}) copy-start(f32[320]{0:T(512)} %param.25) | copy-start | bytes 3844
  2.1 304.4 %copy-start.16 = (f32[320]{0:T(512)S(1)}, f32[320]{0:T(512)}, u32[]{:S(2)}) copy-start(f32[320]{0:T(512)} %param.30) | copy-start | bytes 3844
  2.1 304.4 %copy-start.17 = (f32[320]{0:T(512)S(1)}, f32[320]{0:T(512)}, u32[]{:S(2)}) copy-start(f32[320]{0:T(512)} %param.35) | copy-start | bytes 3844
  307.9 11.5 %copy-start = (f32[432,1152]{1,0:T(8,128)S(1)}, f32[432,1152]{1,0:T(8,128)}, u32[]{:S(2)}) copy-start(f32[432,1152]{1,0:T(8,128)} %wd_in.1) | copy-start | bytes 5971972
  307.9 11.5 %copy-start.1 = (f32[432,1152]{1,0:T(8,128)S(1)}, f32[432,1152]{1,0:T(8,128)}, u32[]{:S(2)}) copy-start(f32[432,1152]{1,0:T(8,128)} %param.29) | copy-start | bytes 5971972
  307.9 11.7 %copy-start.2 = (f32[432,1152]{1,0:T(8,128)S(1)}, f32[432,1152]{1,0:T(8,128)}, u32[]{:S(2)}) copy-start(f32[432,1152]{1,0:T(8,128)} %param.34) | copy-start | bytes 5971972
  307.9 12.5 %copy-start.5 = (bf16[27,16,1152]{2,1,0:T(8,128)(2,1)S(1)}, bf16[27,16,1152]{2,1,0:T(8,128)(2,1)}, u32[]{:S(2)}) copy-start(bf16[27,16,1152]{2,1,0:T(8,128)(2,1)} %get-tuple-element.34) | copy-start | bytes 2985988
  320.4 3.7 %copy-start.3 = (f32[96,1152]{1,0:T(8,128)S(1)}, f32[96,1152]{1,0:T(8,128)}, u32[]{:S(2)}) copy-start(f32[96,1152]{1,0:T(8,128)} %wq.1) | copy-start | bytes 1327108
  320.4 3.7 %copy-start.7 = (f32[96,1152]{1,0:T(8,128)S(1)}, f32[96,1152]{1,0:T(8,128)}, u32[]{:S(2)}) copy-start(f32[96,1152]{1,0:T(8,128)} %param.26) | copy-start | bytes 1327108
  320.4 3.8 %copy-start.8 = (f32[96,1152]{1,0:T(8,128)S(1)}, f32[96,1152]{1,0:T(8,128)}, u32[]{:S(2)}) copy-start(f32[96,1152]{1,0:T(8,128)} %param.31) | copy-start | bytes 1327108
  320.4 3.8 %copy-start.12 = (bf16[2,3,16,1152]{3,2,1,0:T(8,128)(2,1)S(1)}, bf16[2,3,16,1152]{3,2,1,0:T(8,128)(2,1)}, u32[]{:S(2)}) copy-start(bf16[2,3,16,1152]{3,2,1,0:T(8,128)(2,1)} %get-tuple-element.31) | copy-start | bytes 663556
  324.1 1.4 copy-start.4
  324.1 1.4 copy-start.9
  324.1 1.4 copy-start.10
  324.1 1.5 copy-start.13
  324.1 2.5 copy-start.11
  325.5 1.9 copy-start.6

commit v5 on v4

--- a/solution.py
+++ b/solution.py
@@ -335,7 +335,36 @@
         self.sent, self.some = [], []
 
 
+class Feed:
+    def __init__(self, links):
+        self.links, self.copies, self.begun = links, [], 0
+
+    def add(self, source, target, device, condition=None):
+        self.copies.append((condition, self.links.make(source, target, device)))
+
+    def do(self, condition, action):
+        if condition is None:
+            action()
+        else:
+            pl.when(condition)(action)
+
+    def __call__(self, count=1):
+        for condition, copy in self.copies[self.begun : self.begun + count]:
+            self.do(condition, copy.start)
+        self.begun = min(self.begun + count, len(self.copies))
+
+    def arrive(self, first, last):
+        for condition, copy in self.copies[first:last]:
+            self.do(condition, copy.wait_recv)
+
+    def drain(self):
+        assert self.begun == len(self.copies)
+        for condition, copy in self.copies:
+            self.do(condition, copy.wait_send)
+
+
 TILE = 16
+CHUNK = 3
 AXES = (1, 2, 4)
 ORDERS = ((0, 1, 2), (1, 2, 0), (2, 0, 1))
 
@@ -364,7 +393,7 @@
         start, size = self.parts[p]
         return buf.at[pl.ds(self.block(mask) * self.tiles + start, size)]
 
-    def gather(self, buf):
+    def gather(self, buf, feed=lambda: None):
         sent = {}
 
         def go(p, index, mask, dim):
@@ -374,21 +403,51 @@
         for index, where in ((0, 0), (1, 1), (3, 2)):
             for p, order in enumerate(ORDERS):
                 go(p, index, 0, order[where])
+        feed()
         for p, (a, b, c) in enumerate(ORDERS):
             sent[p, 0].wait_recv()
             go(p, 2, AXES[a], b)
             go(p, 4, AXES[a], c)
+        feed()
         for p, (a, b, c) in enumerate(ORDERS):
             sent[p, 1].wait_recv()
             go(p, 5, AXES[b], c)
             sent[p, 2].wait_recv()
             go(p, 6, AXES[a] | AXES[b], c)
+        feed()
         for index in (3, 4, 5, 6):
             for p in range(3):
                 sent[p, index].wait_recv()
 
-    def scatter(self, buf, one, two, three, beside=None):
-        sent = {}
+    def pair(self, step):
+        high = (self.me // 4 + (3 - step) // 2) % 2
+        return 2 * high + (self.me // 2 + 3 - step) % 2
+
+    def first_copies(self, buf, one):
+        copies = {}
+        for index in range(4):
+            for p, (a, b, c) in enumerate(ORDERS):
+                mask = (AXES[b], AXES[b] | AXES[a], AXES[a], 0)[index] | AXES[c]
+                start, size = self.parts[p]
+                target = one.at[index, pl.ds(start, size)]
+                copies[p, index] = (
+                    3 - mask // 2,
+                    self.links.make(self.cut(buf, p, mask), target, self.peers[c]),
+                )
+        return copies
+
+    def release(self, copies, step):
+        for turn in range(4):
+
+            @pl.when(step == turn)
+            def _():
+                for when, copy in copies.values():
+                    if when == turn:
+                        copy.start()
+
+    def scatter(self, buf, copies, one, two, three, beside=None, feed=lambda: None):
+        sent = {key: copy for key, (_, copy) in copies.items()}
+        self.links.sent += list(sent.values())
 
         def go(p, index, mask, slot, dim):
             start, size = self.parts[p]
@@ -400,10 +459,6 @@
             mine = self.cut(buf, p, mask)
             mine[...] = (mine[...].astype(F32) + slot[pl.ds(start, size)].astype(F32)).astype(BF)
 
-        for index in range(4):
-            for p, (a, b, c) in enumerate(ORDERS):
-                mask = (AXES[b], AXES[b] | AXES[a], AXES[a], 0)[index]
-                go(p, index, AXES[c] | mask, one.at[index], c)
         if beside is not None:
             beside()
         for index in range(2):
@@ -412,12 +467,14 @@
                 sent[p, 1 - index].wait_recv()
                 add(p, mask, one.at[1 - index])
                 go(p, 4 + index, mask, two.at[index], b)
+            feed()
         for p, (a, b, c) in enumerate(ORDERS):
             sent[p, 2].wait_recv()
             add(p, AXES[a], one.at[2])
             sent[p, 4].wait_recv()
             add(p, AXES[a], two.at[0])
             go(p, 6, AXES[a], three, a)
+        feed()
         for p in range(3):
             sent[p, 3].wait_recv()
             add(p, 0, one.at[3])
@@ -634,23 +691,25 @@
             line = fulls[t].at[:, yy, xx, dp]
             sib[t].append(links.go(line, line, sibling))
 
+    cuts = [(i, min(CHUNK, thalf - i)) for i in range(0, thalf, CHUNK)]
+    down_local = pltpu.make_async_copy(d_in, wd.at[pl.ds(x * thalf, thalf)], local.at[5])
+    pl.when(stays_in)(down_local.start)
+    leaves_in = jnp.logical_not(stays_in)
+    down_feed, gu_feed = Feed(links), Feed(links)
+    for first, size in cuts:
+        target = wd.at[pl.ds(x * thalf + first, size)]
+        down_feed.add(d_in.at[pl.ds(first, size)], target, user, leaves_in)
+        part = wgu.at[cube_of, pl.ds(dp * half + first * TILE, size * TILE)]
+        gu_feed.add(part, part, across)
+    down_feed(0)
+    gu_feed(0)
     second_steps(0)
     behind = [lax.rem(z + layers - 1 - i, layers) for i in range(layers - 1)]
     for i, copy in enumerate(firsts[1]):
         copy.wait_recv()
         passed.append(pass_on(behind[i], y, x, second, third, sibling))
-    own_down = wd.at[pl.ds(x * thalf, thalf)]
-    down_local = pltpu.make_async_copy(d_in, own_down, local.at[5])
-    down_move = links.make(d_in, own_down, user)
-
-    @pl.when(stays_in)
-    def _():
-        down_local.start()
-
-    @pl.when(jnp.logical_not(stays_in))
-    def _():
-        down_move.start()
-
+        down_feed(3)
+        gu_feed(0)
     firsts.append(first_steps(out_w))
     third_steps(0)
     line_order = [z] + behind
@@ -658,6 +717,8 @@
     for i, zz in enumerate(line_order):
         passed[i][0].wait_recv()
         far.append(pass_on(zz, y2, x2, third, sibling))
+        down_feed(0)
+        gu_feed(0)
     last_steps(0)
     ends_q = []
     for i, zz in enumerate(line_order):
@@ -665,6 +726,8 @@
         ends_q += pass_on(zz, y3, x3, sibling)
         far[i][0].wait_recv()
         ends_q += pass_on(zz, 1 - y, 1 - x, sibling)
+        down_feed(0)
+        gu_feed(0)
     second_steps(2)
     ends_q += [copies[2] for copies in passed] + [copies[1] for copies in far]
     for copy in ends_q + sib[0]:
@@ -725,8 +788,8 @@
     for k in range(1, layers):
         pl.when(z >= k)(pair_side[k].wait_recv)
 
-    half_rows = wgu.at[cube_of, pl.ds(dp * half, half)]
-    gu_cross = links.go(half_rows, half_rows, across)
+    down_feed(0)
+    gu_feed(3)
     def allowed(b):
         key_pos = b * rows + lax.broadcasted_iota(jnp.int32, (1, rows), 1)
         return (key_pos <= position) & (seg[b : b + 1, :] == ids)
@@ -765,7 +828,10 @@
 
     me = cube.me
     put_block(acts, me, (value * norm_scale(value) * gain_pre).astype(BF))
-    cube.gather(acts)
+    gu_feed(0)
+    cube.gather(acts, lambda: gu_feed(2))
+    gu_feed(len(cuts))
+    down_feed(len(cuts))
     pair = 2
 
     def pair_of(buf, j):
@@ -784,9 +850,18 @@
         return carry
 
     lax.fori_loop(0, 8 // pair, near, 0)
-    gu_cross.wait_recv()
-    landed = wgu.at[1 - cube_of, pl.ds(dp * half, half)]
-    links.go(landed, landed, sibling).wait_recv()
+    def hand_on(feed, ref, base, unit):
+        handed = []
+        for i in range(0, len(cuts), 3):
+            chunk = cuts[i : i + 3]
+            feed.arrive(i, i + 3)
+            first, size = chunk[0][0], sum(size for _, size in chunk)
+            part = ref.at[pl.ds(base + first * unit, size * unit)]
+            handed.append(links.go(part, part, sibling))
+        for copy in handed:
+            copy.wait_recv()
+
+    hand_on(gu_feed, wgu.at[1 - cube_of], dp * half, TILE)
 
     def forward(j, carry):
         here = pl.ds(j * pair, pair)
@@ -796,29 +871,22 @@
 
     lax.fori_loop(0, 8 // pair, forward, 0)
 
-    @pl.when(stays_in)
-    def _():
-        down_local.wait()
-
-    @pl.when(jnp.logical_not(stays_in))
-    def _():
-        down_move.wait_send()
-
-    @pl.when(jnp.logical_not(stays_in))
-    def _():
-        down_move.wait_recv()
-
-    landed = wd.at[pl.ds(dp * thalf, thalf)]
-    links.go(landed, landed, sibling).wait_recv()
-
-    def project(j, carry):
+    pl.when(stays_in)(down_local.wait)
+    down_feed.drain()
+    gu_feed.drain()
+    hand_on(down_feed, wd, dp * thalf, 1)
+    links.drain()
+    first_sums = cube.first_copies(sums, one)
+
+    def project(i, carry):
+        j = cube.pair(i)
         m = flat(mixed[pl.ds(j * pair, pair)])
         put_pair(sums, j, jnp.dot(m, flat(wd[...]), preferred_element_type=F32).astype(BF))
+        cube.release(first_sums, i)
         return carry
 
     lax.fori_loop(0, 8 // pair, project, 0)
-    links.drain()
-    cube.scatter(sums, one, two, three)
+    cube.scatter(sums, first_sums, one, two, three)
     links.drain()
     down = block_of(sums, me).astype(F32) + flat(three[...]).astype(F32)
     down_scale = norm_scale(down)
@@ -836,74 +904,84 @@
     put_gain(3 * width, jnp.sum(dy * normal, axis=0, keepdims=True))
     cube.gather(downs)
 
-    def put_rows(first, limit, block):
-        kept = min(block.shape[0], limit)
-        pool[first // TILE : (first + kept) // TILE] = tiled(block[:kept].astype(BF))
-
-    downs_all = flat(downs[...])
-    acts_all = flat(acts[...])
     tokens = 8 * rows
-    for lo in range(0, wide, 128):
-        cut = slice(lo, lo + 128)
-        mx = mixed[:, :, cut].reshape(tokens, 128)
-        put_rows(2 * units + lo, units - lo, contract_first(mx, downs_all))
+    whole_chunks = units // 128
+
+    def weight_grad(part, tokens_in, base):
+        def chunk(first, size, at):
+            left = part(pl.ds(first, 128)).reshape(tokens, 128)
+            block = contract_first(left, flat(tokens_in[...]))[:size].astype(BF)
+            pool[pl.ds(at, size // TILE)] = tiled(block)
+
+        def body(i, carry):
+            chunk(pl.multiple_of(i * 128, 128), 128, base + i * (128 // TILE))
+            return carry
+
+        lax.fori_loop(0, whole_chunks, body, 0)
+        if units % 128:
+            chunk(whole_chunks * 128, units % 128, base + whole_chunks * (128 // TILE))
+
+    weight_grad(lambda cut: mixed[:, :, cut], downs, 4 * thalf)
 
     def slab(first, size):
         return pool.at[pl.ds(first, size)]
 
     d_swap = links.go(slab(4 * thalf + (1 - dp) * thalf, thalf), d_in, sibling)
 
-    def backward(j, carry):
-        here = pl.ds(j * pair, pair)
-        d = spread(contract_last(pair_of(downs, j), flat(wd[...])))
-        value, slope = gelu_parts(ff[0, here])
-        dg = (d * ff[1, here] * slope).astype(BF)
-        du = (d * value).astype(BF)
-        ff[0, here] = dg.astype(F32)
-        ff[1, here] = du.astype(F32)
-        put_pair(
-            sums,
-            j,
-            (
-                jnp.dot(flat(dg), wgu[0], preferred_element_type=F32)
-                + jnp.dot(flat(du), wgu[1], preferred_element_type=F32)
-            ).astype(BF),
-        )
+    def backward(i, carry):
+        first = cube.pair(i) * pair
+        for j in range(pair):
+            here = first + j
+            d = contract_last(flat(downs[pl.ds(here * tiles, tiles)]), flat(wd[...]))
+            value, slope = gelu_parts(ff[0, here])
+            dg = (d * ff[1, here] * slope).astype(BF)
+            du = (d * value).astype(BF)
+            ff[0, here] = dg.astype(F32)
+            ff[1, here] = du.astype(F32)
+            total = jnp.dot(dg, wgu[0], preferred_element_type=F32) + jnp.dot(
+                du, wgu[1], preferred_element_type=F32
+            )
+            sums[pl.ds(here * tiles, tiles)] = tiled(total.astype(BF))
+        cube.release(first_sums, i)
         return carry
 
     links.drain()
+    first_sums = cube.first_copies(sums, one)
     lax.fori_loop(0, 8 // pair, backward, 0)
     moved = {}
+    leaves_back = jnp.logical_not(stays_back)
+    down_stay = pltpu.make_async_copy(d_in, d_far.at[cube_of], local.at[6])
+    down_back, gu_back = Feed(links), Feed(links)
+    for first, size in cuts:
+        cut = pl.ds(first, size)
+        down_back.add(d_in.at[cut], d_far.at[cube_of, cut], owner, leaves_back)
+        gu_back.add(gu_in.at[1 - cube_of, cut], gu_far.at[cut], across)
+
+    def feed_back(downs_count, gu_count):
+        down_back(downs_count)
+        gu_back(gu_count)
+
 
     def weights():
         d_swap.wait_recv()
         d_in[...] = add_low(d_in[...], pool[pl.ds(4 * thalf + dp * thalf, thalf)])
-        moved["local"] = pltpu.make_async_copy(d_in, d_far.at[cube_of], local.at[6])
-        moved["down"] = links.make(d_in, d_far.at[cube_of], owner)
-
-        @pl.when(stays_back)
-        def _():
-            moved["local"].start()
-
-        @pl.when(jnp.logical_not(stays_back))
-        def _():
-            moved["down"].start()
-
-        for lo in range(0, wide, 128):
-            cut = slice(lo, lo + 128)
-            for i in range(2):
-                grad = ff[i, :, :, cut].reshape(tokens, 128).astype(BF)
-                put_rows(i * units + lo, units - lo, contract_first(grad, acts_all))
-        swap = [
-            links.go(slab(i * 2 * thalf + (1 - dp) * thalf, thalf), gu_in.at[i], sibling)
-            for i in range(2)
-        ]
-        for i in range(2):
-            swap[i].wait_recv()
-            gu_in[i] = add_low(gu_in[i], pool[pl.ds(i * 2 * thalf + dp * thalf, thalf)])
-        moved["gu"] = links.go(gu_in.at[1 - cube_of], gu_far, across)
-
-    cube.scatter(sums, one, two, three, weights)
+        pl.when(stays_back)(down_stay.start)
+        down_back(2)
+
+        for turn in range(2):
+            side = cube_of if turn else 1 - cube_of
+            weight_grad(lambda cut: ff[side, :, :, cut].astype(BF), acts, side * 2 * thalf)
+            swap = links.go(
+                slab(side * 2 * thalf + (1 - dp) * thalf, thalf), gu_in.at[side], sibling
+            )
+            if turn:
+                moved["swap"] = swap
+                continue
+            swap.wait_recv()
+            gu_in[side] = add_low(gu_in[side], pool[pl.ds(side * 2 * thalf + dp * thalf, thalf)])
+            feed_back(2, 1)
+
+    cube.scatter(sums, first_sums, one, two, three, weights, lambda: feed_back(1, 1))
     value = hidden[...]
     hidden_scale = norm_scale(value)
     total = block_of(sums, me).astype(F32) + flat(three[...]).astype(F32)
@@ -914,6 +992,10 @@
     branch_scale = norm_scale(value)
     put_gain(width, jnp.sum(grad * (value * branch_scale), axis=0, keepdims=True))
     grad_branch = norm_back(value, branch_scale, grad * gain_attend).astype(BF)
+    moved["swap"].wait_recv()
+    gu_in[cube_of] = add_low(
+        gu_in[cube_of], pool[pl.ds(cube_of * 2 * thalf + dp * thalf, thalf)]
+    )
     links.drain()
 
     class Reduce:
@@ -926,19 +1008,18 @@
             self.whole = self.size == layers
             self.takes = (z >= layers_in[0]) & (z <= layers_in[-1])
 
-        def put(self, block):
+        def put(self, make):
             size = self.count * TILE
             for zi in range(self.size):
+                block = make(pl.ds(zi * 8 * size, 8 * size)).astype(BF)
                 for yy in range(2):
                     for xx in range(2):
                         for h in range(2):
                             a, b = (yy, xx) if h == 0 else (xx, yy)
-                            first = (((zi * 2 + yy) * 2 + xx) * 2 + h) * size
+                            first = ((yy * 2 + xx) * 2 + h) * size
                             spot = (b * 2 + a) * self.size + zi
                             at = self.base + h * self.per + spot * self.count
-                            pool[at : at + self.count] = tiled(
-                                block[first : first + size].astype(BF)
-                            )
+                            pool[at : at + self.count] = tiled(block[first : first + size])
             self.swap = links.go(
                 slab(self.base + (1 - dp) * self.per, self.per), self.came, sibling
             )
@@ -1014,7 +1095,10 @@
         for i in range(2)
     ]
     outs = Reduce(4 * per_qkv, to, tuple(range(layers)), o_in, o_one, o_two, o_far)
-    outs.put(contract_first(attended[...], grad_branch))
+    outs.put(lambda cut: contract_first(attended[:, cut], grad_branch))
+    keys = flat(pairs[:, :, :, :HD])
+    values = flat(pairs[:, :, :, HD:])
+    feed_back(1, 1)
     grad_att = contract_last(grad_branch, flat(out_w[...])).astype(BF)
     for h in range(H):
         part = slice(h * rows, (h + 1) * rows)
@@ -1042,6 +1126,7 @@
         return norm_back(part, part_scale, grad * gain), gain_term
 
     outs.on_chip()
+    feed_back(0, 1)
     query_term = jnp.zeros((1, HD), F32)
     grads = []
     for h in range(H):
@@ -1069,7 +1154,12 @@
 
         for to_layer, copy in kv_copies:
             pl.when((to_layer == zz) & (z > zz))(copy.start)
-    sets[0].put(contract_first(grad_queries[:, :half_cols], xn[...]))
+    feed_back(0, 0)
+
+    def columns(value, first, cut):
+        return value[:, first + cut.start : first + cut.start + cut.size]
+
+    sets[0].put(lambda cut: contract_first(columns(grad_queries, 0, cut), xn[...]))
     outs.across_third()
     sets[0].on_chip()
     kv_total = stage.at[3 * rows : 4 * rows, 0 : 2 * HD]
@@ -1081,6 +1171,7 @@
             copy.wait_recv()
             kv_total[...] += kv_far[i].astype(F32)
 
+    feed_back(0, 2)
     grad_pair = kv_total[...]
     grad, term = turned_back(
         proj[:, query_width : query_width + HD], gain_key, grad_pair[:, :HD]
@@ -1089,9 +1180,10 @@
     grad_proj = jnp.concatenate(
         [grad_queries, grad.astype(BF), grad_pair[:, HD:].astype(BF)], axis=1
     )
-    sets[1].put(contract_first(grad_proj[:, half_cols:], xn[...]))
+    sets[1].put(lambda cut: contract_first(columns(grad_proj, half_cols, cut), xn[...]))
     sets[0].across_third()
     sets[1].on_chip()
+    feed_back(len(cuts), len(cuts))
     grad_normed = jnp.dot(grad_proj, flat(qkv_w[...]), preferred_element_type=F32)
     value = tok[...].astype(F32)
     in_scale = norm_scale(value)
@@ -1125,25 +1217,17 @@
         value = value + g_in[4 + i]
     rg[...] = value
 
-    @pl.when(stays_back)
-    def _():
-        moved["local"].wait()
-
-    @pl.when(jnp.logical_not(stays_back))
-    def _():
-        moved["down"].wait_send()
-
-    @pl.when(jnp.logical_not(stays_back))
-    def _():
-        moved["down"].wait_recv()
-
+    pl.when(stays_back)(down_stay.wait)
+    down_back.arrive(0, len(cuts))
+    down_back.drain()
     landed = d_far.at[dp]
     d_end = links.go(landed, landed, sibling)
     d_end.wait_recv()
     d_in[...] = add_low(d_far[0], d_far[1])
     keep_d = pltpu.make_async_copy(d_in, rd, local.at[7])
     keep_d.start()
-    moved["gu"].wait_recv()
+    gu_back.arrive(0, len(cuts))
+    gu_back.drain()
     gu_far[...] = add_low(gu_in[cube_of], gu_far[...])
     keep_gu = pltpu.make_async_copy(gu_far, rgu.at[dp], local.at[8])
     keep_gu.start()
@@ -1225,8 +1309,8 @@
             tile(thalf),
             tile(thalf),
             tile(2, thalf),
-            pltpu.SemaphoreType.DMA((220,)),
-            pltpu.SemaphoreType.DMA((220,)),
+            pltpu.SemaphoreType.DMA((300,)),
+            pltpu.SemaphoreType.DMA((300,)),
             pltpu.SemaphoreType.DMA((9,)),
         ],
         compiler_params=pltpu.CompilerParams(

time: 330 us -> 322 us (0.976)
  Pallas kernels: 304 us -> 295 us
    pallas_call x1, Pallas kernels: 304 us -> 295 us  [whole_layer(): pl.pallas_call(layer_kernel, out_shape=(jax.ShapeDtypeStruct((rows, width...]
where the time goes in v5:
time: 322 us; the launch traced here: 319 us
  Pallas kernels  295 us (92%)
  other arithmetic  19.8 us (6%)
    pallas_call x1, Pallas kernels, whole_layer(): pl.pallas_call(layer_kernel, out_shape=(jax.ShapeDtypeStruct((rows, width...  295 us
    sub x5, other arithmetic, adamw(): weight - 0.03 * (first_hat / (jnp.sqrt(second_hat) + 1e-08) + 0.1 * weight)  19 us

profile of v5, /device:TPU:0, one launch (start us, length us, event | category | flops | bytes accessed | tf_op | source)
XLA Modules:
  0.0 318.7 jit_solution(16944953443198996788)
XLA Ops:
  0.7 0.8 convert_dynamic-update-slice_fusion
  1.5 0.0 copy-start.14
  1.5 0.6 copy-done.14
  2.1 0.0 copy-start.15
  2.1 0.0 copy-start.16
  2.1 0.0 copy-start.17
  2.1 294.9 %shard_map.345 = (bf16[128,1152]{1,0:T(8,128)(2,1)}, f32[128,1152]{1,0:T(8,128)}, bf16[2,3,16,1152]{3,2,1,0:T(8,128)(2,1)}, bf16[2,2,16,1152]{3,2,1,0:T(8,128)(2...) custom-call(bf16[128,1152]{1,0:T(8,128)(2,1)} %bitcast.24, ...), custom_call_target="tpu_custom_call" | custom-call | tf_op jit(solution)/shard_map/pallas_call | solution.py:1261
  297.0 0.0 copy-done.15
  297.0 0.0 copy-done.16
  297.0 0.0 copy-done.17
  297.0 1.4 multiply_subtract_fusion.4
  298.4 11.5 %multiply_subtract_fusion = (f32[864,1152]{1,0:T(8,128)}, f32[864,1152]{1,0:T(8,128)}, f32[864,1152]{1,0:T(8,128)}, f32[864,1152]{1,0:T(8,128)}) fusion(f32[864,1152]{1,0:T(8,128)} %wgu_in.1, f32[864,1152]{1,0:T(8,128)} %param.28, f32[864,1152]{1,0:T(8,128)} %param.33, bf16[2,27,16,1152]{3,2,1,0:T(8,128)(2,1)} %get-tuple-element.33), kind=kLoop, calls=%fused_computation.2 | loop fusion | flops 15925248 | bytes 29859840 | tf_op jit(solution)/shard_map/sub | solution.py:67
  310.0 0.0 copy-done
  310.0 0.0 copy-done.1
  310.0 0.1 copy-done.2
  310.1 0.8 copy-done.5
  310.9 3.7 %multiply_subtract_fusion.1 = (f32[432,1152]{1,0:T(8,128)}, f32[432,1152]{1,0:T(8,128)}, f32[432,1152]{1,0:T(8,128)}, f32[432,1152]{1,0:T(8,128)}) fusion(f32[432,1152]{1,0:T(8,128)S(1)} %copy-done, f32[432,1152]{1,0:T(8,128)S(1)} %copy-done.1, f32[432,1152]{1,0:T(8,128)S(1)} %copy-done.2, bf16[27,16,1152]{2,1,0:T(8,128)(2,1)S(1)} %copy-done.5), kind=kLoop, calls=%fused_computation.7 | loop fusion | flops 7962624 | bytes 14929920 | tf_op jit(solution)/shard_map/sub | solution.py:67
  314.6 0.0 copy-done.3
  314.7 0.0 copy-done.7
  314.7 0.0 copy-done.8
  314.7 0.0 copy-done.12
  314.7 0.0 copy-start.11
  314.7 1.3 multiply_subtract_fusion.2
  316.0 0.0 copy-done.4
  316.0 0.0 copy-done.9
  316.0 0.0 copy-done.10
  316.0 0.1 copy-done.13
  316.1 1.1 multiply_subtract_fusion.3
  317.2 0.0 copy-done.11
  317.2 0.7 copy.43
  317.9 0.0 copy-done.6
  317.9 0.8 copy.44
  (14 shorter events, 0.0 us)
Async XLA Ops:
  1.5 0.6 copy-start.14
  2.1 294.9 %copy-start.15 = (f32[320]{0:T(512)S(1)}, f32[320]{0:T(512)}, u32[]{:S(2)}) copy-start(f32[320]{0:T(512)} %param.25) | copy-start | bytes 3844
  2.1 294.9 %copy-start.16 = (f32[320]{0:T(512)S(1)}, f32[320]{0:T(512)}, u32[]{:S(2)}) copy-start(f32[320]{0:T(512)} %param.30) | copy-start | bytes 3844
  2.1 294.9 %copy-start.17 = (f32[320]{0:T(512)S(1)}, f32[320]{0:T(512)}, u32[]{:S(2)}) copy-start(f32[320]{0:T(512)} %param.35) | copy-start | bytes 3844
  298.4 11.5 %copy-start = (f32[432,1152]{1,0:T(8,128)S(1)}, f32[432,1152]{1,0:T(8,128)}, u32[]{:S(2)}) copy-start(f32[432,1152]{1,0:T(8,128)} %wd_in.1) | copy-start | bytes 5971972
  298.4 11.5 %copy-start.1 = (f32[432,1152]{1,0:T(8,128)S(1)}, f32[432,1152]{1,0:T(8,128)}, u32[]{:S(2)}) copy-start(f32[432,1152]{1,0:T(8,128)} %param.29) | copy-start | bytes 5971972
  298.4 11.7 %copy-start.2 = (f32[432,1152]{1,0:T(8,128)S(1)}, f32[432,1152]{1,0:T(8,128)}, u32[]{:S(2)}) copy-start(f32[432,1152]{1,0:T(8,128)} %param.34) | copy-start | bytes 5971972
  298.4 12.5 %copy-start.5 = (bf16[27,16,1152]{2,1,0:T(8,128)(2,1)S(1)}, bf16[27,16,1152]{2,1,0:T(8,128)(2,1)}, u32[]{:S(2)}) copy-start(bf16[27,16,1152]{2,1,0:T(8,128)(2,1)} %get-tuple-element.34) | copy-start | bytes 2985988
  310.9 3.7 %copy-start.3 = (f32[96,1152]{1,0:T(8,128)S(1)}, f32[96,1152]{1,0:T(8,128)}, u32[]{:S(2)}) copy-start(f32[96,1152]{1,0:T(8,128)} %wq.1) | copy-start | bytes 1327108
  310.9 3.7 %copy-start.7 = (f32[96,1152]{1,0:T(8,128)S(1)}, f32[96,1152]{1,0:T(8,128)}, u32[]{:S(2)}) copy-start(f32[96,1152]{1,0:T(8,128)} %param.26) | copy-start | bytes 1327108
  310.9 3.8 %copy-start.8 = (f32[96,1152]{1,0:T(8,128)S(1)}, f32[96,1152]{1,0:T(8,128)}, u32[]{:S(2)}) copy-start(f32[96,1152]{1,0:T(8,128)} %param.31) | copy-start | bytes 1327108
  310.9 3.8 %copy-start.12 = (bf16[2,3,16,1152]{3,2,1,0:T(8,128)(2,1)S(1)}, bf16[2,3,16,1152]{3,2,1,0:T(8,128)(2,1)}, u32[]{:S(2)}) copy-start(bf16[2,3,16,1152]{3,2,1,0:T(8,128)(2,1)} %get-tuple-element.31) | copy-start | bytes 663556
  314.6 1.4 copy-start.4
  314.6 1.4 copy-start.9
  314.6 1.4 copy-start.10
  314.6 1.5 copy-start.13
  314.7 2.5 copy-start.11
  316.0 1.9 copy-start.6
